TPU v7x, 256 devices: a whole 4x4x8 slice. The times are simulated.
256 devices in a mesh: section: 8 (over x_hi, y), dp: 32 (over z, x_lo, core).
Axes of the slice: x: 4 (x_hi: 2, x_lo: 2; x = x_hi * 2 + x_lo), y: 4, z: 8, core: 2. Of those that a mesh axis runs over, the one named last changes fastest.
Arguments:
- patches: bfloat16 [256, 16, 2048], P('dp'), may hold values from -40 to 40
- lengths: int32 [256, 16], P('dp'), may hold values from 1 to 16, 80 in all within a row
- cotangent: bfloat16 [256, 16, 2048], P('dp'), may hold values from -6 to 6
- weights: bfloat16 [2, 8, 2048, 1792], P(None, 'section', 'dp'), may hold values from -0.125 to 0.125
Outputs:
- grad_weights: float32 [2, 8, 2048, 1792], P(None, 'section', 'dp')
Inputs may be any that keep to these rules, and one draw needn't show every extreme that they name: Each row is one sequence's patch lengths in bytes, summing to 80, the largest exactly 16.
All inputs are finite; a program needn't handle non-finite values.
Results may differ from a plain program's by a relative error of at most 0.035.
Values may be sent and summed in bfloat16 or wider, within the bound.
No kernel may reach another device: no remote copies, remote signals or barrier semaphores. Data moves between devices by JAX's collectives and lax.ppermute only.
A program may use at most 128 MiB of HBM per device.

v0:
```python
from functools import partial
import math

import jax
import jax.numpy as jnp
from jax import lax
from jax.sharding import PartitionSpec as P

D = 2048
HEADS = 16
KV_HEADS = 4
QK_DIM = 64
V_DIM = 128


ROPE_BASE = 500000.0
EPSILON = 1e-05


def shifted(value, axis, by):
    size = lax.axis_size(axis)
    return lax.ppermute(value, axis, [(i, (i + by) % size) for i in range(size)])


def rotary_tables(lengths, half_size):
    starts = jnp.cumsum(lengths, axis=-1) - lengths
    freqs = ROPE_BASE ** (-jnp.arange(half_size, dtype=jnp.float32) * 2.0 / (2 * half_size))
    angles = starts.astype(jnp.float32)[..., None] * freqs
    return (jnp.cos(angles), jnp.sin(angles))


def normalize(widened):
    return widened * lax.rsqrt(jnp.mean(widened * widened, axis=-1, keepdims=True) + EPSILON)


def rotate(values, cosine, sine):
    half_size = values.shape[-1] // 2
    extra = (1,) * (values.ndim - 3)
    cosine_wide = cosine.reshape(cosine.shape[:2] + extra + cosine.shape[2:])
    sine_wide = sine.reshape(sine.shape[:2] + extra + sine.shape[2:])
    first_half = values[..., :half_size]
    second_half = values[..., half_size:]
    return jnp.concatenate(
        [
            first_half * cosine_wide - second_half * sine_wide,
            first_half * sine_wide + second_half * cosine_wide,
        ],
        axis=-1,
    )


def attend(packed, cosine, sine, rounding):
    seq_count = packed.shape[0]
    patch_count = packed.shape[1]
    group_size = HEADS // KV_HEADS
    query_width = HEADS * QK_DIM
    key_width = KV_HEADS * QK_DIM
    queries = packed[..., :query_width].reshape(
        seq_count, patch_count, KV_HEADS, group_size, QK_DIM
    )
    keys_part = packed[..., query_width : query_width + key_width].reshape(
        seq_count, patch_count, KV_HEADS, QK_DIM
    )
    values_part = packed[..., query_width + key_width :].reshape(
        seq_count, patch_count, KV_HEADS, V_DIM
    )
    queries = rotate(queries, cosine, sine)
    keys_part = rotate(keys_part, cosine, sine)
    scores = jnp.einsum("bqgrd,bkgd->bgrqk", queries, keys_part) / math.sqrt(QK_DIM)
    causal = jnp.tril(jnp.ones((patch_count, patch_count), jnp.float32))
    raised = jnp.exp(jnp.where(causal > 0.5, scores, 0.0)) * causal
    probs = raised / jnp.sum(raised, axis=-1, keepdims=True)
    if rounding:
        probs = lax.optimization_barrier(probs.astype(jnp.bfloat16)).astype(jnp.float32)
    mixed = jnp.einsum("bgrqk,bkgv->bqgrv", probs, values_part)
    return mixed.reshape(seq_count, patch_count, HEADS * V_DIM)


def layer_forward(inputs, weight, cosine, sine):
    widened = inputs.astype(jnp.float32)
    normed = normalize(widened).astype(jnp.bfloat16)
    flat_normed = normed.reshape(-1, normed.shape[-1])
    qkv = jnp.dot(flat_normed, weight, preferred_element_type=jnp.float32).astype(jnp.bfloat16)
    qkv = qkv.reshape(inputs.shape[0], inputs.shape[1], weight.shape[1])
    mixed = attend(qkv.astype(jnp.float32), cosine, sine, True)
    return ((widened + mixed).astype(jnp.bfloat16), normed, qkv)


def layer_backward(upstream, inputs, qkv, weight, cosine, sine):
    grad_up = upstream.astype(jnp.float32)

    def plain_attend(packed):
        return attend(packed, cosine, sine, False)

    _, attend_pull = jax.vjp(plain_attend, qkv.astype(jnp.float32))
    grad_qkv = attend_pull(grad_up)[0].astype(jnp.bfloat16)
    flat_grad = grad_qkv.reshape(-1, grad_qkv.shape[-1])
    grad_normed = lax.dot_general(
        flat_grad, weight, (((1,), (1,)), ((), ())), preferred_element_type=jnp.float32
    )
    grad_normed = grad_normed.reshape(inputs.shape)
    _, norm_pull = jax.vjp(normalize, inputs.astype(jnp.float32))
    grad_inputs = norm_pull(grad_normed)[0]
    return ((grad_up + grad_inputs).astype(jnp.bfloat16), grad_qkv)


def local(patches, lengths, cotangent, weights):
    sections = lax.axis_size("section")
    position = lax.axis_index("section")
    groups = lax.axis_size("dp")
    micro_count = patches.shape[0]
    patch_count = patches.shape[1]
    cosine, sine = rotary_tables(lengths, QK_DIM // 2)
    local_weights = weights[:, 0]
    row_count = local_weights.shape[1]
    width = local_weights.shape[2]
    tick_count = micro_count + 2 * sections - 1
    zero_index = jnp.int32(0)

    def table_rows(slot):
        return (
            lax.dynamic_index_in_dim(cosine, slot, 0, keepdims=True),
            lax.dynamic_index_in_dim(sine, slot, 0, keepdims=True),
        )

    def forward_tick(tick_index, state, first_weight, second_weight):
        outgoing, inputs_store, normed_store, qkv_store = state
        incoming = shifted(outgoing, "section", 1)
        first_micro = tick_index - position
        second_micro = first_micro - sections
        first_live = (first_micro >= 0) & (first_micro < micro_count)
        second_live = (second_micro >= 0) & (second_micro < micro_count)
        selector = jnp.where(first_live, 1, jnp.where(second_live, 2, 0))
        first_slot = jnp.clip(first_micro, 0, micro_count - 1)
        second_slot = jnp.clip(second_micro, 0, micro_count - 1)
        fresh = lax.dynamic_index_in_dim(patches, first_slot, 0, keepdims=False)
        first_source = jnp.where(position == 0, fresh, incoming)

        def run_layer(virtual, slot, source, weight):
            cosine_row, sine_row = table_rows(slot)
            output, normed, qkv = layer_forward(source[None], weight, cosine_row, sine_row)
            place = (jnp.int32(virtual), slot, zero_index, zero_index)
            return (
                output[0],
                lax.dynamic_update_slice(inputs_store, source[None, None], place),
                lax.dynamic_update_slice(normed_store, normed[None], place),
                lax.dynamic_update_slice(qkv_store, qkv[None], place),
            )

        def forward_stay_still():
            return (outgoing, inputs_store, normed_store, qkv_store)

        def forward_first_run():
            return run_layer(0, first_slot, first_source, first_weight)

        def forward_second_run():
            return run_layer(1, second_slot, incoming, second_weight)

        return lax.switch(selector, [forward_stay_still, forward_first_run, forward_second_run])

    forward_state = (
        jnp.zeros((patch_count, D), jnp.bfloat16),
        jnp.zeros((2, micro_count, patch_count, D), jnp.bfloat16),
        jnp.zeros((2, micro_count, patch_count, D), jnp.bfloat16),
        jnp.zeros((2, micro_count, patch_count, width), jnp.bfloat16),
    )
    gathered = lax.all_gather(local_weights, "dp", axis=1, tiled=True)
    first_weight = gathered[0]
    second_weight = gathered[1]
    forward_state = lax.fori_loop(
        0,
        tick_count,
        partial(forward_tick, first_weight=first_weight, second_weight=second_weight),
        forward_state,
    )
    _, inputs_store, normed_store, qkv_store = forward_state

    def backward_tick(tick_index, state):
        outgoing, grad_store = state
        incoming = shifted(outgoing, "section", -1)
        second_micro = tick_index - (sections - 1 - position)
        first_micro = second_micro - sections
        first_live = (first_micro >= 0) & (first_micro < micro_count)
        second_live = (second_micro >= 0) & (second_micro < micro_count)
        selector = jnp.where(second_live, 2, jnp.where(first_live, 1, 0))
        first_slot = jnp.clip(first_micro, 0, micro_count - 1)
        second_slot = jnp.clip(second_micro, 0, micro_count - 1)
        fresh = lax.dynamic_index_in_dim(cotangent, second_slot, 0, keepdims=False)
        second_source = jnp.where(position == sections - 1, fresh, incoming)

        def run_layer(virtual, slot, source, weight):
            cosine_row, sine_row = table_rows(slot)
            stored_inputs = lax.dynamic_index_in_dim(inputs_store[virtual], slot, 0, keepdims=True)
            stored_qkv = lax.dynamic_index_in_dim(qkv_store[virtual], slot, 0, keepdims=True)
            grad_inputs, grad_qkv = layer_backward(
                source[None], stored_inputs, stored_qkv, weight, cosine_row, sine_row
            )
            place = (jnp.int32(virtual), slot, zero_index, zero_index)
            return (grad_inputs[0], lax.dynamic_update_slice(grad_store, grad_qkv[None], place))

        def backward_stay_still():
            return (outgoing, grad_store)

        def backward_first_run():
            return run_layer(0, first_slot, incoming, first_weight)

        def backward_second_run():
            return run_layer(1, second_slot, second_source, second_weight)

        return lax.switch(selector, [backward_stay_still, backward_first_run, backward_second_run])

    def layer_term(virtual, grad_store):
        normed_rows = normed_store[virtual].reshape(micro_count * patch_count, D)
        grad_rows = grad_store[virtual].reshape(micro_count * patch_count, width)
        product = lax.dot_general(
            normed_rows, grad_rows, (((0,), (0,)), ((), ())), preferred_element_type=jnp.float32
        )
        return product.astype(jnp.bfloat16)

    def add_groups(received):
        return jnp.sum(received.reshape(groups, row_count, width).astype(jnp.float32), axis=0)

    backward_state = (
        jnp.zeros((patch_count, D), jnp.bfloat16),
        jnp.zeros((2, micro_count, patch_count, width), jnp.bfloat16),
    )
    backward_state = lax.fori_loop(0, tick_count, backward_tick, backward_state)
    terms = jnp.stack([layer_term(0, backward_state[1]), layer_term(1, backward_state[1])])
    received = lax.all_to_all(terms, "dp", split_axis=1, concat_axis=1, tiled=True)
    result = jnp.stack([add_groups(received[0]), add_groups(received[1])])
    return result[:, None]


def solution(mesh):
    return jax.shard_map(
        local,
        mesh=mesh,
        in_specs=(
            P("dp", None, None),
            P("dp", None),
            P("dp", None, None),
            P(None, "section", "dp", None),
        ),
        out_specs=P(None, "section", "dp", None),
        check_vma=False,
    )
```

profile of v0, /device:TPU:1, one launch (start us, length us, event | category | flops | bytes accessed | tf_op | source)
XLA Modules:
  0.0 1310.6 jit_solution(4144159355346928819)
XLA Ops:
  9.4 93.3 %all-gather.3.cloned.1.call-done = bf16[2,1,2048,1792]{3,2,1,0:T(8,128)(2,1)} async-done(((bf16[2,1,64,1792]{3,2,1,0:T(8,128)(2,1)}), bf16[2,1,2048,1792]{3,2,1,0:T(8,128)(2,1)}) %all-gather.3.cloned.1.call-update) | async-done | bytes 14680080 | tf_op jit(solution)/shard_map/all_gather | solution.py:167
  102.7 10.3 slice_bitcast_fusion
  114.0 288.4 %while.42 = (s32[]{:T(128)}, bf16[16,2048]{1,0:T(8,128)(2,1)}, bf16[2,8,16,2048]{3,2,1,0:T(8,128)(2,1)S(1)}, bf16[2,8,16,2048]{3,2,1,0:T(8,128)(2,1)S(1)}, bf16[...) while((s32[]{:T(128)}, bf16[16,2048]{1,0:T(8,128)(2,1)}, ...), condition=%wide.region_9.10_spmd.clone.clone, body=%wide.region_1.9_spmd.clone.clone.sunk | while | flops 119690272 | bytes 10172850 | solution.py:170
  403.7 353.4 %while.43 = (s32[]{:T(128)}, bf16[16,2048]{1,0:T(8,128)(2,1)S(1)}, bf16[2,8,16,1792]{3,2,1,0:T(8,128)(2,1)}, s32[]{:T(128)}, bf16[2,8,16,1792]{3,2,1,0:T(8,128)(...) while((s32[]{:T(128)}, bf16[16,2048]{1,0:T(8,128)(2,1)S(1)}, ...), condition=%wide.region_22.23_spmd.clone.clone, body=%wide.region_10.22_spmd.clone.clone.sunk | while | flops 122121808 | bytes 12898974 | solution.py:227
  412.9 15.4 %collective-permute-start.1 = (bf16[16,2048]{1,0:T(8,128)(2,1)S(1)}, bf16[16,2048]{1,0:T(8,128)(2,1)S(1)}, u32[]{:S(2)}, u32[]{:S(2)}) collective-permute-start(bf16[16,2048]{1,0:T(8,128)(2,1)S(1)} %get-tuple-element.1353), channel_id=1, source_target_pairs={{0,224},{32,0},{64,32},{96,64},{128,96},{160,128},{192,160},{224,1... | collective-permute-start | bytes 196616 | tf_op jit(solution)/shard_map/while/body/eval_jaxpr/ppermute | solution.py:22
  429.6 15.4 %collective-permute-start.1 = (bf16[16,2048]{1,0:T(8,128)(2,1)S(1)}, bf16[16,2048]{1,0:T(8,128)(2,1)S(1)}, u32[]{:S(2)}, u32[]{:S(2)}) collective-permute-start(bf16[16,2048]{1,0:T(8,128)(2,1)S(1)} %get-tuple-element.1353), channel_id=1, source_target_pairs={{0,224},{32,0},{64,32},{96,64},{128,96},{160,128},{192,160},{224,1... | collective-permute-start | bytes 196616 | tf_op jit(solution)/shard_map/while/body/eval_jaxpr/ppermute | solution.py:22
  446.3 15.4 %collective-permute-start.1 = (bf16[16,2048]{1,0:T(8,128)(2,1)S(1)}, bf16[16,2048]{1,0:T(8,128)(2,1)S(1)}, u32[]{:S(2)}, u32[]{:S(2)}) collective-permute-start(bf16[16,2048]{1,0:T(8,128)(2,1)S(1)} %get-tuple-element.1353), channel_id=1, source_target_pairs={{0,224},{32,0},{64,32},{96,64},{128,96},{160,128},{192,160},{224,1... | collective-permute-start | bytes 196616 | tf_op jit(solution)/shard_map/while/body/eval_jaxpr/ppermute | solution.py:22
  463.0 15.4 %collective-permute-start.1 = (bf16[16,2048]{1,0:T(8,128)(2,1)S(1)}, bf16[16,2048]{1,0:T(8,128)(2,1)S(1)}, u32[]{:S(2)}, u32[]{:S(2)}) collective-permute-start(bf16[16,2048]{1,0:T(8,128)(2,1)S(1)} %get-tuple-element.1353), channel_id=1, source_target_pairs={{0,224},{32,0},{64,32},{96,64},{128,96},{160,128},{192,160},{224,1... | collective-permute-start | bytes 196616 | tf_op jit(solution)/shard_map/while/body/eval_jaxpr/ppermute | solution.py:22
  479.7 15.4 %collective-permute-start.1 = (bf16[16,2048]{1,0:T(8,128)(2,1)S(1)}, bf16[16,2048]{1,0:T(8,128)(2,1)S(1)}, u32[]{:S(2)}, u32[]{:S(2)}) collective-permute-start(bf16[16,2048]{1,0:T(8,128)(2,1)S(1)} %get-tuple-element.1353), channel_id=1, source_target_pairs={{0,224},{32,0},{64,32},{96,64},{128,96},{160,128},{192,160},{224,1... | collective-permute-start | bytes 196616 | tf_op jit(solution)/shard_map/while/body/eval_jaxpr/ppermute | solution.py:22
  496.4 15.4 %collective-permute-start.1 = (bf16[16,2048]{1,0:T(8,128)(2,1)S(1)}, bf16[16,2048]{1,0:T(8,128)(2,1)S(1)}, u32[]{:S(2)}, u32[]{:S(2)}) collective-permute-start(bf16[16,2048]{1,0:T(8,128)(2,1)S(1)} %get-tuple-element.1353), channel_id=1, source_target_pairs={{0,224},{32,0},{64,32},{96,64},{128,96},{160,128},{192,160},{224,1... | collective-permute-start | bytes 196616 | tf_op jit(solution)/shard_map/while/body/eval_jaxpr/ppermute | solution.py:22
  513.1 15.4 %collective-permute-start.1 = (bf16[16,2048]{1,0:T(8,128)(2,1)S(1)}, bf16[16,2048]{1,0:T(8,128)(2,1)S(1)}, u32[]{:S(2)}, u32[]{:S(2)}) collective-permute-start(bf16[16,2048]{1,0:T(8,128)(2,1)S(1)} %get-tuple-element.1353), channel_id=1, source_target_pairs={{0,224},{32,0},{64,32},{96,64},{128,96},{160,128},{192,160},{224,1... | collective-permute-start | bytes 196616 | tf_op jit(solution)/shard_map/while/body/eval_jaxpr/ppermute | solution.py:22
  529.8 10.0 conditional.9
  547.0 10.0 conditional.9
  563.1 10.0 conditional.9
  578.9 10.0 conditional.9
  594.8 10.0 conditional.9
  610.6 10.0 conditional.9
  626.5 10.0 conditional.9
  642.3 10.0 conditional.9
  764.1 103.4 %copy.135 = bf16[2,2048,1792]{2,0,1:T(2,128)(2,1)} copy(bf16[2,2048,1792]{2,1,0:T(8,128)(2,1)S(1)} %pad_maximum_fusion) | data formatting | bytes 29360128 | tf_op jit(solution)/shard_map/stack | solution.py:228
  867.5 379.0 %all_to_all.5 = bf16[2,2048,1792]{2,0,1:T(2,128)(2,1)S(1)} all-to-all(bf16[2,2048,1792]{2,0,1:T(2,128)(2,1)} %copy.135), channel_id=1, replica_groups=mesh['section'=8,'dp'=32] {'dp'}, dimensions={1} | all-to-all | bytes 29360128 | tf_op jit(solution)/shard_map/all_to_all | solution.py:229
  1246.5 21.9 %slice_convert_fusion.1 = (f32[1,2048,1792]{2,0,1:T(1,128)}, f32[1,2048,1792]{2,0,1:T(1,128)}) fusion(bf16[2,2048,1792]{2,0,1:T(2,128)(2,1)S(1)} %all_to_all.5), kind=kLoop, calls=%fused_computation.216 | loop fusion | flops 7340032 | bytes 44040192 | tf_op jit(solution)/shard_map/convert_element_type | solution.py:221
  1268.4 11.3 copy.180
  1279.7 11.3 copy.181
  (1216 shorter events, 735.5 us)
Async XLA Ops:
  6.5 96.2 %all-gather.3.cloned.1.call-start = ((), (), s32[]{:S(2)}) async-start(), calls=%async_computation.1 | async-start | bytes 15138816 | tf_op jit(solution)/shard_map/all_gather | solution.py:167
  142.6 7.0 collective-permute-start
  156.9 7.0 collective-permute-start
  171.2 7.0 collective-permute-start
  199.9 7.0 collective-permute-start
  228.5 7.0 collective-permute-start
  242.0 7.0 collective-permute-start
  255.4 7.0 collective-permute-start
  282.4 7.8 collective-permute-start
  344.1 8.2 collective-permute-start
  352.2 9.8 collective-permute-start
  362.1 10.4 collective-permute-start
  372.5 10.6 collective-permute-start
  383.1 9.4 collective-permute-start
  392.6 9.8 collective-permute-start
  403.7 9.2 collective-permute-start.1
  412.9 16.7 %collective-permute-start.1 = (bf16[16,2048]{1,0:T(8,128)(2,1)S(1)}, bf16[16,2048]{1,0:T(8,128)(2,1)S(1)}, u32[]{:S(2)}, u32[]{:S(2)}) collective-permute-start(bf16[16,2048]{1,0:T(8,128)(2,1)S(1)} %get-tuple-element.1353), channel_id=1, source_target_pairs={{0,224},{32,0},{64,32},{96,64},{128,96},{160,128},{192,160},{224,1... | collective-permute-start | bytes 196616 | tf_op jit(solution)/shard_map/while/body/eval_jaxpr/ppermute | solution.py:22
  429.6 16.7 %collective-permute-start.1 = (bf16[16,2048]{1,0:T(8,128)(2,1)S(1)}, bf16[16,2048]{1,0:T(8,128)(2,1)S(1)}, u32[]{:S(2)}, u32[]{:S(2)}) collective-permute-start(bf16[16,2048]{1,0:T(8,128)(2,1)S(1)} %get-tuple-element.1353), channel_id=1, source_target_pairs={{0,224},{32,0},{64,32},{96,64},{128,96},{160,128},{192,160},{224,1... | collective-permute-start | bytes 196616 | tf_op jit(solution)/shard_map/while/body/eval_jaxpr/ppermute | solution.py:22
  446.3 16.7 %collective-permute-start.1 = (bf16[16,2048]{1,0:T(8,128)(2,1)S(1)}, bf16[16,2048]{1,0:T(8,128)(2,1)S(1)}, u32[]{:S(2)}, u32[]{:S(2)}) collective-permute-start(bf16[16,2048]{1,0:T(8,128)(2,1)S(1)} %get-tuple-element.1353), channel_id=1, source_target_pairs={{0,224},{32,0},{64,32},{96,64},{128,96},{160,128},{192,160},{224,1... | collective-permute-start | bytes 196616 | tf_op jit(solution)/shard_map/while/body/eval_jaxpr/ppermute | solution.py:22
  463.0 16.7 %collective-permute-start.1 = (bf16[16,2048]{1,0:T(8,128)(2,1)S(1)}, bf16[16,2048]{1,0:T(8,128)(2,1)S(1)}, u32[]{:S(2)}, u32[]{:S(2)}) collective-permute-start(bf16[16,2048]{1,0:T(8,128)(2,1)S(1)} %get-tuple-element.1353), channel_id=1, source_target_pairs={{0,224},{32,0},{64,32},{96,64},{128,96},{160,128},{192,160},{224,1... | collective-permute-start | bytes 196616 | tf_op jit(solution)/shard_map/while/body/eval_jaxpr/ppermute | solution.py:22
  479.7 16.7 %collective-permute-start.1 = (bf16[16,2048]{1,0:T(8,128)(2,1)S(1)}, bf16[16,2048]{1,0:T(8,128)(2,1)S(1)}, u32[]{:S(2)}, u32[]{:S(2)}) collective-permute-start(bf16[16,2048]{1,0:T(8,128)(2,1)S(1)} %get-tuple-element.1353), channel_id=1, source_target_pairs={{0,224},{32,0},{64,32},{96,64},{128,96},{160,128},{192,160},{224,1... | collective-permute-start | bytes 196616 | tf_op jit(solution)/shard_map/while/body/eval_jaxpr/ppermute | solution.py:22
  496.4 16.7 %collective-permute-start.1 = (bf16[16,2048]{1,0:T(8,128)(2,1)S(1)}, bf16[16,2048]{1,0:T(8,128)(2,1)S(1)}, u32[]{:S(2)}, u32[]{:S(2)}) collective-permute-start(bf16[16,2048]{1,0:T(8,128)(2,1)S(1)} %get-tuple-element.1353), channel_id=1, source_target_pairs={{0,224},{32,0},{64,32},{96,64},{128,96},{160,128},{192,160},{224,1... | collective-permute-start | bytes 196616 | tf_op jit(solution)/shard_map/while/body/eval_jaxpr/ppermute | solution.py:22
  513.1 16.7 %collective-permute-start.1 = (bf16[16,2048]{1,0:T(8,128)(2,1)S(1)}, bf16[16,2048]{1,0:T(8,128)(2,1)S(1)}, u32[]{:S(2)}, u32[]{:S(2)}) collective-permute-start(bf16[16,2048]{1,0:T(8,128)(2,1)S(1)} %get-tuple-element.1353), channel_id=1, source_target_pairs={{0,224},{32,0},{64,32},{96,64},{128,96},{160,128},{192,160},{224,1... | collective-permute-start | bytes 196616 | tf_op jit(solution)/shard_map/while/body/eval_jaxpr/ppermute | solution.py:22
  539.8 7.2 collective-permute-start.1
  (26 other events, 138.7 us)
Sparse Core Ops, SparseCore 0:
  9.2 93.5 all-gather.2
where the time goes:
time: 1310 us
  blocking collectives  379 us (29%)
  waiting for transfers between devices  264 us (20%)
  matrix products  187 us (14%)
  local copies, waits for them, and re-layouts  172 us (13%)
  starting transfers between devices  164 us (13%)
  other arithmetic  126 us (10%)
  between operations  13.5 us (1%)
    all_to_all x1, blocking collectives, local(): lax.all_to_all(terms, 'dp', split_axis=1, concat_axis=1, tiled=True)  379 us
    ppermute x46, waiting for transfers between devices, shifted(): lax.ppermute(value, axis, [(i, (i + by) % size) for i in range(size)])  170 us
    ppermute x46, starting transfers between devices, shifted(): lax.ppermute(value, axis, [(i, (i + by) % size) for i in range(size)])  164 us
    another operation x1, local copies, waits for them, and re-layouts, local(): jnp.stack([layer_term(0, backward_state[1]), layer_term(1, backward_state...  103 us
    all_gather x1, waiting for transfers between devices, local(): gathered = lax.all_gather(local_weights, 'dp', axis=1, tiled=True)  93.3 us
    dot_general x16, matrix products, layer_backward(): lax.dot_general(flat_grad, weight, (((1,), (1,)), ((), ())), preferred_el...  83.2 us
    dot_general x16, matrix products, layer_forward(): jnp.dot(flat_normed, weight, preferred_element_type=jnp.float32)  67 us
    sin x46, other arithmetic, rotary_tables(): return (jnp.cos(angles), jnp.sin(angles))  44.3 us
  transfers between devices with their start and end apart: 47, of which 47 were waited for; matrix products, arithmetic and copies ran while one was open for 4% of the time, Pallas kernels for 0%

commit v1 on v0

v1 whole, which is shorter than its diff:
```python
import jax
import jax.numpy as jnp
from jax import lax
from jax.experimental import pallas as pl
from jax.experimental.pallas import tpu as pltpu
from jax.sharding import Mesh, PartitionSpec as P

D = 2048
HEADS = 16
KV_HEADS = 4
GROUP = HEADS // KV_HEADS
QK_DIM = 64
V_DIM = 128
PATCH = 16
QUERY_WIDTH = HEADS * QK_DIM
KEY_WIDTH = KV_HEADS * QK_DIM
VALUE_START = QUERY_WIDTH + KEY_WIDTH
WIDTH = VALUE_START + KV_HEADS * V_DIM
ROPE_BASE = 500000.0
EPSILON = 1e-05
LAYERS = 4
LANES = 128
COLUMNS = 256
STAGE_X = (0, 2, 1, 3)
F32 = jnp.float32
BF16 = jnp.bfloat16


def dot(a, b, a_dim, b_dim):
    return lax.dot_general(
        a, b, (((a_dim,), (b_dim,)), ((), ())), preferred_element_type=F32
    )


def lane_index(rows):
    return lax.broadcasted_iota(jnp.int32, (rows, LANES), 1)


def swap_halves(chunk):
    lanes = lane_index(chunk.shape[0])
    ahead = pltpu.roll(chunk, LANES - QK_DIM // 2, 1)
    behind = pltpu.roll(chunk, QK_DIM // 2, 1)
    return jnp.where(lanes % QK_DIM < QK_DIM // 2, ahead, behind)


def score_mask(tokens):
    rows = lax.broadcasted_iota(jnp.int32, (GROUP * tokens, tokens), 0) % tokens
    columns = lax.broadcasted_iota(jnp.int32, (GROUP * tokens, tokens), 1)
    return (rows // PATCH == columns // PATCH) & (columns <= rows)


def rotated_chunk(qkv, index, cosine, sine):
    chunk = qkv[:, index * LANES : (index + 1) * LANES]
    return chunk * cosine + swap_halves(chunk) * sine


def group_parts(qkv, group, cosine, sine):
    low = lane_index(qkv.shape[0]) < QK_DIM
    rows = []
    for pair in range(2):
        chunk = rotated_chunk(qkv, 2 * group + pair, cosine, sine)
        rows.append(jnp.where(low, chunk, 0.0))
        rows.append(jnp.where(low, 0.0, chunk))
    queries = jnp.concatenate(rows, axis=0).astype(BF16)
    chunk = rotated_chunk(qkv, QUERY_WIDTH // LANES + group // 2, cosine, sine)
    other = pltpu.roll(chunk, QK_DIM, 1)
    keys_part = jnp.where(low, chunk, other) if group % 2 == 0 else jnp.where(low, other, chunk)
    values_part = qkv[:, VALUE_START + group * V_DIM : VALUE_START + (group + 1) * V_DIM]
    return queries, keys_part.astype(BF16), values_part.astype(BF16)


def group_probs(queries, keys_part, mask):
    scores = dot(queries, keys_part, 1, 1) * (1.0 / QK_DIM**0.5)
    raised = jnp.where(mask, jnp.exp(jnp.where(mask, scores, 0.0)), 0.0)
    return raised / jnp.sum(raised, axis=-1, keepdims=True)


def weight_copies(layer, weights_ref, held, sems):
    copies = []
    for core in range(2):
        for low in range(2):
            copies.append(
                pltpu.make_async_copy(
                    weights_ref.at[layer, :, core, low],
                    held.at[layer, :, low, core],
                    sems.at[layer, core, low],
                )
            )
    return copies


def forward_kernel(
    x_ref, cosine_ref, sine_ref, weights_ref, last_ref, inputs_ref, normed_ref, qkv_ref,
    held, current, sems,
):
    layer = pl.program_id(0)
    tokens = x_ref.shape[0]

    @pl.when(layer == 0)
    def start():
        for each in range(LAYERS):
            for copy in weight_copies(each, weights_ref, held, sems):
                copy.start()
        current[...] = x_ref[...]

    x = current[...]
    inputs_ref[0] = x
    wide = x.astype(F32)
    scale = lax.rsqrt(jnp.mean(wide * wide, axis=-1, keepdims=True) + EPSILON)
    normed = (wide * scale).astype(BF16)
    normed_ref[0] = normed
    for copy in weight_copies(layer, weights_ref, held, sems):
        copy.wait()
    for step in range(WIDTH // COLUMNS):
        columns = slice(step * COLUMNS, (step + 1) * COLUMNS)
        block = held[layer, :, :, :, :, columns].reshape(D, COLUMNS)
        qkv_ref[0, :, columns] = dot(normed, block, 1, 0).astype(BF16)
    qkv = qkv_ref[0].astype(F32)
    cosine = cosine_ref[...]
    sine = sine_ref[...]
    mask = score_mask(tokens)
    for group in range(KV_HEADS):
        queries, keys_part, values_part = group_parts(qkv, group, cosine, sine)
        probs = group_probs(queries, keys_part, mask).astype(BF16)
        mixed = dot(probs, values_part, 1, 0)
        for r in range(GROUP):
            head = group * GROUP + r
            span = slice(head * V_DIM, (head + 1) * V_DIM)
            current[:, span] = (
                x[:, span].astype(F32) + mixed[r * tokens : (r + 1) * tokens]
            ).astype(BF16)

    @pl.when(layer == LAYERS - 1)
    def finish():
        last_ref[...] = current[...]


def backward_kernel(
    g_ref, cosine_ref, sine_ref, inputs_ref, qkv_ref, weights_ref, first_ref, grad_ref,
    held, current, sems,
):
    step = pl.program_id(0)
    layer = LAYERS - 1 - step
    tokens = g_ref.shape[0]

    @pl.when(step == 0)
    def start():
        for each in reversed(range(LAYERS)):
            for copy in weight_copies(each, weights_ref, held, sems):
                copy.start()
        current[...] = g_ref[...]

    upstream = current[...]
    cosine = cosine_ref[...]
    sine = sine_ref[...]
    mask = score_mask(tokens)
    low = lane_index(tokens) < QK_DIM
    qkv = qkv_ref[0].astype(F32)
    key_grads = []
    for group in range(KV_HEADS):
        queries, keys_part, values_part = group_parts(qkv, group, cosine, sine)
        probs = group_probs(queries, keys_part, mask)
        rows = [
            upstream[:, (group * GROUP + r) * V_DIM : (group * GROUP + r + 1) * V_DIM]
            for r in range(GROUP)
        ]
        stacked = jnp.concatenate(rows, axis=0)
        grad_probs = dot(stacked, values_part, 1, 1)
        weighted = jnp.sum(probs * grad_probs, axis=-1, keepdims=True)
        grad_scores = (probs * (grad_probs - weighted) * (1.0 / QK_DIM**0.5)).astype(BF16)
        grad_values = dot(probs.astype(BF16), stacked, 0, 0)
        grad_ref[0, :, VALUE_START + group * V_DIM : VALUE_START + (group + 1) * V_DIM] = (
            grad_values.astype(BF16)
        )
        grad_queries = dot(grad_scores, keys_part, 1, 0)
        for pair in range(2):
            first = grad_queries[2 * pair * tokens : (2 * pair + 1) * tokens]
            second = grad_queries[(2 * pair + 1) * tokens : (2 * pair + 2) * tokens]
            chunk = jnp.where(low, first, second)
            chunk = chunk * cosine - swap_halves(chunk) * sine
            start_at = (2 * group + pair) * LANES
            grad_ref[0, :, start_at : start_at + LANES] = chunk.astype(BF16)
        halves = dot(grad_scores, queries, 0, 0)
        key_grads.append(halves + pltpu.roll(halves, QK_DIM, 1))
    for pair in range(2):
        chunk = jnp.where(low, key_grads[2 * pair], key_grads[2 * pair + 1])
        chunk = chunk * cosine - swap_halves(chunk) * sine
        start_at = QUERY_WIDTH + pair * LANES
        grad_ref[0, :, start_at : start_at + LANES] = chunk.astype(BF16)
    for copy in weight_copies(layer, weights_ref, held, sems):
        copy.wait()
    grad_qkv = grad_ref[0]
    wide = inputs_ref[0].astype(F32)
    parts = []
    for z in range(D // COLUMNS):
        block = held[layer, z].reshape(COLUMNS, WIDTH)
        parts.append(dot(grad_qkv, block, 1, 1))
    grad_normed = jnp.concatenate(parts, axis=1)
    scale = lax.rsqrt(jnp.mean(wide * wide, axis=-1, keepdims=True) + EPSILON)
    inner = jnp.mean(grad_normed * wide, axis=-1, keepdims=True)
    grad_inputs = scale * grad_normed - wide * (scale * scale * scale * inner)
    current[...] = (upstream.astype(F32) + grad_inputs).astype(BF16)

    @pl.when(step == LAYERS - 1)
    def finish():
        first_ref[...] = current[...]


def whole(shape):
    return pl.BlockSpec(shape, lambda i: (0,) * len(shape))


def scratches(tokens):
    return [
        pltpu.VMEM((LAYERS, 8, 2, 2, 64, WIDTH), BF16),
        pltpu.VMEM((tokens, D), BF16),
        pltpu.SemaphoreType.DMA((LAYERS, 2, 2)),
    ]


PARAMS = dict(vmem_limit_bytes=52 * 1024 * 1024)


def run_forward(x, cosine, sine, weights):
    tokens = x.shape[0]
    per_layer = lambda width: pl.BlockSpec((1, tokens, width), lambda i: (i, 0, 0))
    return pl.pallas_call(
        forward_kernel,
        grid=(LAYERS,),
        in_specs=[
            whole((tokens, D)),
            whole((tokens, LANES)),
            whole((tokens, LANES)),
            pl.BlockSpec(memory_space=pl.ANY),
        ],
        out_specs=[whole((tokens, D)), per_layer(D), per_layer(D), per_layer(WIDTH)],
        out_shape=[
            jax.ShapeDtypeStruct((tokens, D), BF16),
            jax.ShapeDtypeStruct((LAYERS, tokens, D), BF16),
            jax.ShapeDtypeStruct((LAYERS, tokens, D), BF16),
            jax.ShapeDtypeStruct((LAYERS, tokens, WIDTH), BF16),
        ],
        scratch_shapes=scratches(tokens),
        compiler_params=pltpu.CompilerParams(**PARAMS),
        cost_estimate=pl.CostEstimate(
            flops=2 * LAYERS * tokens * D * WIDTH,
            bytes_accessed=2 * LAYERS * D * WIDTH,
            transcendentals=0,
        ),
        name="forward_stage",
    )(x, cosine, sine, weights)


def run_backward(g, cosine, sine, inputs, qkv, weights):
    tokens = g.shape[0]
    per_layer = lambda width: pl.BlockSpec((1, tokens, width), lambda i: (LAYERS - 1 - i, 0, 0))
    return pl.pallas_call(
        backward_kernel,
        grid=(LAYERS,),
        in_specs=[
            whole((tokens, D)),
            whole((tokens, LANES)),
            whole((tokens, LANES)),
            per_layer(D),
            per_layer(WIDTH),
            pl.BlockSpec(memory_space=pl.ANY),
        ],
        out_specs=[whole((tokens, D)), per_layer(WIDTH)],
        out_shape=[
            jax.ShapeDtypeStruct((tokens, D), BF16),
            jax.ShapeDtypeStruct((LAYERS, tokens, WIDTH), BF16),
        ],
        scratch_shapes=scratches(tokens),
        compiler_params=pltpu.CompilerParams(**PARAMS),
        cost_estimate=pl.CostEstimate(
            flops=2 * LAYERS * tokens * D * WIDTH,
            bytes_accessed=2 * LAYERS * D * WIDTH,
            transcendentals=0,
        ),
        name="backward_stage",
    )(g, cosine, sine, inputs, qkv, weights)


def ring(size, by):
    return [(i, (i + by) % size) for i in range(size)]


def from_partner(value):
    return lax.ppermute(value, "xl", ring(2, 1))


def both_halves(value, low_x):
    other = from_partner(value)
    return jnp.where(low_x == 0, jnp.stack([value, other]), jnp.stack([other, value]))


def rotary_tables(lengths):
    half = QK_DIM // 2
    starts = jnp.cumsum(lengths, axis=-1) - lengths
    freqs = ROPE_BASE ** (-jnp.arange(half, dtype=F32) * 2.0 / (2 * half))
    angles = starts.astype(F32).reshape(-1, 1) * freqs
    cosine, sine = jnp.cos(angles), jnp.sin(angles)
    return (
        jnp.concatenate([cosine] * 4, axis=1),
        jnp.concatenate([-sine, sine, -sine, sine], axis=1),
    )


def spread_over_y(value, place):
    pieces = [lax.dynamic_index_in_dim(value, place, 0, keepdims=False)]
    for by in (1, 3, 2):
        piece = lax.dynamic_index_in_dim(value, (place + by) % 4, 0, keepdims=False)
        pieces.append(lax.ppermute(piece, "y", ring(4, by)))
    return pieces


def local(patches, lengths, cotangent, weights):
    high_x = lax.axis_index("xh")
    low_x = lax.axis_index("xl")
    place = lax.axis_index("y")
    core = lax.axis_index("core")
    stage = high_x + 2 * low_x
    rows = weights.shape[2]

    own = lax.dynamic_index_in_dim(weights, low_x, 0, keepdims=False)[0]
    partner_own = lax.dynamic_index_in_dim(weights, 1 - low_x, 0, keepdims=False)[0]
    other = from_partner(partner_own)
    shard = jnp.where(low_x == 0, jnp.stack([own, other]), jnp.stack([other, own]))
    gathered = lax.all_gather(shard, ("y", "z", "core"), axis=0, tiled=False)
    gathered = gathered.reshape(LAYERS, 8, 2, 2, rows, WIDTH)

    pick = lambda v: lax.dynamic_slice_in_dim(v, 2 * place, 2, 0)
    tokens = 4 * PATCH
    x = both_halves(pick(patches).reshape(2 * PATCH, D), low_x).reshape(tokens, D)
    g = both_halves(pick(cotangent).reshape(2 * PATCH, D), low_x).reshape(tokens, D)
    span = both_halves(pick(lengths).astype(F32), low_x).reshape(4, PATCH).astype(jnp.int32)
    cosine, sine = rotary_tables(span)

    stored = (
        jnp.zeros((LAYERS, tokens, D), BF16),
        jnp.zeros((LAYERS, tokens, D), BF16),
        jnp.zeros((LAYERS, tokens, WIDTH), BF16),
    )
    for turn in range(LAYERS):
        if turn > 0:
            x = lax.ppermute(x, ("xh", "xl"), [(STAGE_X[turn - 1], STAGE_X[turn])])

        def active(x, stored):
            last, inputs, normed, qkv = run_forward(x, cosine, sine, gathered)
            return last, (inputs, normed, qkv)

        x, stored = lax.cond(stage == turn, active, lambda x, s: (x, s), x, stored)
    inputs, normed, qkv = stored

    grads = jnp.zeros((LAYERS, tokens, WIDTH), BF16)
    for turn in reversed(range(LAYERS)):
        if turn < LAYERS - 1:
            g = lax.ppermute(g, ("xh", "xl"), [(STAGE_X[turn + 1], STAGE_X[turn])])

        def active(g, grads):
            return tuple(run_backward(g, cosine, sine, inputs, qkv, gathered))

        g, grads = lax.cond(stage == turn, active, lambda g, s: (g, s), g, grads)

    normed_rows = jnp.concatenate(spread_over_y(normed, place))
    sibling = lambda v: lax.ppermute(v, "core", ring(2, 1))
    normed_rows = jnp.concatenate([normed_rows, sibling(normed_rows)])
    half = WIDTH // 2
    grad_rows = jnp.concatenate(spread_over_y(grads, place))
    mine = lax.dynamic_slice_in_dim(grad_rows, core * half, half, 1)
    sent = lax.dynamic_slice_in_dim(grad_rows, (1 - core) * half, half, 1)
    grad_rows = jnp.concatenate([mine, sibling(sent)])
    terms = dot(normed_rows, grad_rows, 0, 0).astype(BF16)
    total = lax.psum_scatter(terms, "z", scatter_dimension=0, tiled=True)
    total = total.reshape(2, 2, rows, half)
    mine = lax.dynamic_index_in_dim(total, core, 1, keepdims=False)
    received = sibling(lax.dynamic_index_in_dim(total, 1 - core, 1, keepdims=False))
    total = jnp.where(
        core == 0,
        jnp.concatenate([mine, received], axis=2),
        jnp.concatenate([received, mine], axis=2),
    )
    kept = lax.dynamic_index_in_dim(total, low_x, 0, keepdims=False)
    swapped = from_partner(lax.dynamic_index_in_dim(total, 1 - low_x, 0, keepdims=False))
    result = jnp.where(low_x == 0, jnp.stack([kept, swapped]), jnp.stack([swapped, kept]))
    return result.astype(F32)[:, None]


def solution(mesh):
    fine = Mesh(mesh.devices.reshape(2, 4, 8, 2, 2), ("xh", "y", "z", "xl", "core"))
    dp = ("z", "xl", "core")
    return jax.shard_map(
        local,
        mesh=fine,
        in_specs=(
            P(dp, None, None),
            P(dp, None),
            P(dp, None, None),
            P(None, ("xh", "y"), dp, None),
        ),
        out_specs=P(None, ("xh", "y"), dp, None),
        check_vma=False,
    )
```

time: 1310 us -> 437 us (0.33)
  blocking collectives: 379 us -> 0 us
  matrix products: 187 us -> 4.17 us
  local copies, waits for them, and re-layouts: 172 us -> 16.2 us
  starting transfers between devices: 164 us -> 28.5 us
  other arithmetic: 126 us -> 7.27 us
  waiting for transfers between devices: 264 us -> 331 us
  Pallas kernels: 0 us -> 36 us
    all_to_all x1 -> x0, blocking collectives: 379 us -> none  [local(): lax.all_to_all(terms, 'dp', split_axis=1, concat_axis=1, tiled=True)]
    dot_general x146 -> x1, matrix products: 187 us -> 4.17 us  [dot(): lax.dot_general(a, b, (((a_dim,), (b_dim,)), ((), ())), preferred_element...]
    ppermute x46 -> x20, starting transfers between devices: 164 us -> 28.5 us  [the longest x3 8.33 us: local(): sibling = lambda v: lax.ppermute(v, 'core', ring(2, 1))]
    another operation x39 -> x3, local copies, waits for them, and re-layouts: 106 us -> 1.11 us  [the longest x1 103 us: local(): jnp.stack([layer_term(0, backward_state[1]), layer_term(1, backward_state...]
    reduce_scatter x0 -> x1, waiting for transfers between devices: none -> 45.4 us  [local(): total = lax.psum_scatter(terms, 'z', scatter_dimension=0, tiled=True)]
    sin x46 -> x0, other arithmetic: 44.3 us -> none  [rotary_tables(): return (jnp.cos(angles), jnp.sin(angles))]
    all_gather x1, waiting for transfers between devices: 93.3 us -> 131 us  [local(): gathered = lax.all_gather(shard, ('y', 'z', 'core'), axis=0, tiled=False)]
    pallas_call x0 -> x2, Pallas kernels: none -> 36 us  [the longest x1 20.6 us: run_backward(): pl.pallas_call(backward_kernel, grid=(LAYERS,), in_specs=[whole((tokens,...]
  transfers between devices with their start and end apart: 47 -> 22, of which waited for: 47 -> 16; matrix products, arithmetic and copies ran while one was open for 4% -> 4% of each run, Pallas kernels for 0% -> 5%
where the time goes in v1:
time: 437 us
  waiting for transfers between devices  331 us (76%)
  Pallas kernels  36 us (8%)
  starting transfers between devices  28.5 us (7%)
  local copies, waits for them, and re-layouts  16.2 us (4%)
  between operations  13.6 us (3%)
  other arithmetic  7.27 us (2%)
    all_gather x1, waiting for transfers between devices, local(): gathered = lax.all_gather(shard, ('y', 'z', 'core'), axis=0, tiled=False)  131 us
    ppermute x3, waiting for transfers between devices, local(): g = lax.ppermute(g, ('xh', 'xl'), [(STAGE_X[turn + 1], STAGE_X[turn])])  118 us
    reduce_scatter x1, waiting for transfers between devices, local(): total = lax.psum_scatter(terms, 'z', scatter_dimension=0, tiled=True)  45.4 us
    pallas_call x1, Pallas kernels, run_backward(): pl.pallas_call(backward_kernel, grid=(LAYERS,), in_specs=[whole((tokens,...  20.6 us
    pallas_call x1, Pallas kernels, run_forward(): pl.pallas_call(forward_kernel, grid=(LAYERS,), in_specs=[whole((tokens, D...  15.4 us
    ppermute x5, waiting for transfers between devices, from_partner(): return lax.ppermute(value, 'xl', ring(2, 1))  15.2 us
    ppermute x6, waiting for transfers between devices, spread_over_y(): pieces.append(lax.ppermute(piece, 'y', ring(4, by)))  14.2 us
  transfers between devices with their start and end apart: 22, of which 16 were waited for; matrix products, arithmetic and copies ran while one was open for 4% of the time, Pallas kernels for 5%

profile of v1, /device:TPU:1, one launch (start us, length us, event | category | flops | bytes accessed | tf_op | source)
XLA Modules:
  0.0 436.7 jit_solution(8891438501540079046)
XLA Ops:
  7.7 2.1 collective-permute-start.2
  9.8 4.0 collective-permute-done.2
  14.7 2.3 collective-permute-start.1
  21.0 131.2 %all-gather.2.cloned.1.call-done = bf16[64,2,64,1792]{3,2,1,0:T(8,128)(2,1)} async-done(((bf16[1,2,64,1792]{3,2,1,0:T(8,128)(2,1)}), bf16[64,2,64,1792]{3,2,1,0:T(8,128)(2,1)}) %all-gather.2.cloned.1.call-update) | async-done | bytes 29360144 | tf_op jit(solution)/shard_map/all_gather | solution.py:329
  152.2 16.1 %conditional.8 = ((bf16[64,2048]{1,0:T(8,128)(2,1)}, bf16[4,64,2048]{2,1,0:T(8,128)(2,1)S(1)}, bf16[4,64,2048]{2,1,0:T(8,128)(2,1)S(1)}, bf16[4,64,1792]{2,1,0:T(8,128)(2,1)S(1)})) conditional(s32[]{:T(128)} %convert_element_type.55, bf16[64,2048]{1,0:T(8,128)(2,1)S(1)} %bitcast.54, (bf16[64,2048]{1,0:T(8,128)(2,1)S(1)}, f32[64,128]{1,0:T(8,128)}, ...), branch_computations={%region_1.2_spmd, %region_2.3_spmd} | conditional | flops 1879048192 | bytes 30408740 | solution.py:352
  152.9 15.4 %forward_stage.4 = (bf16[64,2048]{1,0:T(8,128)(2,1)}, bf16[4,64,2048]{2,1,0:T(8,128)(2,1)S(1)}, bf16[4,64,2048]{2,1,0:T(8,128)(2,1)S(1)}, bf16[4,64,1792]{2,1,0:T(8,128)(2,1)S(1)}) custom-call(bf16[64,2048]{1,0:T(8,128)(2,1)} %copy-done.3, f32[64,128]{1,0:T(8,128)} %get-tuple-element.127.cosine_ref, f32[64,128]{1,0:T(8,128)} %get-tuple-element.128.sine_ref, ...), custom_call_target="tpu_custom_call" | custom-call | flops 1879048192 | bytes 29360128 | tf_op jit(solution)/shard_map/cond/branch_1_fun/forward_stage/pallas_call | solution.py:227
  170.4 5.4 %collective-permute-done.3 = bf16[64,2048]{1,0:T(8,128)(2,1)} collective-permute-done((bf16[64,2048]{1,0:T(8,128)(2,1)}, bf16[64,2048]{1,0:T(8,128)(2,1)}, u32[]{:S(2)}, u32[]{:S(2)}) %collective-permute-start.3) | collective-permute-done | bytes 262176 | tf_op jit(solution)/shard_map/ppermute | solution.py:346
  180.0 3.2 collective-permute-done.10
  185.1 2.6 conditional.12
  191.4 2.7 collective-permute-start.7
  196.4 3.1 collective-permute-done.6
  199.6 4.7 %collective-permute-done.8 = bf16[64,2048]{1,0:T(8,128)(2,1)} collective-permute-done((bf16[64,2048]{1,0:T(8,128)(2,1)}, bf16[64,2048]{1,0:T(8,128)(2,1)}, u32[]{:S(2)}, u32[]{:S(2)}) %collective-permute-start.8) | collective-permute-done | bytes 262176 | tf_op jit(solution)/shard_map/ppermute | solution.py:313
  204.3 2.2 pad_maximum_fusion
  206.6 2.9 collective-permute-start.9
  211.2 118.4 %collective-permute-done.13 = bf16[64,2048]{1,0:T(8,128)(2,1)S(1)} collective-permute-done((bf16[64,2048]{1,0:T(8,128)(2,1)}, bf16[64,2048]{1,0:T(8,128)(2,1)S(1)}, u32[]{:S(2)}, u32[]{:S(2)}) %collective-permute-start.13) | collective-permute-done | bytes 262176 | tf_op jit(solution)/shard_map/ppermute | solution.py:358
  329.6 20.6 %conditional.15 = (bf16[4,64,1792]{2,1,0:T(8,128)(2,1)}) conditional(s32[]{:T(128)} %convert_element_type.55, bf16[4,64,1792]{2,1,0:T(8,128)(2,1)} %get-tuple-element.210, (bf16[64,2048]{1,0:T(8,128)(2,1)S(1)}, f32[64,128]{1,0:T(8,128)S(1)}, f32[64,128]{1,0:T(8,128)S(1)}, bf16[4,64,2048]{2,1,0:T(8,128)(2,1)S(1)}, ...), branch_computations={%region_15.16_spmd, %region_16.17_spmd} | conditional | flops 1879048192 | bytes 29360136 | solution.py:363
  329.6 20.6 %backward_stage.7 = (bf16[64,2048]{1,0:T(8,128)(2,1)}, bf16[4,64,1792]{2,1,0:T(8,128)(2,1)}) custom-call(bf16[64,2048]{1,0:T(8,128)(2,1)S(1)} %get-tuple-element.163.g_ref, f32[64,128]{1,0:T(8,128)S(1)} %get-tuple-element.164.cosine_ref, f32[64,128]{1,0:T(8,128)S(1)} %get-tuple-element.165.sine_ref, bf16[4,64,2048]{2,1,0:T(8,128)(2,1)S(1)} %get-tuple-element.166.inputs_ref, ...), custom_call_target="tpu_custom_call" | custom-call | flops 1879048192 | bytes 29360128 | tf_op jit(solution)/shard_map/cond/branch_1_fun/backward_stage/pallas_call | solution.py:257
  351.6 2.7 collective-permute-start.15
  357.7 2.0 collective-permute-done.15
  359.7 2.5 collective-permute-done.16
  362.4 4.7 %collective-permute-start.17 = (bf16[256,896]{1,0:T(8,128)(2,1)S(1)}, bf16[256,896]{1,0:T(8,128)(2,1)S(1)}, u32[]{:S(2)}, u32[]{:S(2)}) collective-permute-start(bf16[256,896]{1,0:T(8,128)(2,1)S(1)} %get-tuple-element.218), channel_id=1, source_target_pairs={{0,1},{1,0},{2,3},{3,2},{4,5},{5,4},{6,7},{7,6},{8,9},{9,8},{10,11... | collective-permute-start | bytes 1376264 | tf_op jit(solution)/shard_map/ppermute | solution.py:366
  369.3 4.2 convolution_convert_fusion
  373.5 45.4 %reduce-scatter.2.cloned.1.call-done = bf16[256,896]{1,0:T(8,128)(2,1)} async-done(((bf16[2048,896]{1,0:T(8,128)(2,1)}), bf16[256,896]{1,0:T(8,128)(2,1)}) %reduce-scatter.2.cloned.1.call-update) | async-done | bytes 458768 | tf_op jit(solution)/shard_map/reduce_scatter | solution.py:374
  423.2 5.6 %collective-permute-done.19 = bf16[64,1792]{1,0:T(8,128)(2,1)S(1)} collective-permute-done((bf16[64,1792]{1,0:T(8,128)(2,1)S(1)}, bf16[64,1792]{1,0:T(8,128)(2,1)S(1)}, u32[]{:S(2)}, u32[]{:S(2)}) %collective-permute-start.19) | collective-permute-done | bytes 229408 | tf_op jit(solution)/shard_map/ppermute | solution.py:289
  (79 shorter events, 37.7 us)
Async XLA Ops:
  6.5 145.7 %all-gather.2.cloned.1.call-start = ((), (), s32[]{:S(2)}) async-start(), calls=%async_computation.1 | async-start | bytes 29818880 | tf_op jit(solution)/shard_map/all_gather | solution.py:329
  7.7 6.1 %collective-permute-start.2 = (bf16[64,1792]{1,0:T(8,128)(2,1)S(1)}, bf16[64,1792]{1,0:T(8,128)(2,1)S(1)}, u32[]{:S(2)}, u32[]{:S(2)}) collective-permute-start(bf16[64,1792]{1,0:T(8,128)(2,1)S(1)} %get-tuple-element.228), channel_id=1, source_target_pairs={{0,2},{2,0},{1,3},{3,1},{4,6},{6,4},{5,7},{7,5},{8,10},{10,8},{9,1... | collective-permute-start | bytes 688136 | tf_op jit(solution)/shard_map/ppermute | solution.py:289
  14.7 404.2 %reduce-scatter.2.cloned.1.call-start = ((), (), s32[]{:S(2)}) async-start(), calls=%async_computation.2 | async-start | bytes 4128768 | tf_op jit(solution)/shard_map/reduce_scatter | solution.py:374
  14.7 3.2 collective-permute-start.1
  17.0 3.9 collective-permute-start
  168.4 7.4 %collective-permute-start.3 = (bf16[64,2048]{1,0:T(8,128)(2,1)}, bf16[64,2048]{1,0:T(8,128)(2,1)}, u32[]{:S(2)}, u32[]{:S(2)}) collective-permute-start(bf16[64,2048]{1,0:T(8,128)(2,1)} %get-tuple-element.191), channel_id=1, source_target_pairs={{0,128},{1,129},{4,132},{5,133},{8,136},{9,137},{12,140},{13,141},... | collective-permute-start | bytes 786440 | tf_op jit(solution)/shard_map/ppermute | solution.py:346
  175.7 2.9 collective-permute-start.4
  178.7 4.6 %collective-permute-start.10 = (bf16[32,2048]{1,0:T(8,128)(2,1)}, bf16[32,2048]{1,0:T(8,128)(2,1)}, u32[]{:S(2)}, u32[]{:S(2)}) collective-permute-start(bf16[32,2048]{1,0:T(8,128)(2,1)} %bitcast.15), channel_id=1, source_target_pairs={{0,2},{2,0},{1,3},{3,1},{4,6},{6,4},{5,7},{7,5},{8,10},{10,8},{9,1... | collective-permute-start | bytes 393224 | tf_op jit(solution)/shard_map/ppermute | solution.py:289
  178.7 6.4 %collective-permute-start.5 = (bf16[64,2048]{1,0:T(8,128)(2,1)}, bf16[64,2048]{1,0:T(8,128)(2,1)}, u32[]{:S(2)}, u32[]{:S(2)}) collective-permute-start(bf16[64,2048]{1,0:T(8,128)(2,1)} %get-tuple-element.202), channel_id=1, source_target_pairs={{2,130},{3,131},{6,134},{7,135},{10,138},{11,139},{14,142},{15,143... | collective-permute-start | bytes 786440 | tf_op jit(solution)/shard_map/ppermute | solution.py:346
  187.7 1.3 collective-permute-start.11
  189.1 5.8 %collective-permute-start.12 = (bf16[64,2048]{1,0:T(8,128)(2,1)}, bf16[64,2048]{1,0:T(8,128)(2,1)}, u32[]{:S(2)}, u32[]{:S(2)}) collective-permute-start(bf16[64,2048]{1,0:T(8,128)(2,1)} %get-tuple-element.208), channel_id=1, source_target_pairs={{2,128},{3,129},{6,132},{7,133},{10,136},{11,137},{14,140},{15,141... | collective-permute-start | bytes 786440 | tf_op jit(solution)/shard_map/ppermute | solution.py:358
  191.4 8.1 %collective-permute-start.6 = (bf16[64,2048]{1,0:T(8,128)(2,1)}, bf16[64,2048]{1,0:T(8,128)(2,1)}, u32[]{:S(2)}, u32[]{:S(2)}) collective-permute-start(bf16[64,2048]{1,0:T(8,128)(2,1)} %get-tuple-element.216), channel_id=1, source_target_pairs={{0,32},{32,64},{64,96},{96,0},{1,33},{33,65},{65,97},{97,1},{2,34}... | collective-permute-start | bytes 786440 | tf_op jit(solution)/shard_map/ppermute | solution.py:313
  191.4 8.2 %collective-permute-start.7 = (bf16[64,2048]{1,0:T(8,128)(2,1)}, bf16[64,2048]{1,0:T(8,128)(2,1)}, u32[]{:S(2)}, u32[]{:S(2)}) collective-permute-start(bf16[64,2048]{1,0:T(8,128)(2,1)} %get-tuple-element.215), channel_id=1, source_target_pairs={{0,96},{32,0},{64,32},{96,64},{1,97},{33,1},{65,33},{97,65},{2,98}... | collective-permute-start | bytes 786440 | tf_op jit(solution)/shard_map/ppermute | solution.py:313
  194.1 10.3 %collective-permute-start.8 = (bf16[64,2048]{1,0:T(8,128)(2,1)}, bf16[64,2048]{1,0:T(8,128)(2,1)}, u32[]{:S(2)}, u32[]{:S(2)}) collective-permute-start(bf16[64,2048]{1,0:T(8,128)(2,1)} %get-tuple-element.214), channel_id=1, source_target_pairs={{0,64},{32,96},{64,0},{96,32},{1,65},{33,97},{65,1},{97,33},{2,66}... | collective-permute-start | bytes 786440 | tf_op jit(solution)/shard_map/ppermute | solution.py:313
  194.9 134.7 %copy-start.1 = (f32[64,128]{1,0:T(8,128)S(1)}, f32[64,128]{1,0:T(8,128)}, u32[]{:S(2)}) copy-start(f32[64,128]{1,0:T(8,128)} %get-tuple-element.232) | copy-start | bytes 98308
  194.9 134.7 %copy-start.2 = (f32[64,128]{1,0:T(8,128)S(1)}, f32[64,128]{1,0:T(8,128)}, u32[]{:S(2)}) copy-start(f32[64,128]{1,0:T(8,128)} %get-tuple-element.233) | copy-start | bytes 98308
  194.9 134.6 %collective-permute-start.13 = (bf16[64,2048]{1,0:T(8,128)(2,1)}, bf16[64,2048]{1,0:T(8,128)(2,1)S(1)}, u32[]{:S(2)}, u32[]{:S(2)}) collective-permute-start(bf16[64,2048]{1,0:T(8,128)(2,1)} %get-tuple-element.211), channel_id=1, source_target_pairs={{128,0},{129,1},{132,4},{133,5},{136,8},{137,9},{140,12},{141,13},... | collective-permute-start | bytes 786440 | tf_op jit(solution)/shard_map/ppermute | solution.py:358
  206.6 161.5 %collective-permute-start.9 = (bf16[256,2048]{1,0:T(8,128)(2,1)}, bf16[256,2048]{1,0:T(8,128)(2,1)}, u32[]{:S(2)}, u32[]{:S(2)}) collective-permute-start(bf16[256,2048]{1,0:T(8,128)(2,1)} %pad_maximum_fusion), channel_id=1, source_target_pairs={{0,1},{1,0},{2,3},{3,2},{4,5},{5,4},{6,7},{7,6},{8,9},{9,8},{10,11... | collective-permute-start | bytes 3145736 | tf_op jit(solution)/shard_map/ppermute | solution.py:366
  351.6 6.2 %collective-permute-start.14 = (bf16[64,1792]{1,0:T(8,128)(2,1)S(1)}, bf16[64,1792]{1,0:T(8,128)(2,1)S(1)}, u32[]{:S(2)}, u32[]{:S(2)}) collective-permute-start(bf16[64,1792]{1,0:T(8,128)(2,1)S(1)} %get-tuple-element.222), channel_id=1, source_target_pairs={{0,32},{32,64},{64,96},{96,0},{1,33},{33,65},{65,97},{97,1},{2,34}... | collective-permute-start | bytes 688136 | tf_op jit(solution)/shard_map/ppermute | solution.py:313
  351.6 8.1 %collective-permute-start.15 = (bf16[64,1792]{1,0:T(8,128)(2,1)S(1)}, bf16[64,1792]{1,0:T(8,128)(2,1)S(1)}, u32[]{:S(2)}, u32[]{:S(2)}) collective-permute-start(bf16[64,1792]{1,0:T(8,128)(2,1)S(1)} %get-tuple-element.221), channel_id=1, source_target_pairs={{0,96},{32,0},{64,32},{96,64},{1,97},{33,1},{65,33},{97,65},{2,98}... | collective-permute-start | bytes 688136 | tf_op jit(solution)/shard_map/ppermute | solution.py:313
  354.3 7.9 %collective-permute-start.16 = (bf16[64,1792]{1,0:T(8,128)(2,1)S(1)}, bf16[64,1792]{1,0:T(8,128)(2,1)S(1)}, u32[]{:S(2)}, u32[]{:S(2)}) collective-permute-start(bf16[64,1792]{1,0:T(8,128)(2,1)S(1)} %get-tuple-element.220), channel_id=1, source_target_pairs={{0,64},{32,96},{64,0},{96,32},{1,65},{33,97},{65,1},{97,33},{2,66}... | collective-permute-start | bytes 688136 | tf_op jit(solution)/shard_map/ppermute | solution.py:313
  362.4 7.0 %collective-permute-start.17 = (bf16[256,896]{1,0:T(8,128)(2,1)S(1)}, bf16[256,896]{1,0:T(8,128)(2,1)S(1)}, u32[]{:S(2)}, u32[]{:S(2)}) collective-permute-start(bf16[256,896]{1,0:T(8,128)(2,1)S(1)} %get-tuple-element.218), channel_id=1, source_target_pairs={{0,1},{1,0},{2,3},{3,2},{4,5},{5,4},{6,7},{7,6},{8,9},{9,8},{10,11... | collective-permute-start | bytes 1376264 | tf_op jit(solution)/shard_map/ppermute | solution.py:366
  420.0 1.8 collective-permute-start.18
  421.9 6.9 %collective-permute-start.19 = (bf16[64,1792]{1,0:T(8,128)(2,1)S(1)}, bf16[64,1792]{1,0:T(8,128)(2,1)S(1)}, u32[]{:S(2)}, u32[]{:S(2)}) collective-permute-start(bf16[64,1792]{1,0:T(8,128)(2,1)S(1)} %get-tuple-element.224), channel_id=1, source_target_pairs={{0,2},{2,0},{1,3},{3,1},{4,6},{6,4},{5,7},{7,5},{8,10},{10,8},{9,1... | collective-permute-start | bytes 688136 | tf_op jit(solution)/shard_map/ppermute | solution.py:289
  (5 other events, 39.8 us)
Sparse Core Ops, SparseCore 0:
  14.8 137.3 all-gather.1
  373.6 45.1 reduce-scatter.1

commit v2 on v1

v2 whole, which is shorter than its diff:
```python
import jax
import jax.numpy as jnp
from jax import lax
from jax.experimental import pallas as pl
from jax.experimental.pallas import tpu as pltpu
from jax.sharding import Mesh, PartitionSpec as P

D = 2048
HEADS = 16
KV_HEADS = 4
GROUP = HEADS // KV_HEADS
QK_DIM = 64
V_DIM = 128
PATCH = 16
QUERY_WIDTH = HEADS * QK_DIM
KEY_WIDTH = KV_HEADS * QK_DIM
VALUE_START = QUERY_WIDTH + KEY_WIDTH
WIDTH = VALUE_START + KV_HEADS * V_DIM
ROPE_BASE = 500000.0
EPSILON = 1e-05
LAYERS = 4
LANES = 128
COLUMNS = 256
STAGE_X = (0, 2, 1, 3)
F32 = jnp.float32
BF16 = jnp.bfloat16


def dot(a, b, a_dim, b_dim):
    return lax.dot_general(
        a, b, (((a_dim,), (b_dim,)), ((), ())), preferred_element_type=F32
    )


def lane_index(rows):
    return lax.broadcasted_iota(jnp.int32, (rows, LANES), 1)


def swap_halves(chunk):
    lanes = lane_index(chunk.shape[0])
    ahead = pltpu.roll(chunk, LANES - QK_DIM // 2, 1)
    behind = pltpu.roll(chunk, QK_DIM // 2, 1)
    return jnp.where(lanes % QK_DIM < QK_DIM // 2, ahead, behind)


def score_mask(tokens):
    rows = lax.broadcasted_iota(jnp.int32, (GROUP * tokens, tokens), 0) % tokens
    columns = lax.broadcasted_iota(jnp.int32, (GROUP * tokens, tokens), 1)
    return (rows // PATCH == columns // PATCH) & (columns <= rows)


def rotated_chunk(qkv, index, cosine, sine):
    chunk = qkv[:, index * LANES : (index + 1) * LANES]
    return chunk * cosine + swap_halves(chunk) * sine


def group_parts(qkv, group, cosine, sine):
    low = lane_index(qkv.shape[0]) < QK_DIM
    rows = []
    for pair in range(2):
        chunk = rotated_chunk(qkv, 2 * group + pair, cosine, sine)
        rows.append(jnp.where(low, chunk, 0.0))
        rows.append(jnp.where(low, 0.0, chunk))
    queries = jnp.concatenate(rows, axis=0).astype(BF16)
    chunk = rotated_chunk(qkv, QUERY_WIDTH // LANES + group // 2, cosine, sine)
    other = pltpu.roll(chunk, QK_DIM, 1)
    keys_part = jnp.where(low, chunk, other) if group % 2 == 0 else jnp.where(low, other, chunk)
    values_part = qkv[:, VALUE_START + group * V_DIM : VALUE_START + (group + 1) * V_DIM]
    return queries, keys_part.astype(BF16), values_part.astype(BF16)


def group_probs(queries, keys_part, mask):
    scores = dot(queries, keys_part, 1, 1) * (1.0 / QK_DIM**0.5)
    raised = jnp.where(mask, jnp.exp(jnp.where(mask, scores, 0.0)), 0.0)
    return raised / jnp.sum(raised, axis=-1, keepdims=True)


def column_copies(slot, layer, step, weights_ref, held, sems):
    columns = pl.ds(step * COLUMNS, COLUMNS)
    return [
        pltpu.make_async_copy(
            weights_ref.at[layer, :, core, low, :, columns],
            held.at[slot, :, low, core, :, columns],
            sems.at[slot, step, core, low],
        )
        for core in range(2)
        for low in range(2)
    ]


def row_copies(slot, layer, step, weights_ref, held, sems):
    return [
        pltpu.make_async_copy(
            weights_ref.at[layer, step, core, low],
            held.at[slot, step, low, core],
            sems.at[slot, step, core, low],
        )
        for core in range(2)
        for low in range(2)
    ]


def start_all(copies):
    for copy in copies:
        copy.start()


def wait_all(copies):
    for copy in copies:
        copy.wait()


COLUMN_STEPS = WIDTH // COLUMNS
ROW_STEPS = D // COLUMNS
AHEAD = 5


def forward_layer(
    layer, final, cosine, sine, mask, weights_ref,
    inputs_ref, normed_ref, values_ref, queries_ref, keys_ref, probs_ref, target,
    held, qkv_ref, sems,
):
    x = inputs_ref[layer]
    tokens = x.shape[0]
    slot = layer % 2
    wide = x.astype(F32)
    scale = lax.rsqrt(jnp.mean(wide * wide, axis=-1, keepdims=True) + EPSILON)
    normed = (wide * scale).astype(BF16)
    normed_ref[layer] = normed
    for step in range(COLUMN_STEPS):
        wait_all(column_copies(slot, layer, step, weights_ref, held, sems))
        later = step + AHEAD
        if later < COLUMN_STEPS:
            start_all(column_copies(slot, layer, later, weights_ref, held, sems))
        elif not final:
            later -= COLUMN_STEPS
            start_all(column_copies(1 - slot, layer + 1, later, weights_ref, held, sems))
        columns = slice(step * COLUMNS, (step + 1) * COLUMNS)
        block = held[slot, :, :, :, :, columns].reshape(D, COLUMNS)
        qkv_ref[:, columns] = dot(normed, block, 1, 0).astype(BF16)
    qkv = qkv_ref[...].astype(F32)
    values_ref[layer] = qkv_ref[:, VALUE_START:]
    for group in range(KV_HEADS):
        queries, keys_part, values_part = group_parts(qkv, group, cosine, sine)
        probs = group_probs(queries, keys_part, mask)
        queries_ref[layer, group] = queries
        keys_ref[layer, group] = keys_part
        probs_ref[layer, group] = probs
        mixed = dot(probs.astype(BF16), values_part, 1, 0)
        for r in range(GROUP):
            head = group * GROUP + r
            span = slice(head * V_DIM, (head + 1) * V_DIM)
            value = inputs_ref[layer, :, span].astype(F32) + mixed[r * tokens : (r + 1) * tokens]
            target(span, value.astype(BF16))


def store_copies(layer, local_refs, outer_refs, sems, inward):
    copies = []
    for index, (inner, outer) in enumerate(zip(local_refs, outer_refs)):
        ends = (outer.at[layer], inner.at[layer]) if inward else (inner.at[layer], outer.at[layer])
        copies.append(pltpu.make_async_copy(*ends, sems.at[layer, index]))
    return copies


def forward_kernel(flag_ref, x_ref, cosine_ref, sine_ref, weights_ref, *rest):
    held, qkv_ref, *stores, sems, out_sems = rest[-10:]
    last_ref, *outs = rest[-17:-10]
    inputs_ref = stores[0]

    @pl.when(flag_ref[0] == 1)
    def active():
        for step in range(AHEAD):
            start_all(column_copies(0, 0, step, weights_ref, held, sems))
        inputs_ref[0] = x_ref[...]
        cosine = cosine_ref[...]
        sine = sine_ref[...]
        mask = score_mask(x_ref.shape[0])

        def run(layer, final, target):
            forward_layer(
                layer, final, cosine, sine, mask, weights_ref, *stores, target,
                held, qkv_ref, sems,
            )
            start_all(store_copies(layer, stores, outs, out_sems, False))

        def body(layer, carry):
            def target(span, value):
                inputs_ref[layer + 1, :, span] = value

            run(layer, False, target)
            return carry

        lax.fori_loop(0, LAYERS - 1, body, 0)

        def target(span, value):
            last_ref[:, span] = value

        run(LAYERS - 1, True, target)
        for layer in range(LAYERS):
            wait_all(store_copies(layer, stores, outs, out_sems, False))


def backward_layer(
    layer, final, cosine_ref, sine_ref, weights_ref, inputs_ref, values_ref, queries_ref,
    keys_ref, probs_ref, first_ref, grad_ref, held, sems,
):
    upstream = first_ref[...]
    tokens = upstream.shape[0]
    slot = layer % 2
    cosine = cosine_ref[...]
    sine = sine_ref[...]
    low = lane_index(tokens) < QK_DIM
    key_grads = []
    for group in range(KV_HEADS):
        queries = queries_ref[layer, group]
        keys_part = keys_ref[layer, group]
        probs = probs_ref[layer, group]
        values_part = values_ref[layer, :, group * V_DIM : (group + 1) * V_DIM]
        rows = [
            upstream[:, (group * GROUP + r) * V_DIM : (group * GROUP + r + 1) * V_DIM]
            for r in range(GROUP)
        ]
        stacked = jnp.concatenate(rows, axis=0)
        grad_probs = dot(stacked, values_part, 1, 1)
        weighted = jnp.sum(probs * grad_probs, axis=-1, keepdims=True)
        grad_scores = (probs * (grad_probs - weighted) * (1.0 / QK_DIM**0.5)).astype(BF16)
        grad_values = dot(probs.astype(BF16), stacked, 0, 0)
        grad_ref[layer, :, VALUE_START + group * V_DIM : VALUE_START + (group + 1) * V_DIM] = (
            grad_values.astype(BF16)
        )
        grad_queries = dot(grad_scores, keys_part, 1, 0)
        for pair in range(2):
            first = grad_queries[2 * pair * tokens : (2 * pair + 1) * tokens]
            second = grad_queries[(2 * pair + 1) * tokens : (2 * pair + 2) * tokens]
            chunk = jnp.where(low, first, second)
            chunk = chunk * cosine - swap_halves(chunk) * sine
            start_at = (2 * group + pair) * LANES
            grad_ref[layer, :, start_at : start_at + LANES] = chunk.astype(BF16)
        halves = dot(grad_scores, queries, 0, 0)
        key_grads.append(halves + pltpu.roll(halves, QK_DIM, 1))
    for pair in range(2):
        chunk = jnp.where(low, key_grads[2 * pair], key_grads[2 * pair + 1])
        chunk = chunk * cosine - swap_halves(chunk) * sine
        start_at = QUERY_WIDTH + pair * LANES
        grad_ref[layer, :, start_at : start_at + LANES] = chunk.astype(BF16)
    grad_qkv = grad_ref[layer]
    wide = inputs_ref[layer].astype(F32)
    parts = []
    for step in range(ROW_STEPS):
        wait_all(row_copies(slot, layer, step, weights_ref, held, sems))
        if not final:
            start_all(row_copies(1 - slot, layer - 1, step, weights_ref, held, sems))
        block = held[slot, step].reshape(COLUMNS, WIDTH)
        parts.append(dot(grad_qkv, block, 1, 1))
    grad_normed = jnp.concatenate(parts, axis=1)
    scale = lax.rsqrt(jnp.mean(wide * wide, axis=-1, keepdims=True) + EPSILON)
    inner = jnp.mean(grad_normed * wide, axis=-1, keepdims=True)
    grad_inputs = scale * grad_normed - wide * (scale * scale * scale * inner)
    first_ref[...] = (upstream.astype(F32) + grad_inputs).astype(BF16)


def backward_kernel(flag_ref, g_ref, cosine_ref, sine_ref, weights_ref, *rest):
    outer = rest[:5]
    first_ref, grad_out, held, *stores, grad_ref, sems, in_sems, out_sems = rest[-12:]

    @pl.when(flag_ref[0] == 1)
    def active():
        top = LAYERS - 1
        start_all(store_copies(top, stores, outer, in_sems, True))
        for step in range(ROW_STEPS):
            start_all(row_copies(top % 2, top, step, weights_ref, held, sems))
        for layer in reversed(range(top)):
            start_all(store_copies(layer, stores, outer, in_sems, True))
        first_ref[...] = g_ref[...]

        def run(layer, final):
            wait_all(store_copies(layer, stores, outer, in_sems, True))
            backward_layer(
                layer, final, cosine_ref, sine_ref, weights_ref, *stores, first_ref, grad_ref,
                held, sems,
            )
            start_all(store_copies(layer, [grad_ref], [grad_out], out_sems, False))

        def body(step, carry):
            run(top - step, False)
            return carry

        lax.fori_loop(0, top, body, 0)
        run(0, True)
        for layer in range(LAYERS):
            wait_all(store_copies(layer, [grad_ref], [grad_out], out_sems, False))


VMEM_SPEC = pl.BlockSpec(memory_space=pltpu.VMEM)
SMEM_SPEC = pl.BlockSpec(memory_space=pltpu.SMEM)
HBM_SPEC = pl.BlockSpec(memory_space=pltpu.HBM)
STAGE_PARAMS = pltpu.CompilerParams(vmem_limit_bytes=34 * 1024 * 1024)


def stage_cost(tokens):
    return pl.CostEstimate(
        flops=2 * LAYERS * tokens * D * WIDTH,
        bytes_accessed=2 * LAYERS * D * WIDTH,
        transcendentals=0,
    )


def buffers(shapes):
    return [pltpu.VMEM(each.shape, each.dtype) for each in shapes]


HELD = pltpu.VMEM((2, 8, 2, 2, 64, WIDTH), BF16)
WEIGHT_SEMS = pltpu.SemaphoreType.DMA((2, ROW_STEPS, 2, 2))


def copy_sems(count):
    return pltpu.SemaphoreType.DMA((LAYERS, count))


def store_shapes(tokens):
    return [
        jax.ShapeDtypeStruct((LAYERS, tokens, D), BF16),
        jax.ShapeDtypeStruct((LAYERS, tokens, D), BF16),
        jax.ShapeDtypeStruct((LAYERS, tokens, KV_HEADS * V_DIM), BF16),
        jax.ShapeDtypeStruct((LAYERS, KV_HEADS, GROUP * tokens, LANES), BF16),
        jax.ShapeDtypeStruct((LAYERS, KV_HEADS, tokens, LANES), BF16),
        jax.ShapeDtypeStruct((LAYERS, KV_HEADS, GROUP * tokens, tokens), F32),
    ]


def in_hbm(value):
    return pltpu.with_memory_space_constraint(value, pltpu.HBM)


def in_hbm_shape(shape):
    return pltpu.HBM(shape.shape, shape.dtype)


def grad_shape(tokens):
    return jax.ShapeDtypeStruct((LAYERS, tokens, WIDTH), BF16)


def run_forward(flag, x, cosine, sine, weights, stored):
    tokens = x.shape[0]
    shapes = store_shapes(tokens)
    return pl.pallas_call(
        forward_kernel,
        in_specs=[SMEM_SPEC] + [VMEM_SPEC] * 3 + [HBM_SPEC] * (1 + len(stored)),
        out_specs=[VMEM_SPEC] + [HBM_SPEC] * len(shapes),
        out_shape=[jax.ShapeDtypeStruct((tokens, D), BF16), *map(in_hbm_shape, shapes)],
        input_output_aliases={5 + i: 1 + i for i in range(len(stored))},
        scratch_shapes=[
            HELD,
            pltpu.VMEM((tokens, WIDTH), BF16),
            *buffers(shapes),
            WEIGHT_SEMS,
            copy_sems(len(shapes)),
        ],
        cost_estimate=stage_cost(tokens),
        name="forward_stage",
        compiler_params=STAGE_PARAMS,
    )(flag, x, cosine, sine, *map(in_hbm, [weights, *stored]))


def run_backward(flag, g, cosine, sine, weights, stored, grads):
    tokens = g.shape[0]
    shapes = store_shapes(tokens)
    return pl.pallas_call(
        backward_kernel,
        in_specs=[SMEM_SPEC] + [VMEM_SPEC] * 3 + [HBM_SPEC] * (6 + len(grads)),
        out_specs=[VMEM_SPEC, HBM_SPEC],
        out_shape=[jax.ShapeDtypeStruct((tokens, D), BF16), in_hbm_shape(grad_shape(tokens))],
        input_output_aliases={10: 1} if grads else {},
        scratch_shapes=[
            HELD,
            *buffers([shapes[0], *shapes[2:], grad_shape(tokens)]),
            WEIGHT_SEMS,
            copy_sems(5),
            copy_sems(1),
        ],
        cost_estimate=stage_cost(tokens),
        name="backward_stage",
        compiler_params=STAGE_PARAMS,
    )(flag, g, cosine, sine, *map(in_hbm, [weights, *stored, *grads]))


def ring(size, by):
    return [(i, (i + by) % size) for i in range(size)]


def from_partner(value):
    return lax.ppermute(value, "xl", ring(2, 1))


def both_halves(value, low_x):
    other = from_partner(value)
    return jnp.where(low_x == 0, jnp.stack([value, other]), jnp.stack([other, value]))


def rotary_tables(lengths):
    half = QK_DIM // 2
    starts = jnp.cumsum(lengths, axis=-1) - lengths
    freqs = ROPE_BASE ** (-jnp.arange(half, dtype=F32) * 2.0 / (2 * half))
    angles = starts.astype(F32).reshape(-1, 1) * freqs
    cosine, sine = jnp.cos(angles), jnp.sin(angles)
    return (
        jnp.concatenate([cosine] * 4, axis=1),
        jnp.concatenate([-sine, sine, -sine, sine], axis=1),
    )


def spread_over_y(value, place):
    pieces = [lax.dynamic_index_in_dim(value, place, 0, keepdims=False)]
    for by in (1, 3, 2):
        piece = lax.dynamic_index_in_dim(value, (place + by) % 4, 0, keepdims=False)
        pieces.append(lax.ppermute(piece, "y", ring(4, by)))
    return pieces


def local(patches, lengths, cotangent, weights):
    high_x = lax.axis_index("xh")
    low_x = lax.axis_index("xl")
    place = lax.axis_index("y")
    core = lax.axis_index("core")
    stage = high_x + 2 * low_x
    rows = weights.shape[2]

    own = lax.dynamic_index_in_dim(weights, low_x, 0, keepdims=False)[0]
    partner_own = lax.dynamic_index_in_dim(weights, 1 - low_x, 0, keepdims=False)[0]
    other = from_partner(partner_own)
    shard = jnp.where(low_x == 0, jnp.stack([own, other]), jnp.stack([other, own]))
    gathered = lax.all_gather(shard, ("y", "z", "core"), axis=0, tiled=False)
    gathered = gathered.reshape(LAYERS, 8, 2, 2, rows, WIDTH)

    pick = lambda v: lax.dynamic_slice_in_dim(v, 2 * place, 2, 0)
    tokens = 4 * PATCH
    x = both_halves(pick(patches).reshape(2 * PATCH, D), low_x).reshape(tokens, D)
    g = both_halves(pick(cotangent).reshape(2 * PATCH, D), low_x).reshape(tokens, D)
    span = both_halves(pick(lengths).astype(F32), low_x).reshape(4, PATCH).astype(jnp.int32)
    cosine, sine = rotary_tables(span)

    stored = []
    for turn in range(LAYERS):
        flag = (stage == turn).astype(jnp.int32).reshape(1)
        if turn > 0:
            x = lax.ppermute(x, ("xh", "xl"), [(STAGE_X[turn - 1], STAGE_X[turn])])
        x, *stored = run_forward(flag, x, cosine, sine, gathered, stored)
    inputs, normed, *shared = stored

    grads = []
    for turn in reversed(range(LAYERS)):
        flag = (stage == turn).astype(jnp.int32).reshape(1)
        if turn < LAYERS - 1:
            g = lax.ppermute(g, ("xh", "xl"), [(STAGE_X[turn + 1], STAGE_X[turn])])
        g, *grads = run_backward(flag, g, cosine, sine, gathered, [inputs, *shared], grads)
    grads = grads[0]

    normed_rows = jnp.concatenate(spread_over_y(normed, place))
    sibling = lambda v: lax.ppermute(v, "core", ring(2, 1))
    normed_rows = jnp.concatenate([normed_rows, sibling(normed_rows)])
    half = WIDTH // 2
    grad_rows = jnp.concatenate(spread_over_y(grads, place))
    mine = lax.dynamic_slice_in_dim(grad_rows, core * half, half, 1)
    sent = lax.dynamic_slice_in_dim(grad_rows, (1 - core) * half, half, 1)
    grad_rows = jnp.concatenate([mine, sibling(sent)])
    terms = dot(normed_rows, grad_rows, 0, 0).astype(BF16)
    total = lax.psum_scatter(terms, "z", scatter_dimension=0, tiled=True)
    total = total.reshape(2, 2, rows, half)

    def block(low, row_core):
        return lax.dynamic_slice(total, (low, row_core, 0, 0), (1, 1, rows, half))[0, 0]

    came = [[block(low_x, core), None], [None, None]]
    for far in range(2):
        for beside in range(2):
            if far or beside:
                pairs = [(i, i ^ (2 * far + beside)) for i in range(4)]
                came[far][beside] = lax.ppermute(
                    block(low_x ^ far, core ^ beside), ("xl", "core"), pairs
                )

    def source(low, col):
        same_core = [jnp.where(core == col, came[far][0], came[far][1]) for far in range(2)]
        return jnp.where(low_x == low, same_core[0], same_core[1])

    result = jnp.stack(
        [jnp.concatenate([source(low, col) for col in range(2)], axis=1) for low in range(2)]
    )
    return result.astype(F32)[:, None]


def solution(mesh):
    fine = Mesh(mesh.devices.reshape(2, 4, 8, 2, 2), ("xh", "y", "z", "xl", "core"))
    dp = ("z", "xl", "core")
    return jax.shard_map(
        local,
        mesh=fine,
        in_specs=(
            P(dp, None, None),
            P(dp, None),
            P(dp, None, None),
            P(None, ("xh", "y"), dp, None),
        ),
        out_specs=P(None, ("xh", "y"), dp, None),
        check_vma=False,
    )
```

time: 437 us -> 491 us (1.12); the launches traced: 437 us -> 482 us
  waiting for transfers between devices: 331 us -> 367 us
  Pallas kernels: 36 us -> 58 us
  local copies, waits for them, and re-layouts: 16.2 us -> 5.01 us
    ppermute x3, waiting for transfers between devices: 118 us -> 155 us  [local(): g = lax.ppermute(g, ('xh', 'xl'), [(STAGE_X[turn + 1], STAGE_X[turn])])]
    pallas_call x2 -> x8, Pallas kernels: 36 us -> 58 us  [the longest x4 36 us: run_backward(): pl.pallas_call(backward_kernel, in_specs=[SMEM_SPEC] + [VMEM_SPEC] * 3 +...]
    ppermute x0 -> x3, waiting for transfers between devices: none -> 5.62 us  [local(): lax.ppermute(block(low_x ^ far, core ^ beside), ('xl', 'core'), pairs)]
    ppermute x5 -> x4, waiting for transfers between devices: 15.2 us -> 9.79 us  [from_partner(): return lax.ppermute(value, 'xl', ring(2, 1))]
    unnamed x16 -> x10, local copies, waits for them, and re-layouts: 5.17 us -> 0.11 us
  transfers between devices with their start and end apart: 22 -> 23, of which waited for: 16 -> 16; matrix products, arithmetic and copies ran while one was open for 4% -> 1% of each run, Pallas kernels for 5% -> 7%
where the time goes in v2:
time: 491 us; the launch traced here: 482 us
  waiting for transfers between devices  367 us (75%)
  Pallas kernels  58 us (12%)
  starting transfers between devices  29.8 us (6%)
  between operations  14.3 us (3%)
  local copies, waits for them, and re-layouts  5.01 us (1%)
    ppermute x3, waiting for transfers between devices, local(): g = lax.ppermute(g, ('xh', 'xl'), [(STAGE_X[turn + 1], STAGE_X[turn])])  155 us
    all_gather x1, waiting for transfers between devices, local(): gathered = lax.all_gather(shard, ('y', 'z', 'core'), axis=0, tiled=False)  131 us
    reduce_scatter x1, waiting for transfers between devices, local(): total = lax.psum_scatter(terms, 'z', scatter_dimension=0, tiled=True)  45.6 us
    pallas_call x4, Pallas kernels, run_backward(): pl.pallas_call(backward_kernel, in_specs=[SMEM_SPEC] + [VMEM_SPEC] * 3 +...  36 us
    pallas_call x4, Pallas kernels, run_forward(): pl.pallas_call(forward_kernel, in_specs=[SMEM_SPEC] + [VMEM_SPEC] * 3 + [...  22 us
    ppermute x6, waiting for transfers between devices, spread_over_y(): pieces.append(lax.ppermute(piece, 'y', ring(4, by)))  12.9 us
    ppermute x6, starting transfers between devices, spread_over_y(): pieces.append(lax.ppermute(piece, 'y', ring(4, by)))  10.2 us
  transfers between devices with their start and end apart: 23, of which 16 were waited for; matrix products, arithmetic and copies ran while one was open for 1% of the time, Pallas kernels for 7%

profile of v2, /device:TPU:1, one launch (start us, length us, event | category | flops | bytes accessed | tf_op | source)
XLA Modules:
  0.0 482.0 jit_solution(17315203919474497688)
XLA Ops:
  7.7 2.1 collective-permute-start.2
  9.8 4.0 collective-permute-done.2
  14.7 2.3 collective-permute-start.1
  18.7 2.3 collective-permute-done
  21.0 131.2 %all-gather.2.cloned.1.call-done = bf16[64,2,64,1792]{3,2,1,0:T(8,128)(2,1)} async-done(((bf16[1,2,64,1792]{3,2,1,0:T(8,128)(2,1)}), bf16[64,2,64,1792]{3,2,1,0:T(8,128)(2,1)}) %all-gather.2.cloned.1.call-update) | async-done | bytes 29360144 | tf_op jit(solution)/shard_map/all_gather | solution.py:432
  152.2 18.9 %forward_stage.4 = (bf16[64,2048]{1,0:T(8,128)(2,1)S(1)}, bf16[4,64,2048]{2,1,0:T(8,128)(2,1)}, bf16[4,64,2048]{2,1,0:T(8,128)(2,1)}, bf16[4,64,512]{2,1,0:T(8,1...) custom-call(s32[1]{0:T(128)} %bitcast.3.flag_ref, ...), custom_call_target="tpu_custom_call" | custom-call | flops 1879048192 | bytes 29360128 | tf_op jit(solution)/shard_map/forward_stage/pallas_call | solution.py:346
  172.4 5.7 %collective-permute-done.3.x_ref = bf16[64,2048]{1,0:T(8,128)(2,1)S(1)} collective-permute-done((bf16[64,2048]{1,0:T(8,128)(2,1)S(1)}, bf16[64,2048]{1,0:T(8,128)(2,1)S(1)}, u32[]{:S(2)}, u32[]{:S(2)}) %collective-permute-start.3) | collective-permute-done | bytes 262176 | tf_op jit(solution)/shard_map/ppermute | solution.py:446
  182.7 2.8 collective-permute-done.10
  187.0 3.5 backward_stage.4
  192.9 6.0 %collective-permute-start.7 = (bf16[64,2048]{1,0:T(8,128)(2,1)S(1)}, bf16[64,2048]{1,0:T(8,128)(2,1)S(1)}, u32[]{:S(2)}, u32[]{:S(2)}) collective-permute-start(bf16[64,2048]{1,0:T(8,128)(2,1)S(1)} %get-tuple-element.76), channel_id=1, source_target_pairs={{0,96},{32,0},{64,32},{96,64},{1,97},{33,1},{65,33},{97,65},{2,98}... | collective-permute-start | bytes 786440 | tf_op jit(solution)/shard_map/ppermute | solution.py:416
  202.2 3.2 collective-permute-done.7
  205.4 1.7 collective-permute-done.8
  207.3 2.0 collective-permute-start.9
  209.3 155.1 %collective-permute-done.13.g_ref = bf16[64,2048]{1,0:T(8,128)(2,1)S(1)} collective-permute-done((bf16[64,2048]{1,0:T(8,128)(2,1)S(1)}, bf16[64,2048]{1,0:T(8,128)(2,1)S(1)}, u32[]{:S(2)}, u32[]{:S(2)}) %collective-permute-start.13) | collective-permute-done | bytes 262176 | tf_op jit(solution)/shard_map/ppermute | solution.py:454
  364.4 30.9 %backward_stage.7 = (bf16[64,2048]{1,0:T(8,128)(2,1)}, bf16[4,64,1792]{2,1,0:T(8,128)(2,1)}) custom-call(s32[1]{0:T(128)} %bitcast.3.flag_ref, bf16[64,2048]{1,0:T(8,128)(2,1)S(1)} %collective-permute-done.13.g_ref, f32[64,128]{1,0:T(8,128)S(1)} %get-tuple-element.96.cosine_ref, ...), custom_call_target="tpu_custom_call", output_to_operand_aliasing={{1}: (10, {})} | custom-call | flops 1879048192 | bytes 29360128 | tf_op jit(solution)/shard_map/backward_stage/pallas_call | solution.py:368
  397.0 2.7 collective-permute-start.15
  399.7 3.4 collective-permute-done.14
  403.1 2.0 collective-permute-done.15
  405.1 2.5 collective-permute-done.16
  407.7 4.7 collective-permute-start.17
  413.8 4.2 convolution_convert_fusion
  418.1 45.6 %reduce-scatter.2.cloned.1.call-done = bf16[256,896]{1,0:T(8,128)(2,1)} async-done(((bf16[2048,896]{1,0:T(8,128)(2,1)}), bf16[256,896]{1,0:T(8,128)(2,1)}) %reduce-scatter.2.cloned.1.call-update) | async-done | bytes 458768 | tf_op jit(solution)/shard_map/reduce_scatter | solution.py:467
  467.1 3.0 collective-permute-done.19
  470.1 2.6 collective-permute-done.20
  (70 shorter events, 25.5 us)
Async XLA Ops:
  6.5 10.5 %copy-start = (bf16[8,16,2048]{2,1,0:T(8,128)(2,1)S(1)}, bf16[8,16,2048]{2,1,0:T(8,128)(2,1)}, u32[]{:S(2)}) copy-start(bf16[8,16,2048]{2,1,0:T(8,128)(2,1)} %param.4) | copy-start | bytes 1572868
  6.5 145.7 %all-gather.2.cloned.1.call-start = ((), (), s32[]{:S(2)}) async-start(), calls=%async_computation.1 | async-start | bytes 29818880 | tf_op jit(solution)/shard_map/all_gather | solution.py:432
  7.7 6.1 %collective-permute-start.2 = (bf16[64,1792]{1,0:T(8,128)(2,1)S(1)}, bf16[64,1792]{1,0:T(8,128)(2,1)S(1)}, u32[]{:S(2)}, u32[]{:S(2)}) collective-permute-start(bf16[64,1792]{1,0:T(8,128)(2,1)S(1)} %get-tuple-element.92), channel_id=1, source_target_pairs={{0,2},{2,0},{1,3},{3,1},{4,6},{6,4},{5,7},{7,5},{8,10},{10,8},{9,1... | collective-permute-start | bytes 688136 | tf_op jit(solution)/shard_map/ppermute | solution.py:392
  14.7 449.0 %reduce-scatter.2.cloned.1.call-start = ((), (), s32[]{:S(2)}) async-start(), calls=%async_computation.2 | async-start | bytes 4128768 | tf_op jit(solution)/shard_map/reduce_scatter | solution.py:467
  14.7 3.2 collective-permute-start.1
  17.0 3.9 collective-permute-start
  171.1 7.1 %collective-permute-start.3 = (bf16[64,2048]{1,0:T(8,128)(2,1)S(1)}, bf16[64,2048]{1,0:T(8,128)(2,1)S(1)}, u32[]{:S(2)}, u32[]{:S(2)}) collective-permute-start(bf16[64,2048]{1,0:T(8,128)(2,1)S(1)} %get-tuple-element.39), channel_id=1, source_target_pairs={{0,128},{1,129},{4,132},{5,133},{8,136},{9,137},{12,140},{13,141},... | collective-permute-start | bytes 786440 | tf_op jit(solution)/shard_map/ppermute | solution.py:446
  179.0 2.2 collective-permute-start.4
  180.6 4.8 %collective-permute-start.10 = (bf16[32,2048]{1,0:T(8,128)(2,1)S(1)}, bf16[32,2048]{1,0:T(8,128)(2,1)S(1)}, u32[]{:S(2)}, u32[]{:S(2)}) collective-permute-start(bf16[32,2048]{1,0:T(8,128)(2,1)S(1)} %bitcast.72), channel_id=1, source_target_pairs={{0,2},{2,0},{1,3},{3,1},{4,6},{6,4},{5,7},{7,5},{8,10},{10,8},{9,1... | collective-permute-start | bytes 393224 | tf_op jit(solution)/shard_map/ppermute | solution.py:392
  182.0 3.5 collective-permute-start.5
  190.5 0.7 collective-permute-start.11
  192.1 8.0 %collective-permute-start.12 = (bf16[64,2048]{1,0:T(8,128)(2,1)S(1)}, bf16[64,2048]{1,0:T(8,128)(2,1)S(1)}, u32[]{:S(2)}, u32[]{:S(2)}) collective-permute-start(bf16[64,2048]{1,0:T(8,128)(2,1)S(1)} %get-tuple-element.68), channel_id=1, source_target_pairs={{2,128},{3,129},{6,132},{7,133},{10,136},{11,137},{14,140},{15,141... | collective-permute-start | bytes 786440 | tf_op jit(solution)/shard_map/ppermute | solution.py:454
  192.8 9.4 %collective-permute-start.6 = (bf16[64,2048]{1,0:T(8,128)(2,1)S(1)}, bf16[64,2048]{1,0:T(8,128)(2,1)S(1)}, u32[]{:S(2)}, u32[]{:S(2)}) collective-permute-start(bf16[64,2048]{1,0:T(8,128)(2,1)S(1)} %get-tuple-element.77), channel_id=1, source_target_pairs={{0,32},{32,64},{64,96},{96,0},{1,33},{33,65},{65,97},{97,1},{2,34}... | collective-permute-start | bytes 786440 | tf_op jit(solution)/shard_map/ppermute | solution.py:416
  192.9 12.5 %collective-permute-start.7 = (bf16[64,2048]{1,0:T(8,128)(2,1)S(1)}, bf16[64,2048]{1,0:T(8,128)(2,1)S(1)}, u32[]{:S(2)}, u32[]{:S(2)}) collective-permute-start(bf16[64,2048]{1,0:T(8,128)(2,1)S(1)} %get-tuple-element.76), channel_id=1, source_target_pairs={{0,96},{32,0},{64,32},{96,64},{1,97},{33,1},{65,33},{97,65},{2,98}... | collective-permute-start | bytes 786440 | tf_op jit(solution)/shard_map/ppermute | solution.py:416
  198.9 8.3 %collective-permute-start.8 = (bf16[64,2048]{1,0:T(8,128)(2,1)S(1)}, bf16[64,2048]{1,0:T(8,128)(2,1)S(1)}, u32[]{:S(2)}, u32[]{:S(2)}) collective-permute-start(bf16[64,2048]{1,0:T(8,128)(2,1)S(1)} %get-tuple-element.75), channel_id=1, source_target_pairs={{0,64},{32,96},{64,0},{96,32},{1,65},{33,97},{65,1},{97,33},{2,66}... | collective-permute-start | bytes 786440 | tf_op jit(solution)/shard_map/ppermute | solution.py:416
  200.9 163.5 %collective-permute-start.13 = (bf16[64,2048]{1,0:T(8,128)(2,1)S(1)}, bf16[64,2048]{1,0:T(8,128)(2,1)S(1)}, u32[]{:S(2)}, u32[]{:S(2)}) collective-permute-start(bf16[64,2048]{1,0:T(8,128)(2,1)S(1)} %get-tuple-element.70), channel_id=1, source_target_pairs={{128,0},{129,1},{132,4},{133,5},{136,8},{137,9},{140,12},{141,13},... | collective-permute-start | bytes 786440 | tf_op jit(solution)/shard_map/ppermute | solution.py:454
  207.3 205.1 %collective-permute-start.9 = (bf16[256,2048]{1,0:T(8,128)(2,1)S(1)}, bf16[256,2048]{1,0:T(8,128)(2,1)S(1)}, u32[]{:S(2)}, u32[]{:S(2)}) collective-permute-start(bf16[256,2048]{1,0:T(8,128)(2,1)S(1)} %pad_maximum_fusion), channel_id=1, source_target_pairs={{0,1},{1,0},{2,3},{3,2},{4,5},{5,4},{6,7},{7,6},{8,9},{9,8},{10,11... | collective-permute-start | bytes 3145736 | tf_op jit(solution)/shard_map/ppermute | solution.py:459
  396.6 6.4 %collective-permute-start.14 = (bf16[64,1792]{1,0:T(8,128)(2,1)S(1)}, bf16[64,1792]{1,0:T(8,128)(2,1)S(1)}, u32[]{:S(2)}, u32[]{:S(2)}) collective-permute-start(bf16[64,1792]{1,0:T(8,128)(2,1)S(1)} %get-tuple-element.83), channel_id=1, source_target_pairs={{0,32},{32,64},{64,96},{96,0},{1,33},{33,65},{65,97},{97,1},{2,34}... | collective-permute-start | bytes 688136 | tf_op jit(solution)/shard_map/ppermute | solution.py:416
  397.0 8.1 %collective-permute-start.15 = (bf16[64,1792]{1,0:T(8,128)(2,1)S(1)}, bf16[64,1792]{1,0:T(8,128)(2,1)S(1)}, u32[]{:S(2)}, u32[]{:S(2)}) collective-permute-start(bf16[64,1792]{1,0:T(8,128)(2,1)S(1)} %get-tuple-element.82), channel_id=1, source_target_pairs={{0,96},{32,0},{64,32},{96,64},{1,97},{33,1},{65,33},{97,65},{2,98}... | collective-permute-start | bytes 688136 | tf_op jit(solution)/shard_map/ppermute | solution.py:416
  399.7 7.9 %collective-permute-start.16 = (bf16[64,1792]{1,0:T(8,128)(2,1)S(1)}, bf16[64,1792]{1,0:T(8,128)(2,1)S(1)}, u32[]{:S(2)}, u32[]{:S(2)}) collective-permute-start(bf16[64,1792]{1,0:T(8,128)(2,1)S(1)} %get-tuple-element.81), channel_id=1, source_target_pairs={{0,64},{32,96},{64,0},{96,32},{1,65},{33,97},{65,1},{97,33},{2,66}... | collective-permute-start | bytes 688136 | tf_op jit(solution)/shard_map/ppermute | solution.py:416
  407.7 6.1 %collective-permute-start.17 = (bf16[256,896]{1,0:T(8,128)(2,1)S(1)}, bf16[256,896]{1,0:T(8,128)(2,1)S(1)}, u32[]{:S(2)}, u32[]{:S(2)}) collective-permute-start(bf16[256,896]{1,0:T(8,128)(2,1)S(1)} %get-tuple-element.79), channel_id=1, source_target_pairs={{0,1},{1,0},{2,3},{3,2},{4,5},{5,4},{6,7},{7,6},{8,9},{9,8},{10,11... | collective-permute-start | bytes 1376264 | tf_op jit(solution)/shard_map/ppermute | solution.py:459
  464.7 2.4 collective-permute-start.18
  465.4 4.7 collective-permute-start.19
  466.6 6.1 %collective-permute-start.20 = (bf16[64,896]{1,0:T(8,128)(2,1)S(1)}, bf16[64,896]{1,0:T(8,128)(2,1)S(1)}, u32[]{:S(2)}, u32[]{:S(2)}) collective-permute-start(bf16[64,896]{1,0:T(8,128)(2,1)S(1)} %get-tuple-element.89), channel_id=1, source_target_pairs={{0,3},{1,2},{2,1},{3,0},{4,7},{5,6},{6,5},{7,4},{8,11},{9,10},{10,... | collective-permute-start | bytes 344072 | tf_op jit(solution)/shard_map/ppermute | solution.py:478
  (2 other events, 9.7 us)
Sparse Core Ops, SparseCore 0:
  14.8 137.3 all-gather.1
  418.2 45.4 reduce-scatter.1

commit v3 on v2

--- a/solution.py
+++ b/solution.py
@@ -75,31 +75,16 @@
     return raised / jnp.sum(raised, axis=-1, keepdims=True)
 
 
-def column_copies(slot, layer, step, weights_ref, held, sems):
-    columns = pl.ds(step * COLUMNS, COLUMNS)
+def layer_copies(slot, layer, weights_ref, held, sems):
     return [
         pltpu.make_async_copy(
-            weights_ref.at[layer, :, core, low, :, columns],
-            held.at[slot, :, low, core, :, columns],
-            sems.at[slot, step, core, low],
+            weights_ref.at[layer, :, core, low], held.at[slot, :, low, core], sems.at[slot, core, low]
         )
         for core in range(2)
         for low in range(2)
     ]
 
 
-def row_copies(slot, layer, step, weights_ref, held, sems):
-    return [
-        pltpu.make_async_copy(
-            weights_ref.at[layer, step, core, low],
-            held.at[slot, step, low, core],
-            sems.at[slot, step, core, low],
-        )
-        for core in range(2)
-        for low in range(2)
-    ]
-
-
 def start_all(copies):
     for copy in copies:
         copy.start()
@@ -112,31 +97,23 @@
 
 COLUMN_STEPS = WIDTH // COLUMNS
 ROW_STEPS = D // COLUMNS
-AHEAD = 5
+SLOTS = LAYERS - 1
 
 
 def forward_layer(
-    layer, final, cosine, sine, mask, weights_ref,
-    inputs_ref, normed_ref, values_ref, queries_ref, keys_ref, probs_ref, target,
-    held, qkv_ref, sems,
+    layer, ready, block_of, cosine, sine, mask,
+    inputs_ref, normed_ref, values_ref, queries_ref, keys_ref, probs_ref, target, qkv_ref,
 ):
     x = inputs_ref[layer]
     tokens = x.shape[0]
-    slot = layer % 2
     wide = x.astype(F32)
     scale = lax.rsqrt(jnp.mean(wide * wide, axis=-1, keepdims=True) + EPSILON)
     normed = (wide * scale).astype(BF16)
     normed_ref[layer] = normed
+    ready()
     for step in range(COLUMN_STEPS):
-        wait_all(column_copies(slot, layer, step, weights_ref, held, sems))
-        later = step + AHEAD
-        if later < COLUMN_STEPS:
-            start_all(column_copies(slot, layer, later, weights_ref, held, sems))
-        elif not final:
-            later -= COLUMN_STEPS
-            start_all(column_copies(1 - slot, layer + 1, later, weights_ref, held, sems))
         columns = slice(step * COLUMNS, (step + 1) * COLUMNS)
-        block = held[slot, :, :, :, :, columns].reshape(D, COLUMNS)
+        block = block_of(columns).reshape(D, COLUMNS)
         qkv_ref[:, columns] = dot(normed, block, 1, 0).astype(BF16)
     qkv = qkv_ref[...].astype(F32)
     values_ref[layer] = qkv_ref[:, VALUE_START:]
@@ -169,44 +146,53 @@
 
     @pl.when(flag_ref[0] == 1)
     def active():
-        for step in range(AHEAD):
-            start_all(column_copies(0, 0, step, weights_ref, held, sems))
+        for layer in range(LAYERS):
+            start_all(layer_copies(layer, layer, weights_ref, held, sems))
         inputs_ref[0] = x_ref[...]
         cosine = cosine_ref[...]
         sine = sine_ref[...]
         mask = score_mask(x_ref.shape[0])
 
-        def run(layer, final, target):
+        def run(layer, ready, block_of, target):
             forward_layer(
-                layer, final, cosine, sine, mask, weights_ref, *stores, target,
-                held, qkv_ref, sems,
+                layer, ready, block_of, cosine, sine, mask, *stores, target, qkv_ref
             )
             start_all(store_copies(layer, stores, outs, out_sems, False))
 
-        def body(layer, carry):
+        def onward(layer):
             def target(span, value):
                 inputs_ref[layer + 1, :, span] = value
 
-            run(layer, False, target)
+            return target
+
+        def leave(span, value):
+            last_ref[:, span] = value
+
+        def held_layer(layer, target):
+            run(
+                layer,
+                lambda: wait_all(layer_copies(layer, layer, weights_ref, held, sems)),
+                lambda columns: held[layer, :, :, :, :, columns],
+                target,
+            )
+
+
+        def body(layer, carry):
+            held_layer(layer, onward(layer))
             return carry
 
         lax.fori_loop(0, LAYERS - 1, body, 0)
-
-        def target(span, value):
-            last_ref[:, span] = value
-
-        run(LAYERS - 1, True, target)
+        held_layer(LAYERS - 1, leave)
         for layer in range(LAYERS):
             wait_all(store_copies(layer, stores, outs, out_sems, False))
 
 
 def backward_layer(
-    layer, final, cosine_ref, sine_ref, weights_ref, inputs_ref, values_ref, queries_ref,
-    keys_ref, probs_ref, first_ref, grad_ref, held, sems,
+    layer, ready, block_of, cosine_ref, sine_ref, inputs_ref, values_ref, queries_ref,
+    keys_ref, probs_ref, first_ref, grad_ref,
 ):
     upstream = first_ref[...]
     tokens = upstream.shape[0]
-    slot = layer % 2
     cosine = cosine_ref[...]
     sine = sine_ref[...]
     low = lane_index(tokens) < QK_DIM
@@ -246,11 +232,9 @@
     grad_qkv = grad_ref[layer]
     wide = inputs_ref[layer].astype(F32)
     parts = []
+    ready()
     for step in range(ROW_STEPS):
-        wait_all(row_copies(slot, layer, step, weights_ref, held, sems))
-        if not final:
-            start_all(row_copies(1 - slot, layer - 1, step, weights_ref, held, sems))
-        block = held[slot, step].reshape(COLUMNS, WIDTH)
+        block = block_of(step).reshape(COLUMNS, WIDTH)
         parts.append(dot(grad_qkv, block, 1, 1))
     grad_normed = jnp.concatenate(parts, axis=1)
     scale = lax.rsqrt(jnp.mean(wide * wide, axis=-1, keepdims=True) + EPSILON)
@@ -259,34 +243,38 @@
     first_ref[...] = (upstream.astype(F32) + grad_inputs).astype(BF16)
 
 
-def backward_kernel(flag_ref, g_ref, cosine_ref, sine_ref, weights_ref, *rest):
+def backward_kernel(flag_ref, g_ref, cosine_ref, sine_ref, top_ref, weights_ref, *rest):
     outer = rest[:5]
     first_ref, grad_out, held, *stores, grad_ref, sems, in_sems, out_sems = rest[-12:]
 
     @pl.when(flag_ref[0] == 1)
     def active():
         top = LAYERS - 1
-        start_all(store_copies(top, stores, outer, in_sems, True))
-        for step in range(ROW_STEPS):
-            start_all(row_copies(top % 2, top, step, weights_ref, held, sems))
-        for layer in reversed(range(top)):
+        for layer in reversed(range(LAYERS)):
             start_all(store_copies(layer, stores, outer, in_sems, True))
+            if layer < top:
+                start_all(layer_copies(layer, layer, weights_ref, held, sems))
         first_ref[...] = g_ref[...]
 
-        def run(layer, final):
+        def run(layer, ready, block_of):
             wait_all(store_copies(layer, stores, outer, in_sems, True))
             backward_layer(
-                layer, final, cosine_ref, sine_ref, weights_ref, *stores, first_ref, grad_ref,
-                held, sems,
+                layer, ready, block_of, cosine_ref, sine_ref, *stores, first_ref, grad_ref
             )
             start_all(store_copies(layer, [grad_ref], [grad_out], out_sems, False))
 
+        run(top, lambda: None, lambda step: top_ref[step])
+
         def body(step, carry):
-            run(top - step, False)
+            layer = top - step
+            run(
+                layer,
+                lambda: wait_all(layer_copies(layer, layer, weights_ref, held, sems)),
+                lambda part: held[layer, part],
+            )
             return carry
 
-        lax.fori_loop(0, top, body, 0)
-        run(0, True)
+        lax.fori_loop(1, LAYERS, body, 0)
         for layer in range(LAYERS):
             wait_all(store_copies(layer, [grad_ref], [grad_out], out_sems, False))
 
@@ -294,7 +282,10 @@
 VMEM_SPEC = pl.BlockSpec(memory_space=pltpu.VMEM)
 SMEM_SPEC = pl.BlockSpec(memory_space=pltpu.SMEM)
 HBM_SPEC = pl.BlockSpec(memory_space=pltpu.HBM)
-STAGE_PARAMS = pltpu.CompilerParams(vmem_limit_bytes=34 * 1024 * 1024)
+
+
+def stage_params(limit):
+    return pltpu.CompilerParams(vmem_limit_bytes=limit * 1024 * 1024)
 
 
 def stage_cost(tokens):
@@ -309,8 +300,12 @@
     return [pltpu.VMEM(each.shape, each.dtype) for each in shapes]
 
 
-HELD = pltpu.VMEM((2, 8, 2, 2, 64, WIDTH), BF16)
-WEIGHT_SEMS = pltpu.SemaphoreType.DMA((2, ROW_STEPS, 2, 2))
+def held_scratch(slots):
+    return pltpu.VMEM((slots, 8, 2, 2, 64, WIDTH), BF16)
+
+
+def weight_sems(slots):
+    return pltpu.SemaphoreType.DMA((slots, 2, 2))
 
 
 def copy_sems(count):
@@ -350,38 +345,38 @@
         out_shape=[jax.ShapeDtypeStruct((tokens, D), BF16), *map(in_hbm_shape, shapes)],
         input_output_aliases={5 + i: 1 + i for i in range(len(stored))},
         scratch_shapes=[
-            HELD,
+            held_scratch(LAYERS),
             pltpu.VMEM((tokens, WIDTH), BF16),
             *buffers(shapes),
-            WEIGHT_SEMS,
+            weight_sems(LAYERS),
             copy_sems(len(shapes)),
         ],
         cost_estimate=stage_cost(tokens),
         name="forward_stage",
-        compiler_params=STAGE_PARAMS,
+        compiler_params=stage_params(40),
     )(flag, x, cosine, sine, *map(in_hbm, [weights, *stored]))
 
 
-def run_backward(flag, g, cosine, sine, weights, stored, grads):
+def run_backward(flag, g, cosine, sine, top, weights, stored, grads):
     tokens = g.shape[0]
     shapes = store_shapes(tokens)
     return pl.pallas_call(
         backward_kernel,
-        in_specs=[SMEM_SPEC] + [VMEM_SPEC] * 3 + [HBM_SPEC] * (6 + len(grads)),
+        in_specs=[SMEM_SPEC] + [VMEM_SPEC] * 4 + [HBM_SPEC] * (6 + len(grads)),
         out_specs=[VMEM_SPEC, HBM_SPEC],
         out_shape=[jax.ShapeDtypeStruct((tokens, D), BF16), in_hbm_shape(grad_shape(tokens))],
-        input_output_aliases={10: 1} if grads else {},
+        input_output_aliases={11: 1} if grads else {},
         scratch_shapes=[
-            HELD,
+            held_scratch(SLOTS),
             *buffers([shapes[0], *shapes[2:], grad_shape(tokens)]),
-            WEIGHT_SEMS,
+            weight_sems(SLOTS),
             copy_sems(5),
             copy_sems(1),
         ],
         cost_estimate=stage_cost(tokens),
         name="backward_stage",
-        compiler_params=STAGE_PARAMS,
-    )(flag, g, cosine, sine, *map(in_hbm, [weights, *stored, *grads]))
+        compiler_params=stage_params(32),
+    )(flag, g, cosine, sine, top, *map(in_hbm, [weights, *stored, *grads]))
 
 
 def ring(size, by):
@@ -409,6 +404,10 @@
     )
 
 
+def ordered(gathered, layer):
+    return jnp.swapaxes(gathered[layer], 1, 2)
+
+
 def spread_over_y(value, place):
     pieces = [lax.dynamic_index_in_dim(value, place, 0, keepdims=False)]
     for by in (1, 3, 2):
@@ -445,6 +444,9 @@
         if turn > 0:
             x = lax.ppermute(x, ("xh", "xl"), [(STAGE_X[turn - 1], STAGE_X[turn])])
         x, *stored = run_forward(flag, x, cosine, sine, gathered, stored)
+        if turn == 0:
+            x, late = lax.optimization_barrier((x, gathered))
+            top = ordered(late, LAYERS - 1)
     inputs, normed, *shared = stored
 
     grads = []
@@ -452,7 +454,7 @@
         flag = (stage == turn).astype(jnp.int32).reshape(1)
         if turn < LAYERS - 1:
             g = lax.ppermute(g, ("xh", "xl"), [(STAGE_X[turn + 1], STAGE_X[turn])])
-        g, *grads = run_backward(flag, g, cosine, sine, gathered, [inputs, *shared], grads)
+        g, *grads = run_backward(flag, g, cosine, sine, top, gathered, [inputs, *shared], grads)
     grads = grads[0]
 
     normed_rows = jnp.concatenate(spread_over_y(normed, place))

time: 491 us -> 424 us (0.86)
  waiting for transfers between devices: 367 us -> 311 us
  Pallas kernels: 58 us -> 36.4 us
  local copies, waits for them, and re-layouts: 5.01 us -> 20.9 us
    ppermute x3, waiting for transfers between devices: 155 us -> 97.7 us  [local(): g = lax.ppermute(g, ('xh', 'xl'), [(STAGE_X[turn + 1], STAGE_X[turn])])]
    pallas_call x4, Pallas kernels: 36 us -> 19.7 us  [run_backward(): pl.pallas_call(backward_kernel, in_specs=[SMEM_SPEC] + [VMEM_SPEC] * 4 +...]
    transpose x0 -> x2, local copies, waits for them, and re-layouts: none -> 10.8 us  [ordered(): return jnp.swapaxes(gathered[layer], 1, 2)]
    pallas_call x4, Pallas kernels: 22 us -> 16.7 us  [run_forward(): pl.pallas_call(forward_kernel, in_specs=[SMEM_SPEC] + [VMEM_SPEC] * 3 + [...]
    unnamed x10 -> x16, local copies, waits for them, and re-layouts: 0.11 us -> 5.28 us
  transfers between devices with their start and end apart: 23 -> 23, of which waited for: 16 -> 16; matrix products, arithmetic and copies ran while one was open for 1% -> 3% of each run, Pallas kernels for 7% -> 5%
where the time goes in v3:
time: 424 us; the launch traced here: 416 us
  waiting for transfers between devices  311 us (73%)
  Pallas kernels  36.4 us (9%)
  starting transfers between devices  26.1 us (6%)
  local copies, waits for them, and re-layouts  20.9 us (5%)
  between operations  14.1 us (3%)
    all_gather x1, waiting for transfers between devices, local(): gathered = lax.all_gather(shard, ('y', 'z', 'core'), axis=0, tiled=False)  131 us
    ppermute x3, waiting for transfers between devices, local(): g = lax.ppermute(g, ('xh', 'xl'), [(STAGE_X[turn + 1], STAGE_X[turn])])  97.7 us
    reduce_scatter x1, waiting for transfers between devices, local(): total = lax.psum_scatter(terms, 'z', scatter_dimension=0, tiled=True)  45.5 us
    pallas_call x4, Pallas kernels, run_backward(): pl.pallas_call(backward_kernel, in_specs=[SMEM_SPEC] + [VMEM_SPEC] * 4 +...  19.7 us
    pallas_call x4, Pallas kernels, run_forward(): pl.pallas_call(forward_kernel, in_specs=[SMEM_SPEC] + [VMEM_SPEC] * 3 + [...  16.7 us
    ppermute x6, waiting for transfers between devices, spread_over_y(): pieces.append(lax.ppermute(piece, 'y', ring(4, by)))  15.9 us
    transpose x2, local copies, waits for them, and re-layouts, ordered(): return jnp.swapaxes(gathered[layer], 1, 2)  10.8 us
    ppermute x4, waiting for transfers between devices, from_partner(): return lax.ppermute(value, 'xl', ring(2, 1))  8.79 us
  transfers between devices with their start and end apart: 23, of which 16 were waited for; matrix products, arithmetic and copies ran while one was open for 3% of the time, Pallas kernels for 5%

profile of v3, /device:TPU:1, one launch (start us, length us, event | category | flops | bytes accessed | tf_op | source)
XLA Modules:
  0.0 416.1 jit_solution(17068250939379325090)
XLA Ops:
  7.7 2.1 collective-permute-start.2
  9.8 4.0 collective-permute-done.2
  14.7 2.3 collective-permute-start.1
  18.7 2.3 collective-permute-done
  21.0 131.2 %all-gather.2.cloned.1.call-done = bf16[64,2,64,1792]{3,2,1,0:T(8,128)(2,1)} async-done(((bf16[1,2,64,1792]{3,2,1,0:T(8,128)(2,1)}), bf16[64,2,64,1792]{3,2,1,0:T(8,128)(2,1)}) %all-gather.2.cloned.1.call-update) | async-done | bytes 29360144 | tf_op jit(solution)/shard_map/all_gather | solution.py:431
  152.2 14.5 %forward_stage.4 = (bf16[64,2048]{1,0:T(8,128)(2,1)S(1)}, bf16[4,64,2048]{2,1,0:T(8,128)(2,1)}, bf16[4,64,2048]{2,1,0:T(8,128)(2,1)}, bf16[4,64,512]{2,1,0:T(8,1...) custom-call(s32[1]{0:T(128)} %bitcast.3.flag_ref, ...), custom_call_target="tpu_custom_call" | custom-call | flops 1879048192 | bytes 29360128 | tf_op jit(solution)/shard_map/forward_stage/pallas_call | solution.py:341
  169.1 4.7 %collective-permute-done.3.x_ref = bf16[64,2048]{1,0:T(8,128)(2,1)S(1)} collective-permute-done((bf16[64,2048]{1,0:T(8,128)(2,1)S(1)}, bf16[64,2048]{1,0:T(8,128)(2,1)S(1)}, u32[]{:S(2)}, u32[]{:S(2)}) %collective-permute-start.3) | collective-permute-done | bytes 262176 | tf_op jit(solution)/shard_map/ppermute | solution.py:445
  177.9 6.9 %slice_bitcast_fusion = bf16[8,2,2,64,1792]{4,3,1,2,0:T(8,128)(2,1)} fusion(bf16[4,8,2,2,64,1792]{5,4,3,2,1,0:T(8,128)(2,1)} %bitcast.69), kind=kLoop, calls=%fused_computation | loop fusion | bytes 14680064 | tf_op jit(solution)/shard_map/transpose | solution.py:408
  184.8 3.9 copy.30.top_ref
  193.3 3.1 copy-done.3
  197.7 2.7 collective-permute-start.7
  202.3 4.6 %collective-permute-done.6 = bf16[64,2048]{1,0:T(8,128)(2,1)S(1)} collective-permute-done((bf16[64,2048]{1,0:T(8,128)(2,1)S(1)}, bf16[64,2048]{1,0:T(8,128)(2,1)S(1)}, u32[]{:S(2)}, u32[]{:S(2)}) %collective-permute-start.6) | collective-permute-done | bytes 262176 | tf_op jit(solution)/shard_map/ppermute | solution.py:415
  207.0 3.8 collective-permute-done.8
  210.9 2.6 collective-permute-start.9
  213.5 97.7 %collective-permute-done.13.g_ref = bf16[64,2048]{1,0:T(8,128)(2,1)S(1)} collective-permute-done((bf16[64,2048]{1,0:T(8,128)(2,1)S(1)}, bf16[64,2048]{1,0:T(8,128)(2,1)S(1)}, u32[]{:S(2)}, u32[]{:S(2)}) %collective-permute-start.13) | collective-permute-done | bytes 262176 | tf_op jit(solution)/shard_map/ppermute | solution.py:456
  311.2 18.2 %backward_stage.7 = (bf16[64,2048]{1,0:T(8,128)(2,1)}, bf16[4,64,1792]{2,1,0:T(8,128)(2,1)}) custom-call(s32[1]{0:T(128)} %bitcast.3.flag_ref, bf16[64,2048]{1,0:T(8,128)(2,1)S(1)} %collective-permute-done.13.g_ref, f32[64,128]{1,0:T(8,128)S(1)} %get-tuple-element.100.cosine_ref, ...), custom_call_target="tpu_custom_call", output_to_operand_aliasing={{1}: (11, {})} | custom-call | flops 1879048192 | bytes 29360128 | tf_op jit(solution)/shard_map/backward_stage/pallas_call | solution.py:363
  330.8 2.7 collective-permute-start.15
  333.5 3.4 collective-permute-done.14
  338.9 2.1 collective-permute-done.16
  341.1 5.6 %collective-permute-start.17 = (bf16[256,896]{1,0:T(8,128)(2,1)S(1)}, bf16[256,896]{1,0:T(8,128)(2,1)S(1)}, u32[]{:S(2)}, u32[]{:S(2)}) collective-permute-start(bf16[256,896]{1,0:T(8,128)(2,1)S(1)} %get-tuple-element.83), channel_id=1, source_target_pairs={{0,1},{1,0},{2,3},{3,2},{4,5},{5,4},{6,7},{7,6},{8,9},{9,8},{10,11... | collective-permute-start | bytes 1376264 | tf_op jit(solution)/shard_map/ppermute | solution.py:461
  348.2 4.2 %convolution_convert_fusion = bf16[2048,896]{1,0:T(8,128)(2,1)} fusion(bf16[512,2048]{1,0:T(8,128)(2,1)S(1)} %constant_dynamic-update-slice_fusion, bf16[256,896]{1,0:T(8,128)(2,1)S(1)} %collective-permute-done.17, bf16[256,896]{1,0:T(8,128)(2,1)S(1)} %get-tuple-element.82), kind=kOutput, calls=%fused_computation.1 | convolution fusion | flops 1882718208 | bytes 6684672 | tf_op jit(solution)/shard_map/dot_general | solution.py:30
  352.4 45.5 %reduce-scatter.2.cloned.1.call-done = bf16[256,896]{1,0:T(8,128)(2,1)} async-done(((bf16[2048,896]{1,0:T(8,128)(2,1)}), bf16[256,896]{1,0:T(8,128)(2,1)}) %reduce-scatter.2.cloned.1.call-update) | async-done | bytes 458768 | tf_op jit(solution)/shard_map/reduce_scatter | solution.py:469
  401.4 3.0 collective-permute-done.19
  404.4 2.6 collective-permute-done.20
  (78 shorter events, 28.4 us)
Async XLA Ops:
  6.5 145.7 %all-gather.2.cloned.1.call-start = ((), (), s32[]{:S(2)}) async-start(), calls=%async_computation.1 | async-start | bytes 29818880 | tf_op jit(solution)/shard_map/all_gather | solution.py:431
  7.7 6.1 %collective-permute-start.2 = (bf16[64,1792]{1,0:T(8,128)(2,1)S(1)}, bf16[64,1792]{1,0:T(8,128)(2,1)S(1)}, u32[]{:S(2)}, u32[]{:S(2)}) collective-permute-start(bf16[64,1792]{1,0:T(8,128)(2,1)S(1)} %get-tuple-element.96), channel_id=1, source_target_pairs={{0,2},{2,0},{1,3},{3,1},{4,6},{6,4},{5,7},{7,5},{8,10},{10,8},{9,1... | collective-permute-start | bytes 688136 | tf_op jit(solution)/shard_map/ppermute | solution.py:387
  14.7 383.3 %reduce-scatter.2.cloned.1.call-start = ((), (), s32[]{:S(2)}) async-start(), calls=%async_computation.2 | async-start | bytes 4128768 | tf_op jit(solution)/shard_map/reduce_scatter | solution.py:469
  14.7 3.2 collective-permute-start.1
  17.0 3.9 collective-permute-start
  166.8 7.1 %collective-permute-start.3 = (bf16[64,2048]{1,0:T(8,128)(2,1)S(1)}, bf16[64,2048]{1,0:T(8,128)(2,1)S(1)}, u32[]{:S(2)}, u32[]{:S(2)}) collective-permute-start(bf16[64,2048]{1,0:T(8,128)(2,1)S(1)} %get-tuple-element.42), channel_id=1, source_target_pairs={{0,128},{1,129},{4,132},{5,133},{8,136},{9,137},{12,140},{13,141},... | collective-permute-start | bytes 786440 | tf_op jit(solution)/shard_map/ppermute | solution.py:445
  169.0 7.6 %collective-permute-start.10 = (bf16[32,2048]{1,0:T(8,128)(2,1)S(1)}, bf16[32,2048]{1,0:T(8,128)(2,1)S(1)}, u32[]{:S(2)}, u32[]{:S(2)}) collective-permute-start(bf16[32,2048]{1,0:T(8,128)(2,1)S(1)} %bitcast.77), channel_id=1, source_target_pairs={{0,2},{2,0},{1,3},{3,1},{4,6},{6,4},{5,7},{7,5},{8,10},{10,8},{9,1... | collective-permute-start | bytes 393224 | tf_op jit(solution)/shard_map/ppermute | solution.py:387
  174.2 2.5 collective-permute-start.4
  177.3 11.5 %collective-permute-start.5 = (bf16[64,2048]{1,0:T(8,128)(2,1)S(1)}, bf16[64,2048]{1,0:T(8,128)(2,1)S(1)}, u32[]{:S(2)}, u32[]{:S(2)}) collective-permute-start(bf16[64,2048]{1,0:T(8,128)(2,1)S(1)} %get-tuple-element.56), channel_id=1, source_target_pairs={{2,130},{3,131},{6,134},{7,135},{10,138},{11,139},{14,142},{15,143... | collective-permute-start | bytes 786440 | tf_op jit(solution)/shard_map/ppermute | solution.py:445
  192.5 0.7 collective-permute-start.11
  196.7 3.8 collective-permute-start.12
  197.7 9.3 %collective-permute-start.6 = (bf16[64,2048]{1,0:T(8,128)(2,1)S(1)}, bf16[64,2048]{1,0:T(8,128)(2,1)S(1)}, u32[]{:S(2)}, u32[]{:S(2)}) collective-permute-start(bf16[64,2048]{1,0:T(8,128)(2,1)S(1)} %get-tuple-element.81), channel_id=1, source_target_pairs={{0,32},{32,64},{64,96},{96,0},{1,33},{33,65},{65,97},{97,1},{2,34}... | collective-permute-start | bytes 786440 | tf_op jit(solution)/shard_map/ppermute | solution.py:415
  197.7 9.2 %collective-permute-start.7 = (bf16[64,2048]{1,0:T(8,128)(2,1)S(1)}, bf16[64,2048]{1,0:T(8,128)(2,1)S(1)}, u32[]{:S(2)}, u32[]{:S(2)}) collective-permute-start(bf16[64,2048]{1,0:T(8,128)(2,1)S(1)} %get-tuple-element.80), channel_id=1, source_target_pairs={{0,96},{32,0},{64,32},{96,64},{1,97},{33,1},{65,33},{97,65},{2,98}... | collective-permute-start | bytes 786440 | tf_op jit(solution)/shard_map/ppermute | solution.py:415
  200.4 10.3 %collective-permute-start.8 = (bf16[64,2048]{1,0:T(8,128)(2,1)S(1)}, bf16[64,2048]{1,0:T(8,128)(2,1)S(1)}, u32[]{:S(2)}, u32[]{:S(2)}) collective-permute-start(bf16[64,2048]{1,0:T(8,128)(2,1)S(1)} %get-tuple-element.79), channel_id=1, source_target_pairs={{0,64},{32,96},{64,0},{96,32},{1,65},{33,97},{65,1},{97,33},{2,66}... | collective-permute-start | bytes 786440 | tf_op jit(solution)/shard_map/ppermute | solution.py:415
  201.0 110.1 %collective-permute-start.13 = (bf16[64,2048]{1,0:T(8,128)(2,1)S(1)}, bf16[64,2048]{1,0:T(8,128)(2,1)S(1)}, u32[]{:S(2)}, u32[]{:S(2)}) collective-permute-start(bf16[64,2048]{1,0:T(8,128)(2,1)S(1)} %get-tuple-element.74), channel_id=1, source_target_pairs={{128,0},{129,1},{132,4},{133,5},{136,8},{137,9},{140,12},{141,13},... | collective-permute-start | bytes 786440 | tf_op jit(solution)/shard_map/ppermute | solution.py:456
  210.9 135.9 %collective-permute-start.9 = (bf16[256,2048]{1,0:T(8,128)(2,1)S(1)}, bf16[256,2048]{1,0:T(8,128)(2,1)S(1)}, u32[]{:S(2)}, u32[]{:S(2)}) collective-permute-start(bf16[256,2048]{1,0:T(8,128)(2,1)S(1)} %pad_maximum_fusion), channel_id=1, source_target_pairs={{0,1},{1,0},{2,3},{3,2},{4,5},{5,4},{6,7},{7,6},{8,9},{9,8},{10,11... | collective-permute-start | bytes 3145736 | tf_op jit(solution)/shard_map/ppermute | solution.py:461
  330.7 6.2 %collective-permute-start.14 = (bf16[64,1792]{1,0:T(8,128)(2,1)S(1)}, bf16[64,1792]{1,0:T(8,128)(2,1)S(1)}, u32[]{:S(2)}, u32[]{:S(2)}) collective-permute-start(bf16[64,1792]{1,0:T(8,128)(2,1)S(1)} %get-tuple-element.87), channel_id=1, source_target_pairs={{0,32},{32,64},{64,96},{96,0},{1,33},{33,65},{65,97},{97,1},{2,34}... | collective-permute-start | bytes 688136 | tf_op jit(solution)/shard_map/ppermute | solution.py:415
  330.8 8.1 %collective-permute-start.15 = (bf16[64,1792]{1,0:T(8,128)(2,1)S(1)}, bf16[64,1792]{1,0:T(8,128)(2,1)S(1)}, u32[]{:S(2)}, u32[]{:S(2)}) collective-permute-start(bf16[64,1792]{1,0:T(8,128)(2,1)S(1)} %get-tuple-element.86), channel_id=1, source_target_pairs={{0,96},{32,0},{64,32},{96,64},{1,97},{33,1},{65,33},{97,65},{2,98}... | collective-permute-start | bytes 688136 | tf_op jit(solution)/shard_map/ppermute | solution.py:415
  333.5 7.5 %collective-permute-start.16 = (bf16[64,1792]{1,0:T(8,128)(2,1)S(1)}, bf16[64,1792]{1,0:T(8,128)(2,1)S(1)}, u32[]{:S(2)}, u32[]{:S(2)}) collective-permute-start(bf16[64,1792]{1,0:T(8,128)(2,1)S(1)} %get-tuple-element.85), channel_id=1, source_target_pairs={{0,64},{32,96},{64,0},{96,32},{1,65},{33,97},{65,1},{97,33},{2,66}... | collective-permute-start | bytes 688136 | tf_op jit(solution)/shard_map/ppermute | solution.py:415
  341.1 7.0 %collective-permute-start.17 = (bf16[256,896]{1,0:T(8,128)(2,1)S(1)}, bf16[256,896]{1,0:T(8,128)(2,1)S(1)}, u32[]{:S(2)}, u32[]{:S(2)}) collective-permute-start(bf16[256,896]{1,0:T(8,128)(2,1)S(1)} %get-tuple-element.83), channel_id=1, source_target_pairs={{0,1},{1,0},{2,3},{3,2},{4,5},{5,4},{6,7},{7,6},{8,9},{9,8},{10,11... | collective-permute-start | bytes 1376264 | tf_op jit(solution)/shard_map/ppermute | solution.py:461
  352.4 56.6 %copy-start.1 = (bf16[8,16,2048]{2,1,0:T(8,128)(2,1)S(1)}, bf16[8,16,2048]{2,1,0:T(8,128)(2,1)}, u32[]{:S(2)}) copy-start(bf16[8,16,2048]{2,1,0:T(8,128)(2,1)} %param.4) | copy-start | bytes 1572868
  399.0 2.4 collective-permute-start.18
  399.7 4.7 %collective-permute-start.19 = (bf16[64,896]{1,0:T(8,128)(2,1)S(1)}, bf16[64,896]{1,0:T(8,128)(2,1)S(1)}, u32[]{:S(2)}, u32[]{:S(2)}) collective-permute-start(bf16[64,896]{1,0:T(8,128)(2,1)S(1)} %get-tuple-element.94), channel_id=1, source_target_pairs={{0,2},{1,3},{2,0},{3,1},{4,6},{5,7},{6,4},{7,5},{8,10},{9,11},{10,... | collective-permute-start | bytes 344072 | tf_op jit(solution)/shard_map/ppermute | solution.py:480
  400.9 6.1 %collective-permute-start.20 = (bf16[64,896]{1,0:T(8,128)(2,1)S(1)}, bf16[64,896]{1,0:T(8,128)(2,1)S(1)}, u32[]{:S(2)}, u32[]{:S(2)}) collective-permute-start(bf16[64,896]{1,0:T(8,128)(2,1)S(1)} %get-tuple-element.93), channel_id=1, source_target_pairs={{0,3},{1,2},{2,1},{3,0},{4,7},{5,6},{6,5},{7,4},{8,11},{9,10},{10,... | collective-permute-start | bytes 344072 | tf_op jit(solution)/shard_map/ppermute | solution.py:480
  (5 other events, 26.1 us)
Sparse Core Ops, SparseCore 0:
  14.8 137.3 all-gather.1
  352.5 45.3 reduce-scatter.1

commit v4 on v3

--- a/solution.py
+++ b/solution.py
@@ -139,52 +139,85 @@
     return copies
 
 
+def forward_stage(
+    x_ref, cosine_ref, sine_ref, weights_ref, stores, outs, held, qkv_ref, sems, out_sems, leave
+):
+    inputs_ref = stores[0]
+    for layer in range(LAYERS):
+        start_all(layer_copies(layer, layer, weights_ref, held, sems))
+    inputs_ref[0] = x_ref[...]
+    cosine = cosine_ref[...]
+    sine = sine_ref[...]
+    mask = score_mask(x_ref.shape[0])
+
+    def run(layer, target):
+        forward_layer(
+            layer,
+            lambda: wait_all(layer_copies(layer, layer, weights_ref, held, sems)),
+            lambda columns: held[layer, :, :, :, :, columns],
+            cosine, sine, mask, *stores, target, qkv_ref,
+        )
+        start_all(store_copies(layer, stores[: len(outs)], outs, out_sems, False))
+
+    def body(layer, carry):
+        def target(span, value):
+            inputs_ref[layer + 1, :, span] = value
+
+        run(layer, target)
+        return carry
+
+    lax.fori_loop(0, LAYERS - 1, body, 0)
+    run(LAYERS - 1, leave)
+
+
 def forward_kernel(flag_ref, x_ref, cosine_ref, sine_ref, weights_ref, *rest):
     held, qkv_ref, *stores, sems, out_sems = rest[-10:]
     last_ref, *outs = rest[-17:-10]
-    inputs_ref = stores[0]
 
     @pl.when(flag_ref[0] == 1)
     def active():
-        for layer in range(LAYERS):
-            start_all(layer_copies(layer, layer, weights_ref, held, sems))
-        inputs_ref[0] = x_ref[...]
-        cosine = cosine_ref[...]
-        sine = sine_ref[...]
-        mask = score_mask(x_ref.shape[0])
-
-        def run(layer, ready, block_of, target):
-            forward_layer(
-                layer, ready, block_of, cosine, sine, mask, *stores, target, qkv_ref
-            )
-            start_all(store_copies(layer, stores, outs, out_sems, False))
-
-        def onward(layer):
-            def target(span, value):
-                inputs_ref[layer + 1, :, span] = value
-
-            return target
-
         def leave(span, value):
             last_ref[:, span] = value
 
-        def held_layer(layer, target):
-            run(
-                layer,
-                lambda: wait_all(layer_copies(layer, layer, weights_ref, held, sems)),
-                lambda columns: held[layer, :, :, :, :, columns],
-                target,
-            )
-
-
-        def body(layer, carry):
-            held_layer(layer, onward(layer))
-            return carry
-
-        lax.fori_loop(0, LAYERS - 1, body, 0)
-        held_layer(LAYERS - 1, leave)
+        forward_stage(
+            x_ref, cosine_ref, sine_ref, weights_ref, stores, outs, held, qkv_ref, sems,
+            out_sems, leave,
+        )
         for layer in range(LAYERS):
             wait_all(store_copies(layer, stores, outs, out_sems, False))
+
+
+def turn_kernel(flag_ref, x_ref, g_ref, cosine_ref, sine_ref, weights_ref, _normed, *rest):
+    first_ref, normed_out, grad_out, held, qkv_ref, *stores = rest[:-4]
+    grad_ref, sems, out_sems, grad_sems = rest[-4:]
+    normed_ref, inputs_ref, *shared = stores
+
+    @pl.when(flag_ref[0] == 1)
+    def active():
+        def leave(span, value):
+            first_ref[:, span] = value
+
+        forward_stage(
+            x_ref, cosine_ref, sine_ref, weights_ref, [inputs_ref, normed_ref, *shared], [],
+            held, qkv_ref, sems, out_sems, leave,
+        )
+        for layer in range(LAYERS):
+            start_all(store_copies(layer, [normed_ref], [normed_out], out_sems, False))
+        first_ref[...] = g_ref[...]
+
+        def body(step, carry):
+            layer = LAYERS - 1 - step
+            backward_layer(
+                layer, lambda: None, lambda part: held[layer, part], cosine_ref, sine_ref,
+                inputs_ref, *shared, first_ref, grad_ref,
+            )
+            start_all(store_copies(layer, [grad_ref], [grad_out], grad_sems, False))
+            return carry
+
+        lax.fori_loop(0, LAYERS, body, 0)
+        for layer in range(LAYERS):
+            wait_all(store_copies(layer, [normed_ref], [normed_out], out_sems, False))
+            wait_all(store_copies(layer, [grad_ref], [grad_out], grad_sems, False))
 
 
 def backward_layer(
@@ -357,6 +390,34 @@
     )(flag, x, cosine, sine, *map(in_hbm, [weights, *stored]))
 
 
+def run_turn(flag, x, g, cosine, sine, weights, normed):
+    tokens = g.shape[0]
+    shapes = store_shapes(tokens)
+    return pl.pallas_call(
+        turn_kernel,
+        in_specs=[SMEM_SPEC] + [VMEM_SPEC] * 4 + [HBM_SPEC] * 2,
+        out_specs=[VMEM_SPEC] + [HBM_SPEC] * 2,
+        out_shape=[
+            jax.ShapeDtypeStruct((tokens, D), BF16),
+            in_hbm_shape(shapes[1]),
+            in_hbm_shape(grad_shape(tokens)),
+        ],
+        input_output_aliases={6: 1},
+        scratch_shapes=[
+            held_scratch(LAYERS),
+            pltpu.VMEM((tokens, WIDTH), BF16),
+            *buffers([shapes[1], shapes[0], *shapes[2:]]),
+            pltpu.VMEM((LAYERS, tokens, WIDTH), BF16),
+            weight_sems(LAYERS),
+            copy_sems(1),
+            copy_sems(1),
+        ],
+        cost_estimate=stage_cost(tokens),
+        name="turn_stage",
+        compiler_params=stage_params(42),
+    )(flag, x, g, cosine, sine, *map(in_hbm, [weights, normed]))
+
+
 def run_backward(flag, g, cosine, sine, top, weights, stored, grads):
     tokens = g.shape[0]
     shapes = store_shapes(tokens)
@@ -439,21 +500,22 @@
     cosine, sine = rotary_tables(span)
 
     stored = []
-    for turn in range(LAYERS):
+    for turn in range(LAYERS - 1):
         flag = (stage == turn).astype(jnp.int32).reshape(1)
         if turn > 0:
             x = lax.ppermute(x, ("xh", "xl"), [(STAGE_X[turn - 1], STAGE_X[turn])])
         x, *stored = run_forward(flag, x, cosine, sine, gathered, stored)
-        if turn == 0:
-            x, late = lax.optimization_barrier((x, gathered))
-            top = ordered(late, LAYERS - 1)
     inputs, normed, *shared = stored
 
-    grads = []
-    for turn in reversed(range(LAYERS)):
+    x = lax.ppermute(x, ("xh", "xl"), [(STAGE_X[LAYERS - 2], STAGE_X[LAYERS - 1])])
+    flag = (stage == LAYERS - 1).astype(jnp.int32).reshape(1)
+    g, normed, grads = run_turn(flag, x, g, cosine, sine, gathered, normed)
+    grads = [grads]
+    g, late = lax.optimization_barrier((g, gathered))
+    top = ordered(late, LAYERS - 1)
+    for turn in reversed(range(LAYERS - 1)):
         flag = (stage == turn).astype(jnp.int32).reshape(1)
-        if turn < LAYERS - 1:
-            g = lax.ppermute(g, ("xh", "xl"), [(STAGE_X[turn + 1], STAGE_X[turn])])
+        g = lax.ppermute(g, ("xh", "xl"), [(STAGE_X[turn + 1], STAGE_X[turn])])
         g, *grads = run_backward(flag, g, cosine, sine, top, gathered, [inputs, *shared], grads)
     grads = grads[0]
 

time: 424 us -> 416 us (0.981)
  local copies, waits for them, and re-layouts: 20.9 us -> 15.7 us
    unnamed x16 -> x12, local copies, waits for them, and re-layouts: 5.28 us -> 0.12 us
    pallas_call x4 -> x3, Pallas kernels: 16.7 us -> 15.4 us  [run_forward(): pl.pallas_call(forward_kernel, in_specs=[SMEM_SPEC] + [VMEM_SPEC] * 3 + [...]
    pallas_call x4 -> x3, Pallas kernels: 19.7 us -> 19.3 us  [run_backward(): pl.pallas_call(backward_kernel, in_specs=[SMEM_SPEC] + [VMEM_SPEC] * 4 +...]
  transfers between devices with their start and end apart: 23 -> 23, of which waited for: 16 -> 16; matrix products, arithmetic and copies ran while one was open for 3% -> 4% of each run, Pallas kernels for 5% -> 5%
where the time goes in v4:
time: 416 us; the launch traced here: 409 us
  waiting for transfers between devices  310 us (75%)
  Pallas kernels  34.9 us (8%)
  starting transfers between devices  25.6 us (6%)
  local copies, waits for them, and re-layouts  15.7 us (4%)
  between operations  14.3 us (3%)
  matrix products  4.17 us (1%)
    all_gather x1, waiting for transfers between devices, local(): gathered = lax.all_gather(shard, ('y', 'z', 'core'), axis=0, tiled=False)  131 us
    ppermute x3, waiting for transfers between devices, local(): g = lax.ppermute(g, ('xh', 'xl'), [(STAGE_X[turn + 1], STAGE_X[turn])])  94.8 us
    reduce_scatter x1, waiting for transfers between devices, local(): total = lax.psum_scatter(terms, 'z', scatter_dimension=0, tiled=True)  45.6 us
    pallas_call x3, Pallas kernels, run_backward(): pl.pallas_call(backward_kernel, in_specs=[SMEM_SPEC] + [VMEM_SPEC] * 4 +...  19.3 us
    ppermute x6, waiting for transfers between devices, spread_over_y(): pieces.append(lax.ppermute(piece, 'y', ring(4, by)))  16.1 us
    pallas_call x3, Pallas kernels, run_forward(): pl.pallas_call(forward_kernel, in_specs=[SMEM_SPEC] + [VMEM_SPEC] * 3 + [...  15.4 us
    transpose x2, local copies, waits for them, and re-layouts, ordered(): return jnp.swapaxes(gathered[layer], 1, 2)  10.7 us
    ppermute x4, waiting for transfers between devices, from_partner(): return lax.ppermute(value, 'xl', ring(2, 1))  10 us
  transfers between devices with their start and end apart: 23, of which 16 were waited for; matrix products, arithmetic and copies ran while one was open for 4% of the time, Pallas kernels for 5%

profile of v4, /device:TPU:1, one launch (start us, length us, event | category | flops | bytes accessed | tf_op | source)
XLA Modules:
  0.0 408.7 jit_solution(18110224342015477262)
XLA Ops:
  7.7 2.1 collective-permute-start.2
  9.8 4.0 collective-permute-done.2
  14.7 2.3 collective-permute-start.1
  18.7 2.3 collective-permute-done
  21.0 131.2 %all-gather.2.cloned.1.call-done = bf16[64,2,64,1792]{3,2,1,0:T(8,128)(2,1)} async-done(((bf16[1,2,64,1792]{3,2,1,0:T(8,128)(2,1)}), bf16[64,2,64,1792]{3,2,1,0:T(8,128)(2,1)}) %all-gather.2.cloned.1.call-update) | async-done | bytes 29360144 | tf_op jit(solution)/shard_map/all_gather | solution.py:492
  152.2 14.5 %forward_stage.3 = (bf16[64,2048]{1,0:T(8,128)(2,1)S(1)}, bf16[4,64,2048]{2,1,0:T(8,128)(2,1)}, bf16[4,64,2048]{2,1,0:T(8,128)(2,1)}, bf16[4,64,512]{2,1,0:T(8,1...) custom-call(s32[1]{0:T(128)} %bitcast.3.flag_ref, ...), custom_call_target="tpu_custom_call" | custom-call | flops 1879048192 | bytes 29360128 | tf_op jit(solution)/shard_map/forward_stage/pallas_call | solution.py:374
  168.1 5.7 %collective-permute-done.3.x_ref = bf16[64,2048]{1,0:T(8,128)(2,1)S(1)} collective-permute-done((bf16[64,2048]{1,0:T(8,128)(2,1)S(1)}, bf16[64,2048]{1,0:T(8,128)(2,1)S(1)}, u32[]{:S(2)}, u32[]{:S(2)}) %collective-permute-start.3) | collective-permute-done | bytes 262176 | tf_op jit(solution)/shard_map/ppermute | solution.py:506
  177.2 3.0 collective-permute-done.6
  181.1 6.9 %slice_bitcast_fusion = bf16[8,2,2,64,1792]{4,3,1,2,0:T(8,128)(2,1)} fusion(bf16[4,8,2,2,64,1792]{5,4,3,2,1,0:T(8,128)(2,1)} %bitcast.70), kind=kLoop, calls=%fused_computation | loop fusion | bytes 14680064 | tf_op jit(solution)/shard_map/transpose | solution.py:469
  188.0 3.9 copy.24.top_ref
  193.3 2.7 collective-permute-start.8
  197.7 3.4 collective-permute-done.7
  201.1 4.8 %collective-permute-done.9 = bf16[64,2048]{1,0:T(8,128)(2,1)S(1)} collective-permute-done((bf16[64,2048]{1,0:T(8,128)(2,1)S(1)}, bf16[64,2048]{1,0:T(8,128)(2,1)S(1)}, u32[]{:S(2)}, u32[]{:S(2)}) %collective-permute-start.9) | collective-permute-done | bytes 262176 | tf_op jit(solution)/shard_map/ppermute | solution.py:476
  206.0 3.0 collective-permute-start.10
  209.1 94.8 %collective-permute-done.13.g_ref = bf16[64,2048]{1,0:T(8,128)(2,1)S(1)} collective-permute-done((bf16[64,2048]{1,0:T(8,128)(2,1)S(1)}, bf16[64,2048]{1,0:T(8,128)(2,1)S(1)}, u32[]{:S(2)}, u32[]{:S(2)}) %collective-permute-start.13) | collective-permute-done | bytes 262176 | tf_op jit(solution)/shard_map/ppermute | solution.py:518
  303.9 18.4 %backward_stage.5 = (bf16[64,2048]{1,0:T(8,128)(2,1)}, bf16[4,64,1792]{2,1,0:T(8,128)(2,1)}) custom-call(s32[1]{0:T(128)} %bitcast.3.flag_ref, bf16[64,2048]{1,0:T(8,128)(2,1)S(1)} %collective-permute-done.13.g_ref, f32[64,128]{1,0:T(8,128)S(1)} %get-tuple-element.90.cosine_ref, ...), custom_call_target="tpu_custom_call", output_to_operand_aliasing={{1}: (11, {})} | custom-call | flops 1879048192 | bytes 29360128 | tf_op jit(solution)/shard_map/backward_stage/pallas_call | solution.py:424
  323.7 2.7 collective-permute-start.15
  326.4 3.4 collective-permute-done.14
  331.8 2.5 collective-permute-done.16
  334.5 4.7 %collective-permute-start.17 = (bf16[256,896]{1,0:T(8,128)(2,1)S(1)}, bf16[256,896]{1,0:T(8,128)(2,1)S(1)}, u32[]{:S(2)}, u32[]{:S(2)}) collective-permute-start(bf16[256,896]{1,0:T(8,128)(2,1)S(1)} %get-tuple-element.73), channel_id=1, source_target_pairs={{0,1},{1,0},{2,3},{3,2},{4,5},{5,4},{6,7},{7,6},{8,9},{9,8},{10,11... | collective-permute-start | bytes 1376264 | tf_op jit(solution)/shard_map/ppermute | solution.py:523
  340.6 4.2 %convolution_convert_fusion = bf16[2048,896]{1,0:T(8,128)(2,1)} fusion(bf16[512,2048]{1,0:T(8,128)(2,1)S(1)} %constant_dynamic-update-slice_fusion, bf16[256,896]{1,0:T(8,128)(2,1)S(1)} %collective-permute-done.17, bf16[256,896]{1,0:T(8,128)(2,1)S(1)} %get-tuple-element.72), kind=kOutput, calls=%fused_computation.1 | convolution fusion | flops 1882718208 | bytes 6684672 | tf_op jit(solution)/shard_map/dot_general | solution.py:30
  344.8 45.6 %reduce-scatter.2.cloned.1.call-done = bf16[256,896]{1,0:T(8,128)(2,1)} async-done(((bf16[2048,896]{1,0:T(8,128)(2,1)}), bf16[256,896]{1,0:T(8,128)(2,1)}) %reduce-scatter.2.cloned.1.call-update) | async-done | bytes 458768 | tf_op jit(solution)/shard_map/reduce_scatter | solution.py:531
  393.8 3.0 collective-permute-done.19
  396.8 2.6 collective-permute-done.20
  (73 shorter events, 22.9 us)
Async XLA Ops:
  6.5 145.7 %all-gather.2.cloned.1.call-start = ((), (), s32[]{:S(2)}) async-start(), calls=%async_computation.1 | async-start | bytes 29818880 | tf_op jit(solution)/shard_map/all_gather | solution.py:492
  7.7 6.1 %collective-permute-start.2 = (bf16[64,1792]{1,0:T(8,128)(2,1)S(1)}, bf16[64,1792]{1,0:T(8,128)(2,1)S(1)}, u32[]{:S(2)}, u32[]{:S(2)}) collective-permute-start(bf16[64,1792]{1,0:T(8,128)(2,1)S(1)} %get-tuple-element.86), channel_id=1, source_target_pairs={{0,2},{2,0},{1,3},{3,1},{4,6},{6,4},{5,7},{7,5},{8,10},{10,8},{9,1... | collective-permute-start | bytes 688136 | tf_op jit(solution)/shard_map/ppermute | solution.py:448
  14.7 375.7 %reduce-scatter.2.cloned.1.call-start = ((), (), s32[]{:S(2)}) async-start(), calls=%async_computation.2 | async-start | bytes 4128768 | tf_op jit(solution)/shard_map/reduce_scatter | solution.py:531
  14.7 3.2 collective-permute-start.1
  17.0 3.9 collective-permute-start
  166.8 7.1 %collective-permute-start.3 = (bf16[64,2048]{1,0:T(8,128)(2,1)S(1)}, bf16[64,2048]{1,0:T(8,128)(2,1)S(1)}, u32[]{:S(2)}, u32[]{:S(2)}) collective-permute-start(bf16[64,2048]{1,0:T(8,128)(2,1)S(1)} %get-tuple-element.36), channel_id=1, source_target_pairs={{0,128},{1,129},{4,132},{5,133},{8,136},{9,137},{12,140},{13,141},... | collective-permute-start | bytes 786440 | tf_op jit(solution)/shard_map/ppermute | solution.py:506
  174.2 1.7 collective-permute-start.4
  175.8 4.4 %collective-permute-start.6 = (bf16[32,2048]{1,0:T(8,128)(2,1)S(1)}, bf16[32,2048]{1,0:T(8,128)(2,1)S(1)}, u32[]{:S(2)}, u32[]{:S(2)}) collective-permute-start(bf16[32,2048]{1,0:T(8,128)(2,1)S(1)} %bitcast.74), channel_id=1, source_target_pairs={{0,2},{2,0},{1,3},{3,1},{4,6},{6,4},{5,7},{7,5},{8,10},{10,8},{9,1... | collective-permute-start | bytes 393224 | tf_op jit(solution)/shard_map/ppermute | solution.py:448
  176.5 3.7 collective-permute-start.5
  180.4 11.4 %collective-permute-start.11 = (bf16[64,2048]{1,0:T(8,128)(2,1)S(1)}, bf16[64,2048]{1,0:T(8,128)(2,1)S(1)}, u32[]{:S(2)}, u32[]{:S(2)}) collective-permute-start(bf16[64,2048]{1,0:T(8,128)(2,1)S(1)} %get-tuple-element.54), channel_id=1, source_target_pairs={{130,2},{131,3},{134,6},{135,7},{138,10},{139,11},{142,14},{143,15... | collective-permute-start | bytes 786440 | tf_op jit(solution)/shard_map/ppermute | solution.py:518
  192.4 3.6 collective-permute-start.12
  193.2 7.9 %collective-permute-start.7 = (bf16[64,2048]{1,0:T(8,128)(2,1)S(1)}, bf16[64,2048]{1,0:T(8,128)(2,1)S(1)}, u32[]{:S(2)}, u32[]{:S(2)}) collective-permute-start(bf16[64,2048]{1,0:T(8,128)(2,1)S(1)} %get-tuple-element.71), channel_id=1, source_target_pairs={{0,32},{32,64},{64,96},{96,0},{1,33},{33,65},{65,97},{97,1},{2,34}... | collective-permute-start | bytes 786440 | tf_op jit(solution)/shard_map/ppermute | solution.py:476
  193.3 7.8 %collective-permute-start.8 = (bf16[64,2048]{1,0:T(8,128)(2,1)S(1)}, bf16[64,2048]{1,0:T(8,128)(2,1)S(1)}, u32[]{:S(2)}, u32[]{:S(2)}) collective-permute-start(bf16[64,2048]{1,0:T(8,128)(2,1)S(1)} %get-tuple-element.70), channel_id=1, source_target_pairs={{0,96},{32,0},{64,32},{96,64},{1,97},{33,1},{65,33},{97,65},{2,98}... | collective-permute-start | bytes 786440 | tf_op jit(solution)/shard_map/ppermute | solution.py:476
  196.0 9.9 %collective-permute-start.9 = (bf16[64,2048]{1,0:T(8,128)(2,1)S(1)}, bf16[64,2048]{1,0:T(8,128)(2,1)S(1)}, u32[]{:S(2)}, u32[]{:S(2)}) collective-permute-start(bf16[64,2048]{1,0:T(8,128)(2,1)S(1)} %get-tuple-element.69), channel_id=1, source_target_pairs={{0,64},{32,96},{64,0},{96,32},{1,65},{33,97},{65,1},{97,33},{2,66}... | collective-permute-start | bytes 786440 | tf_op jit(solution)/shard_map/ppermute | solution.py:476
  196.4 107.5 %collective-permute-start.13 = (bf16[64,2048]{1,0:T(8,128)(2,1)S(1)}, bf16[64,2048]{1,0:T(8,128)(2,1)S(1)}, u32[]{:S(2)}, u32[]{:S(2)}) collective-permute-start(bf16[64,2048]{1,0:T(8,128)(2,1)S(1)} %get-tuple-element.64), channel_id=1, source_target_pairs={{128,0},{129,1},{132,4},{133,5},{136,8},{137,9},{140,12},{141,13},... | collective-permute-start | bytes 786440 | tf_op jit(solution)/shard_map/ppermute | solution.py:518
  206.0 133.1 %collective-permute-start.10 = (bf16[256,2048]{1,0:T(8,128)(2,1)S(1)}, bf16[256,2048]{1,0:T(8,128)(2,1)S(1)}, u32[]{:S(2)}, u32[]{:S(2)}) collective-permute-start(bf16[256,2048]{1,0:T(8,128)(2,1)S(1)} %pad_maximum_fusion), channel_id=1, source_target_pairs={{0,1},{1,0},{2,3},{3,2},{4,5},{5,4},{6,7},{7,6},{8,9},{9,8},{10,11... | collective-permute-start | bytes 3145736 | tf_op jit(solution)/shard_map/ppermute | solution.py:523
  323.6 6.2 %collective-permute-start.14 = (bf16[64,1792]{1,0:T(8,128)(2,1)S(1)}, bf16[64,1792]{1,0:T(8,128)(2,1)S(1)}, u32[]{:S(2)}, u32[]{:S(2)}) collective-permute-start(bf16[64,1792]{1,0:T(8,128)(2,1)S(1)} %get-tuple-element.77), channel_id=1, source_target_pairs={{0,32},{32,64},{64,96},{96,0},{1,33},{33,65},{65,97},{97,1},{2,34}... | collective-permute-start | bytes 688136 | tf_op jit(solution)/shard_map/ppermute | solution.py:476
  323.7 8.1 %collective-permute-start.15 = (bf16[64,1792]{1,0:T(8,128)(2,1)S(1)}, bf16[64,1792]{1,0:T(8,128)(2,1)S(1)}, u32[]{:S(2)}, u32[]{:S(2)}) collective-permute-start(bf16[64,1792]{1,0:T(8,128)(2,1)S(1)} %get-tuple-element.76), channel_id=1, source_target_pairs={{0,96},{32,0},{64,32},{96,64},{1,97},{33,1},{65,33},{97,65},{2,98}... | collective-permute-start | bytes 688136 | tf_op jit(solution)/shard_map/ppermute | solution.py:476
  326.4 7.9 %collective-permute-start.16 = (bf16[64,1792]{1,0:T(8,128)(2,1)S(1)}, bf16[64,1792]{1,0:T(8,128)(2,1)S(1)}, u32[]{:S(2)}, u32[]{:S(2)}) collective-permute-start(bf16[64,1792]{1,0:T(8,128)(2,1)S(1)} %get-tuple-element.75), channel_id=1, source_target_pairs={{0,64},{32,96},{64,0},{96,32},{1,65},{33,97},{65,1},{97,33},{2,66}... | collective-permute-start | bytes 688136 | tf_op jit(solution)/shard_map/ppermute | solution.py:476
  334.5 6.1 %collective-permute-start.17 = (bf16[256,896]{1,0:T(8,128)(2,1)S(1)}, bf16[256,896]{1,0:T(8,128)(2,1)S(1)}, u32[]{:S(2)}, u32[]{:S(2)}) collective-permute-start(bf16[256,896]{1,0:T(8,128)(2,1)S(1)} %get-tuple-element.73), channel_id=1, source_target_pairs={{0,1},{1,0},{2,3},{3,2},{4,5},{5,4},{6,7},{7,6},{8,9},{9,8},{10,11... | collective-permute-start | bytes 1376264 | tf_op jit(solution)/shard_map/ppermute | solution.py:523
  344.7 56.7 %copy-start.1 = (bf16[8,16,2048]{2,1,0:T(8,128)(2,1)S(1)}, bf16[8,16,2048]{2,1,0:T(8,128)(2,1)}, u32[]{:S(2)}) copy-start(bf16[8,16,2048]{2,1,0:T(8,128)(2,1)} %param.4) | copy-start | bytes 1572868
  391.4 2.4 collective-permute-start.18
  392.1 4.7 %collective-permute-start.19 = (bf16[64,896]{1,0:T(8,128)(2,1)S(1)}, bf16[64,896]{1,0:T(8,128)(2,1)S(1)}, u32[]{:S(2)}, u32[]{:S(2)}) collective-permute-start(bf16[64,896]{1,0:T(8,128)(2,1)S(1)} %get-tuple-element.84), channel_id=1, source_target_pairs={{0,2},{1,3},{2,0},{3,1},{4,6},{5,7},{6,4},{7,5},{8,10},{9,11},{10,... | collective-permute-start | bytes 344072 | tf_op jit(solution)/shard_map/ppermute | solution.py:542
  393.3 6.1 %collective-permute-start.20 = (bf16[64,896]{1,0:T(8,128)(2,1)S(1)}, bf16[64,896]{1,0:T(8,128)(2,1)S(1)}, u32[]{:S(2)}, u32[]{:S(2)}) collective-permute-start(bf16[64,896]{1,0:T(8,128)(2,1)S(1)} %get-tuple-element.83), channel_id=1, source_target_pairs={{0,3},{1,2},{2,1},{3,0},{4,7},{5,6},{6,5},{7,4},{8,11},{9,10},{10,... | collective-permute-start | bytes 344072 | tf_op jit(solution)/shard_map/ppermute | solution.py:542
  (3 other events, 19.9 us)
Sparse Core Ops, SparseCore 0:
  14.8 137.3 all-gather.1
  344.9 45.4 reduce-scatter.1

commit v5 on v4

--- a/solution.py
+++ b/solution.py
@@ -76,13 +76,13 @@
 
 
 def layer_copies(slot, layer, weights_ref, held, sems):
-    return [
-        pltpu.make_async_copy(
-            weights_ref.at[layer, :, core, low], held.at[slot, :, low, core], sems.at[slot, core, low]
-        )
-        for core in range(2)
-        for low in range(2)
-    ]
+    return [pltpu.make_async_copy(weights_ref.at[layer], held.at[slot], sems.at[slot])]
+
+
+def rows_in_order(pieces):
+    return lambda count: jnp.concatenate(
+        [pieces(z, core, low) for z in range(count) for low in range(2) for core in range(2)]
+    )
 
 
 def start_all(copies):
@@ -113,7 +113,7 @@
     ready()
     for step in range(COLUMN_STEPS):
         columns = slice(step * COLUMNS, (step + 1) * COLUMNS)
-        block = block_of(columns).reshape(D, COLUMNS)
+        block = rows_in_order(lambda z, core, low: block_of(z, core, low, columns))(8)
         qkv_ref[:, columns] = dot(normed, block, 1, 0).astype(BF16)
     qkv = qkv_ref[...].astype(F32)
     values_ref[layer] = qkv_ref[:, VALUE_START:]
@@ -154,7 +154,7 @@
         forward_layer(
             layer,
             lambda: wait_all(layer_copies(layer, layer, weights_ref, held, sems)),
-            lambda columns: held[layer, :, :, :, :, columns],
+            lambda z, core, low, columns: held[layer, z, core, low, :, columns],
             cosine, sine, mask, *stores, target, qkv_ref,
         )
         start_all(store_copies(layer, stores[: len(outs)], outs, out_sems, False))
@@ -208,7 +208,7 @@
         def body(step, carry):
             layer = LAYERS - 1 - step
             backward_layer(
-                layer, lambda: None, lambda part: held[layer, part], cosine_ref, sine_ref,
+                layer, lambda: None, lambda z, core, low: held[layer, z, core, low], cosine_ref, sine_ref,
                 inputs_ref, *shared, first_ref, grad_ref,
             )
             start_all(store_copies(layer, [grad_ref], [grad_out], grad_sems, False))
@@ -267,7 +267,7 @@
     parts = []
     ready()
     for step in range(ROW_STEPS):
-        block = block_of(step).reshape(COLUMNS, WIDTH)
+        block = rows_in_order(lambda z, core, low: block_of(step, core, low))(1)
         parts.append(dot(grad_qkv, block, 1, 1))
     grad_normed = jnp.concatenate(parts, axis=1)
     scale = lax.rsqrt(jnp.mean(wide * wide, axis=-1, keepdims=True) + EPSILON)
@@ -276,38 +276,24 @@
     first_ref[...] = (upstream.astype(F32) + grad_inputs).astype(BF16)
 
 
-def backward_kernel(flag_ref, g_ref, cosine_ref, sine_ref, top_ref, weights_ref, *rest):
-    outer = rest[:5]
-    first_ref, grad_out, held, *stores, grad_ref, sems, in_sems, out_sems = rest[-12:]
+def backward_kernel(flag_ref, g_ref, cosine_ref, sine_ref, *rest):
+    layer_refs = rest[:LAYERS]
+    outer = rest[LAYERS : LAYERS + 5]
+    first_ref, grad_out, *stores, grad_ref, in_sems, out_sems = rest[-10:]
 
     @pl.when(flag_ref[0] == 1)
     def active():
-        top = LAYERS - 1
         for layer in reversed(range(LAYERS)):
             start_all(store_copies(layer, stores, outer, in_sems, True))
-            if layer < top:
-                start_all(layer_copies(layer, layer, weights_ref, held, sems))
         first_ref[...] = g_ref[...]
-
-        def run(layer, ready, block_of):
+        for layer in reversed(range(LAYERS)):
+            held = layer_refs[layer]
             wait_all(store_copies(layer, stores, outer, in_sems, True))
             backward_layer(
-                layer, ready, block_of, cosine_ref, sine_ref, *stores, first_ref, grad_ref
+                layer, lambda: None, lambda z, core, low, held=held: held[z, core, low],
+                cosine_ref, sine_ref, *stores, first_ref, grad_ref,
             )
             start_all(store_copies(layer, [grad_ref], [grad_out], out_sems, False))
-
-        run(top, lambda: None, lambda step: top_ref[step])
-
-        def body(step, carry):
-            layer = top - step
-            run(
-                layer,
-                lambda: wait_all(layer_copies(layer, layer, weights_ref, held, sems)),
-                lambda part: held[layer, part],
-            )
-            return carry
-
-        lax.fori_loop(1, LAYERS, body, 0)
         for layer in range(LAYERS):
             wait_all(store_copies(layer, [grad_ref], [grad_out], out_sems, False))
 
@@ -338,7 +324,7 @@
 
 
 def weight_sems(slots):
-    return pltpu.SemaphoreType.DMA((slots, 2, 2))
+    return pltpu.SemaphoreType.DMA((slots,))
 
 
 def copy_sems(count):
@@ -418,26 +404,24 @@
     )(flag, x, g, cosine, sine, *map(in_hbm, [weights, normed]))
 
 
-def run_backward(flag, g, cosine, sine, top, weights, stored, grads):
+def run_backward(flag, g, cosine, sine, weights, stored, grads):
     tokens = g.shape[0]
     shapes = store_shapes(tokens)
     return pl.pallas_call(
         backward_kernel,
-        in_specs=[SMEM_SPEC] + [VMEM_SPEC] * 4 + [HBM_SPEC] * (6 + len(grads)),
+        in_specs=[SMEM_SPEC] + [VMEM_SPEC] * (3 + LAYERS) + [HBM_SPEC] * (5 + len(grads)),
         out_specs=[VMEM_SPEC, HBM_SPEC],
         out_shape=[jax.ShapeDtypeStruct((tokens, D), BF16), in_hbm_shape(grad_shape(tokens))],
-        input_output_aliases={11: 1} if grads else {},
+        input_output_aliases={9 + LAYERS: 1},
         scratch_shapes=[
-            held_scratch(SLOTS),
             *buffers([shapes[0], *shapes[2:], grad_shape(tokens)]),
-            weight_sems(SLOTS),
             copy_sems(5),
             copy_sems(1),
         ],
         cost_estimate=stage_cost(tokens),
         name="backward_stage",
-        compiler_params=stage_params(32),
-    )(flag, g, cosine, sine, top, *map(in_hbm, [weights, *stored, *grads]))
+        compiler_params=stage_params(12),
+    )(flag, g, cosine, sine, *weights, *map(in_hbm, [*stored, *grads]))
 
 
 def ring(size, by):
@@ -465,10 +449,6 @@
     )
 
 
-def ordered(gathered, layer):
-    return jnp.swapaxes(gathered[layer], 1, 2)
-
-
 def spread_over_y(value, place):
     pieces = [lax.dynamic_index_in_dim(value, place, 0, keepdims=False)]
     for by in (1, 3, 2):
@@ -512,11 +492,11 @@
     g, normed, grads = run_turn(flag, x, g, cosine, sine, gathered, normed)
     grads = [grads]
     g, late = lax.optimization_barrier((g, gathered))
-    top = ordered(late, LAYERS - 1)
+    layers = [late[layer] for layer in range(LAYERS)]
     for turn in reversed(range(LAYERS - 1)):
         flag = (stage == turn).astype(jnp.int32).reshape(1)
         g = lax.ppermute(g, ("xh", "xl"), [(STAGE_X[turn + 1], STAGE_X[turn])])
-        g, *grads = run_backward(flag, g, cosine, sine, top, gathered, [inputs, *shared], grads)
+        g, *grads = run_backward(flag, g, cosine, sine, layers, [inputs, *shared], grads)
     grads = grads[0]
 
     normed_rows = jnp.concatenate(spread_over_y(normed, place))

time: 416 us -> 413 us (level)
  waiting for transfers between devices: 310 us -> 301 us
  local copies, waits for them, and re-layouts: 15.7 us -> 21.4 us
    squeeze x0 -> x1, local copies, waits for them, and re-layouts: none -> 13.3 us  [local(): layers = [late[layer] for layer in range(LAYERS)]]
    transpose x2 -> x0, local copies, waits for them, and re-layouts: 10.7 us -> none  [ordered(): return jnp.swapaxes(gathered[layer], 1, 2)]
    ppermute x3, waiting for transfers between devices: 94.8 us -> 88.1 us  [local(): g = lax.ppermute(g, ('xh', 'xl'), [(STAGE_X[turn + 1], STAGE_X[turn])])]
where the time goes in v5:
time: 413 us; the launch traced here: 406 us
  waiting for transfers between devices  301 us (73%)
  Pallas kernels  35.2 us (9%)
  starting transfers between devices  26 us (6%)
  local copies, waits for them, and re-layouts  21.4 us (5%)
  between operations  14.3 us (3%)
  matrix products  4.21 us (1%)
    all_gather x1, waiting for transfers between devices, local(): gathered = lax.all_gather(shard, ('y', 'z', 'core'), axis=0, tiled=False)  131 us
    ppermute x3, waiting for transfers between devices, local(): g = lax.ppermute(g, ('xh', 'xl'), [(STAGE_X[turn + 1], STAGE_X[turn])])  88.1 us
    reduce_scatter x1, waiting for transfers between devices, local(): total = lax.psum_scatter(terms, 'z', scatter_dimension=0, tiled=True)  45.5 us
    pallas_call x3, Pallas kernels, run_backward(): pl.pallas_call(backward_kernel, in_specs=[SMEM_SPEC] + [VMEM_SPEC] * (3 +...  19.7 us
    pallas_call x3, Pallas kernels, run_forward(): pl.pallas_call(forward_kernel, in_specs=[SMEM_SPEC] + [VMEM_SPEC] * 3 + [...  15.4 us
    ppermute x6, waiting for transfers between devices, spread_over_y(): pieces.append(lax.ppermute(piece, 'y', ring(4, by)))  13.6 us
    squeeze x1, local copies, waits for them, and re-layouts, local(): layers = [late[layer] for layer in range(LAYERS)]  13.3 us
    ppermute x4, waiting for transfers between devices, from_partner(): return lax.ppermute(value, 'xl', ring(2, 1))  9.75 us
  transfers between devices with their start and end apart: 23, of which 16 were waited for; matrix products, arithmetic and copies ran while one was open for 4% of the time, Pallas kernels for 5%

profile of v5, /device:TPU:1, one launch (start us, length us, event | category | flops | bytes accessed | tf_op | source)
XLA Modules:
  0.0 405.6 jit_solution(1603778007315059240)
XLA Ops:
  7.7 2.1 collective-permute-start.2
  9.8 4.0 collective-permute-done.2
  14.7 2.3 collective-permute-start.1
  18.7 2.3 collective-permute-done
  21.0 131.2 %all-gather.2.cloned.1.call-done = bf16[64,2,64,1792]{3,2,1,0:T(8,128)(2,1)} async-done(((bf16[1,2,64,1792]{3,2,1,0:T(8,128)(2,1)}), bf16[64,2,64,1792]{3,2,1,0:T(8,128)(2,1)}) %all-gather.2.cloned.1.call-update) | async-done | bytes 29360144 | tf_op jit(solution)/shard_map/all_gather | solution.py:472
  152.2 14.3 %forward_stage.3 = (bf16[64,2048]{1,0:T(8,128)(2,1)S(1)}, bf16[4,64,2048]{2,1,0:T(8,128)(2,1)}, bf16[4,64,2048]{2,1,0:T(8,128)(2,1)}, bf16[4,64,512]{2,1,0:T(8,1...) custom-call(s32[1]{0:T(128)} %bitcast.3.flag_ref, ...), custom_call_target="tpu_custom_call" | custom-call | flops 1879048192 | bytes 29360128 | tf_op jit(solution)/shard_map/forward_stage/pallas_call | solution.py:360
  167.9 5.7 %collective-permute-done.3.x_ref = bf16[64,2048]{1,0:T(8,128)(2,1)S(1)} collective-permute-done((bf16[64,2048]{1,0:T(8,128)(2,1)S(1)}, bf16[64,2048]{1,0:T(8,128)(2,1)S(1)}, u32[]{:S(2)}, u32[]{:S(2)}) %collective-permute-start.3) | collective-permute-done | bytes 262176 | tf_op jit(solution)/shard_map/ppermute | solution.py:486
  177.1 2.7 collective-permute-done.6
  180.7 13.3 %slice_bitcast_fusion = (bf16[8,2,2,64,1792]{4,3,2,1,0:T(8,128)(2,1)S(1)}, bf16[8,2,2,64,1792]{4,3,2,1,0:T(8,128)(2,1)S(1)}, bf16[8,2,2,64,1792]{4,3,2,1,0:T(8,128)(2,1)S(1)}, bf16[8,2,2,64,1792]{4,3,2,1,0:T(8,128)(2,1)}) fusion(bf16[4,8,2,2,64,1792]{5,4,3,2,1,0:T(8,128)(2,1)} %bitcast.74), kind=kLoop, calls=%fused_computation | loop fusion | bytes 58720256 | tf_op jit(solution)/shard_map/squeeze | solution.py:495
  194.0 3.1 copy-done.2
  198.4 2.7 collective-permute-start.8
  201.2 2.8 backward_stage.4
  206.2 4.8 %collective-permute-done.9 = bf16[64,2048]{1,0:T(8,128)(2,1)S(1)} collective-permute-done((bf16[64,2048]{1,0:T(8,128)(2,1)S(1)}, bf16[64,2048]{1,0:T(8,128)(2,1)S(1)}, u32[]{:S(2)}, u32[]{:S(2)}) %collective-permute-start.9) | collective-permute-done | bytes 262176 | tf_op jit(solution)/shard_map/ppermute | solution.py:456
  211.1 3.0 collective-permute-start.10
  214.2 88.1 %collective-permute-done.13.g_ref = bf16[64,2048]{1,0:T(8,128)(2,1)S(1)} collective-permute-done((bf16[64,2048]{1,0:T(8,128)(2,1)S(1)}, bf16[64,2048]{1,0:T(8,128)(2,1)S(1)}, u32[]{:S(2)}, u32[]{:S(2)}) %collective-permute-start.13) | collective-permute-done | bytes 262176 | tf_op jit(solution)/shard_map/ppermute | solution.py:498
  302.3 16.5 %backward_stage.5 = (bf16[64,2048]{1,0:T(8,128)(2,1)}, bf16[4,64,1792]{2,1,0:T(8,128)(2,1)}) custom-call(s32[1]{0:T(128)} %bitcast.3.flag_ref, bf16[64,2048]{1,0:T(8,128)(2,1)S(1)} %collective-permute-done.13.g_ref, f32[64,128]{1,0:T(8,128)S(1)} %get-tuple-element.94.cosine_ref, ...), custom_call_target="tpu_custom_call", output_to_operand_aliasing={{1}: (13, {})} | custom-call | flops 1879048192 | bytes 29360128 | tf_op jit(solution)/shard_map/backward_stage/pallas_call | solution.py:410
  320.2 2.7 collective-permute-start.15
  322.9 3.4 collective-permute-done.14
  328.3 2.5 collective-permute-done.16
  331.0 4.9 %collective-permute-start.17 = (bf16[256,896]{1,0:T(8,128)(2,1)S(1)}, bf16[256,896]{1,0:T(8,128)(2,1)S(1)}, u32[]{:S(2)}, u32[]{:S(2)}) collective-permute-start(bf16[256,896]{1,0:T(8,128)(2,1)S(1)} %get-tuple-element.77), channel_id=1, source_target_pairs={{0,1},{1,0},{2,3},{3,2},{4,5},{5,4},{6,7},{7,6},{8,9},{9,8},{10,11... | collective-permute-start | bytes 1376264 | tf_op jit(solution)/shard_map/ppermute | solution.py:503
  337.4 4.2 %convolution_convert_fusion = bf16[2048,896]{1,0:T(8,128)(2,1)} fusion(bf16[512,2048]{1,0:T(8,128)(2,1)S(1)} %constant_dynamic-update-slice_fusion, bf16[256,896]{1,0:T(8,128)(2,1)S(1)} %collective-permute-done.17, bf16[256,896]{1,0:T(8,128)(2,1)S(1)} %get-tuple-element.76), kind=kOutput, calls=%fused_computation.4 | convolution fusion | flops 1882718208 | bytes 6684672 | tf_op jit(solution)/shard_map/dot_general | solution.py:30
  341.6 45.5 %reduce-scatter.2.cloned.1.call-done = bf16[256,896]{1,0:T(8,128)(2,1)} async-done(((bf16[2048,896]{1,0:T(8,128)(2,1)}), bf16[256,896]{1,0:T(8,128)(2,1)}) %reduce-scatter.2.cloned.1.call-update) | async-done | bytes 458768 | tf_op jit(solution)/shard_map/reduce_scatter | solution.py:511
  390.6 3.0 collective-permute-done.19
  393.6 2.6 collective-permute-done.20
  (76 shorter events, 23.5 us)
Async XLA Ops:
  6.5 145.7 %all-gather.2.cloned.1.call-start = ((), (), s32[]{:S(2)}) async-start(), calls=%async_computation.1 | async-start | bytes 29818880 | tf_op jit(solution)/shard_map/all_gather | solution.py:472
  7.7 6.1 %collective-permute-start.2 = (bf16[64,1792]{1,0:T(8,128)(2,1)S(1)}, bf16[64,1792]{1,0:T(8,128)(2,1)S(1)}, u32[]{:S(2)}, u32[]{:S(2)}) collective-permute-start(bf16[64,1792]{1,0:T(8,128)(2,1)S(1)} %get-tuple-element.90), channel_id=1, source_target_pairs={{0,2},{2,0},{1,3},{3,1},{4,6},{6,4},{5,7},{7,5},{8,10},{10,8},{9,1... | collective-permute-start | bytes 688136 | tf_op jit(solution)/shard_map/ppermute | solution.py:432
  14.7 372.5 %reduce-scatter.2.cloned.1.call-start = ((), (), s32[]{:S(2)}) async-start(), calls=%async_computation.2 | async-start | bytes 4128768 | tf_op jit(solution)/shard_map/reduce_scatter | solution.py:511
  14.7 3.2 collective-permute-start.1
  17.0 3.9 collective-permute-start
  166.6 7.1 %collective-permute-start.3 = (bf16[64,2048]{1,0:T(8,128)(2,1)S(1)}, bf16[64,2048]{1,0:T(8,128)(2,1)S(1)}, u32[]{:S(2)}, u32[]{:S(2)}) collective-permute-start(bf16[64,2048]{1,0:T(8,128)(2,1)S(1)} %get-tuple-element.36), channel_id=1, source_target_pairs={{0,128},{1,129},{4,132},{5,133},{8,136},{9,137},{12,140},{13,141},... | collective-permute-start | bytes 786440 | tf_op jit(solution)/shard_map/ppermute | solution.py:486
  173.9 1.7 collective-permute-start.4
  175.5 4.4 %collective-permute-start.6 = (bf16[32,2048]{1,0:T(8,128)(2,1)S(1)}, bf16[32,2048]{1,0:T(8,128)(2,1)S(1)}, u32[]{:S(2)}, u32[]{:S(2)}) collective-permute-start(bf16[32,2048]{1,0:T(8,128)(2,1)S(1)} %bitcast.75), channel_id=1, source_target_pairs={{0,2},{2,0},{1,3},{3,1},{4,6},{6,4},{5,7},{7,5},{8,10},{10,8},{9,1... | collective-permute-start | bytes 393224 | tf_op jit(solution)/shard_map/ppermute | solution.py:432
  176.4 3.5 collective-permute-start.5
  180.0 14.0 %collective-permute-start.11 = (bf16[64,2048]{1,0:T(8,128)(2,1)S(1)}, bf16[64,2048]{1,0:T(8,128)(2,1)S(1)}, u32[]{:S(2)}, u32[]{:S(2)}) collective-permute-start(bf16[64,2048]{1,0:T(8,128)(2,1)S(1)} %get-tuple-element.54), channel_id=1, source_target_pairs={{130,2},{131,3},{134,6},{135,7},{138,10},{139,11},{142,14},{143,15... | collective-permute-start | bytes 786440 | tf_op jit(solution)/shard_map/ppermute | solution.py:498
  197.4 3.7 collective-permute-start.12
  198.3 7.9 %collective-permute-start.7 = (bf16[64,2048]{1,0:T(8,128)(2,1)S(1)}, bf16[64,2048]{1,0:T(8,128)(2,1)S(1)}, u32[]{:S(2)}, u32[]{:S(2)}) collective-permute-start(bf16[64,2048]{1,0:T(8,128)(2,1)S(1)} %get-tuple-element.75), channel_id=1, source_target_pairs={{0,32},{32,64},{64,96},{96,0},{1,33},{33,65},{65,97},{97,1},{2,34}... | collective-permute-start | bytes 786440 | tf_op jit(solution)/shard_map/ppermute | solution.py:456
  198.4 7.8 %collective-permute-start.8 = (bf16[64,2048]{1,0:T(8,128)(2,1)S(1)}, bf16[64,2048]{1,0:T(8,128)(2,1)S(1)}, u32[]{:S(2)}, u32[]{:S(2)}) collective-permute-start(bf16[64,2048]{1,0:T(8,128)(2,1)S(1)} %get-tuple-element.74), channel_id=1, source_target_pairs={{0,96},{32,0},{64,32},{96,64},{1,97},{33,1},{65,33},{97,65},{2,98}... | collective-permute-start | bytes 786440 | tf_op jit(solution)/shard_map/ppermute | solution.py:456
  201.1 9.9 %collective-permute-start.9 = (bf16[64,2048]{1,0:T(8,128)(2,1)S(1)}, bf16[64,2048]{1,0:T(8,128)(2,1)S(1)}, u32[]{:S(2)}, u32[]{:S(2)}) collective-permute-start(bf16[64,2048]{1,0:T(8,128)(2,1)S(1)} %get-tuple-element.73), channel_id=1, source_target_pairs={{0,64},{32,96},{64,0},{96,32},{1,65},{33,97},{65,1},{97,33},{2,66}... | collective-permute-start | bytes 786440 | tf_op jit(solution)/shard_map/ppermute | solution.py:456
  204.0 98.2 %collective-permute-start.13 = (bf16[64,2048]{1,0:T(8,128)(2,1)S(1)}, bf16[64,2048]{1,0:T(8,128)(2,1)S(1)}, u32[]{:S(2)}, u32[]{:S(2)}) collective-permute-start(bf16[64,2048]{1,0:T(8,128)(2,1)S(1)} %get-tuple-element.64), channel_id=1, source_target_pairs={{128,0},{129,1},{132,4},{133,5},{136,8},{137,9},{140,12},{141,13},... | collective-permute-start | bytes 786440 | tf_op jit(solution)/shard_map/ppermute | solution.py:498
  211.1 124.8 %collective-permute-start.10 = (bf16[256,2048]{1,0:T(8,128)(2,1)S(1)}, bf16[256,2048]{1,0:T(8,128)(2,1)S(1)}, u32[]{:S(2)}, u32[]{:S(2)}) collective-permute-start(bf16[256,2048]{1,0:T(8,128)(2,1)S(1)} %pad_maximum_fusion), channel_id=1, source_target_pairs={{0,1},{1,0},{2,3},{3,2},{4,5},{5,4},{6,7},{7,6},{8,9},{9,8},{10,11... | collective-permute-start | bytes 3145736 | tf_op jit(solution)/shard_map/ppermute | solution.py:503
  320.1 6.2 %collective-permute-start.14 = (bf16[64,1792]{1,0:T(8,128)(2,1)S(1)}, bf16[64,1792]{1,0:T(8,128)(2,1)S(1)}, u32[]{:S(2)}, u32[]{:S(2)}) collective-permute-start(bf16[64,1792]{1,0:T(8,128)(2,1)S(1)} %get-tuple-element.81), channel_id=1, source_target_pairs={{0,32},{32,64},{64,96},{96,0},{1,33},{33,65},{65,97},{97,1},{2,34}... | collective-permute-start | bytes 688136 | tf_op jit(solution)/shard_map/ppermute | solution.py:456
  320.2 8.1 %collective-permute-start.15 = (bf16[64,1792]{1,0:T(8,128)(2,1)S(1)}, bf16[64,1792]{1,0:T(8,128)(2,1)S(1)}, u32[]{:S(2)}, u32[]{:S(2)}) collective-permute-start(bf16[64,1792]{1,0:T(8,128)(2,1)S(1)} %get-tuple-element.80), channel_id=1, source_target_pairs={{0,96},{32,0},{64,32},{96,64},{1,97},{33,1},{65,33},{97,65},{2,98}... | collective-permute-start | bytes 688136 | tf_op jit(solution)/shard_map/ppermute | solution.py:456
  322.9 7.9 %collective-permute-start.16 = (bf16[64,1792]{1,0:T(8,128)(2,1)S(1)}, bf16[64,1792]{1,0:T(8,128)(2,1)S(1)}, u32[]{:S(2)}, u32[]{:S(2)}) collective-permute-start(bf16[64,1792]{1,0:T(8,128)(2,1)S(1)} %get-tuple-element.79), channel_id=1, source_target_pairs={{0,64},{32,96},{64,0},{96,32},{1,65},{33,97},{65,1},{97,33},{2,66}... | collective-permute-start | bytes 688136 | tf_op jit(solution)/shard_map/ppermute | solution.py:456
  331.0 6.4 %collective-permute-start.17 = (bf16[256,896]{1,0:T(8,128)(2,1)S(1)}, bf16[256,896]{1,0:T(8,128)(2,1)S(1)}, u32[]{:S(2)}, u32[]{:S(2)}) collective-permute-start(bf16[256,896]{1,0:T(8,128)(2,1)S(1)} %get-tuple-element.77), channel_id=1, source_target_pairs={{0,1},{1,0},{2,3},{3,2},{4,5},{5,4},{6,7},{7,6},{8,9},{9,8},{10,11... | collective-permute-start | bytes 1376264 | tf_op jit(solution)/shard_map/ppermute | solution.py:503
  341.6 56.6 %copy-start.1 = (bf16[8,16,2048]{2,1,0:T(8,128)(2,1)S(1)}, bf16[8,16,2048]{2,1,0:T(8,128)(2,1)}, u32[]{:S(2)}) copy-start(bf16[8,16,2048]{2,1,0:T(8,128)(2,1)} %param.4) | copy-start | bytes 1572868
  388.2 2.4 collective-permute-start.18
  388.9 4.7 %collective-permute-start.19 = (bf16[64,896]{1,0:T(8,128)(2,1)S(1)}, bf16[64,896]{1,0:T(8,128)(2,1)S(1)}, u32[]{:S(2)}, u32[]{:S(2)}) collective-permute-start(bf16[64,896]{1,0:T(8,128)(2,1)S(1)} %get-tuple-element.88), channel_id=1, source_target_pairs={{0,2},{1,3},{2,0},{3,1},{4,6},{5,7},{6,4},{7,5},{8,10},{9,11},{10,... | collective-permute-start | bytes 344072 | tf_op jit(solution)/shard_map/ppermute | solution.py:522
  390.1 6.1 %collective-permute-start.20 = (bf16[64,896]{1,0:T(8,128)(2,1)S(1)}, bf16[64,896]{1,0:T(8,128)(2,1)S(1)}, u32[]{:S(2)}, u32[]{:S(2)}) collective-permute-start(bf16[64,896]{1,0:T(8,128)(2,1)S(1)} %get-tuple-element.87), channel_id=1, source_target_pairs={{0,3},{1,2},{2,1},{3,0},{4,7},{5,6},{6,5},{7,4},{8,11},{9,10},{10,... | collective-permute-start | bytes 344072 | tf_op jit(solution)/shard_map/ppermute | solution.py:522
  (5 other events, 27.1 us)
Sparse Core Ops, SparseCore 0:
  14.8 137.3 all-gather.1
  341.7 45.3 reduce-scatter.1

commit v6 on v5

--- a/solution.py
+++ b/solution.py
@@ -283,12 +283,14 @@
 
     @pl.when(flag_ref[0] == 1)
     def active():
-        for layer in reversed(range(LAYERS)):
-            start_all(store_copies(layer, stores, outer, in_sems, True))
+        top = LAYERS - 1
+        start_all(store_copies(top, stores, outer, in_sems, True))
         first_ref[...] = g_ref[...]
         for layer in reversed(range(LAYERS)):
             held = layer_refs[layer]
             wait_all(store_copies(layer, stores, outer, in_sems, True))
+            if layer > 0:
+                start_all(store_copies(layer - 1, stores, outer, in_sems, True))
             backward_layer(
                 layer, lambda: None, lambda z, core, low, held=held: held[z, core, low],
                 cosine_ref, sine_ref, *stores, first_ref, grad_ref,

time: 413 us -> 413 us (level)
  no operation moved by 1% of the time
where the time goes in v6:
time: 413 us; the launch traced here: 406 us
  waiting for transfers between devices  301 us (73%)
  Pallas kernels  35.2 us (9%)
  starting transfers between devices  26 us (6%)
  local copies, waits for them, and re-layouts  21.4 us (5%)
  between operations  14.3 us (3%)
  matrix products  4.21 us (1%)
    all_gather x1, waiting for transfers between devices, local(): gathered = lax.all_gather(shard, ('y', 'z', 'core'), axis=0, tiled=False)  131 us
    ppermute x3, waiting for transfers between devices, local(): g = lax.ppermute(g, ('xh', 'xl'), [(STAGE_X[turn + 1], STAGE_X[turn])])  88.1 us
    reduce_scatter x1, waiting for transfers between devices, local(): total = lax.psum_scatter(terms, 'z', scatter_dimension=0, tiled=True)  45.5 us
    pallas_call x3, Pallas kernels, run_backward(): pl.pallas_call(backward_kernel, in_specs=[SMEM_SPEC] + [VMEM_SPEC] * (3 +...  19.7 us
    pallas_call x3, Pallas kernels, run_forward(): pl.pallas_call(forward_kernel, in_specs=[SMEM_SPEC] + [VMEM_SPEC] * 3 + [...  15.4 us
    ppermute x6, waiting for transfers between devices, spread_over_y(): pieces.append(lax.ppermute(piece, 'y', ring(4, by)))  13.6 us
    squeeze x1, local copies, waits for them, and re-layouts, local(): layers = [late[layer] for layer in range(LAYERS)]  13.3 us
    ppermute x4, waiting for transfers between devices, from_partner(): return lax.ppermute(value, 'xl', ring(2, 1))  9.75 us
  transfers between devices with their start and end apart: 23, of which 16 were waited for; matrix products, arithmetic and copies ran while one was open for 4% of the time, Pallas kernels for 5%

profile of v6, /device:TPU:1, one launch (start us, length us, event | category | flops | bytes accessed | tf_op | source)
XLA Modules:
  0.0 405.6 jit_solution(8603927948333035249)
XLA Ops:
  7.7 2.1 collective-permute-start.2
  9.8 4.0 collective-permute-done.2
  14.7 2.3 collective-permute-start.1
  18.7 2.3 collective-permute-done
  21.0 131.2 %all-gather.2.cloned.1.call-done = bf16[64,2,64,1792]{3,2,1,0:T(8,128)(2,1)} async-done(((bf16[1,2,64,1792]{3,2,1,0:T(8,128)(2,1)}), bf16[64,2,64,1792]{3,2,1,0:T(8,128)(2,1)}) %all-gather.2.cloned.1.call-update) | async-done | bytes 29360144 | tf_op jit(solution)/shard_map/all_gather | solution.py:474
  152.2 14.3 %forward_stage.3 = (bf16[64,2048]{1,0:T(8,128)(2,1)S(1)}, bf16[4,64,2048]{2,1,0:T(8,128)(2,1)}, bf16[4,64,2048]{2,1,0:T(8,128)(2,1)}, bf16[4,64,512]{2,1,0:T(8,1...) custom-call(s32[1]{0:T(128)} %bitcast.3.flag_ref, ...), custom_call_target="tpu_custom_call" | custom-call | flops 1879048192 | bytes 29360128 | tf_op jit(solution)/shard_map/forward_stage/pallas_call | solution.py:362
  167.9 5.7 %collective-permute-done.3.x_ref = bf16[64,2048]{1,0:T(8,128)(2,1)S(1)} collective-permute-done((bf16[64,2048]{1,0:T(8,128)(2,1)S(1)}, bf16[64,2048]{1,0:T(8,128)(2,1)S(1)}, u32[]{:S(2)}, u32[]{:S(2)}) %collective-permute-start.3) | collective-permute-done | bytes 262176 | tf_op jit(solution)/shard_map/ppermute | solution.py:488
  177.1 2.7 collective-permute-done.6
  180.7 13.3 %slice_bitcast_fusion = (bf16[8,2,2,64,1792]{4,3,2,1,0:T(8,128)(2,1)S(1)}, bf16[8,2,2,64,1792]{4,3,2,1,0:T(8,128)(2,1)S(1)}, bf16[8,2,2,64,1792]{4,3,2,1,0:T(8,128)(2,1)S(1)}, bf16[8,2,2,64,1792]{4,3,2,1,0:T(8,128)(2,1)}) fusion(bf16[4,8,2,2,64,1792]{5,4,3,2,1,0:T(8,128)(2,1)} %bitcast.74), kind=kLoop, calls=%fused_computation | loop fusion | bytes 58720256 | tf_op jit(solution)/shard_map/squeeze | solution.py:497
  194.0 3.1 copy-done.2
  198.4 2.7 collective-permute-start.8
  201.2 2.8 backward_stage.4
  206.2 4.8 %collective-permute-done.9 = bf16[64,2048]{1,0:T(8,128)(2,1)S(1)} collective-permute-done((bf16[64,2048]{1,0:T(8,128)(2,1)S(1)}, bf16[64,2048]{1,0:T(8,128)(2,1)S(1)}, u32[]{:S(2)}, u32[]{:S(2)}) %collective-permute-start.9) | collective-permute-done | bytes 262176 | tf_op jit(solution)/shard_map/ppermute | solution.py:458
  211.1 3.0 collective-permute-start.10
  214.2 88.1 %collective-permute-done.13.g_ref = bf16[64,2048]{1,0:T(8,128)(2,1)S(1)} collective-permute-done((bf16[64,2048]{1,0:T(8,128)(2,1)S(1)}, bf16[64,2048]{1,0:T(8,128)(2,1)S(1)}, u32[]{:S(2)}, u32[]{:S(2)}) %collective-permute-start.13) | collective-permute-done | bytes 262176 | tf_op jit(solution)/shard_map/ppermute | solution.py:500
  302.3 16.5 %backward_stage.5 = (bf16[64,2048]{1,0:T(8,128)(2,1)}, bf16[4,64,1792]{2,1,0:T(8,128)(2,1)}) custom-call(s32[1]{0:T(128)} %bitcast.3.flag_ref, bf16[64,2048]{1,0:T(8,128)(2,1)S(1)} %collective-permute-done.13.g_ref, f32[64,128]{1,0:T(8,128)S(1)} %get-tuple-element.94.cosine_ref, ...), custom_call_target="tpu_custom_call", output_to_operand_aliasing={{1}: (13, {})} | custom-call | flops 1879048192 | bytes 29360128 | tf_op jit(solution)/shard_map/backward_stage/pallas_call | solution.py:412
  320.2 2.7 collective-permute-start.15
  322.9 3.4 collective-permute-done.14
  328.3 2.5 collective-permute-done.16
  331.0 4.9 %collective-permute-start.17 = (bf16[256,896]{1,0:T(8,128)(2,1)S(1)}, bf16[256,896]{1,0:T(8,128)(2,1)S(1)}, u32[]{:S(2)}, u32[]{:S(2)}) collective-permute-start(bf16[256,896]{1,0:T(8,128)(2,1)S(1)} %get-tuple-element.77), channel_id=1, source_target_pairs={{0,1},{1,0},{2,3},{3,2},{4,5},{5,4},{6,7},{7,6},{8,9},{9,8},{10,11... | collective-permute-start | bytes 1376264 | tf_op jit(solution)/shard_map/ppermute | solution.py:505
  337.4 4.2 %convolution_convert_fusion = bf16[2048,896]{1,0:T(8,128)(2,1)} fusion(bf16[512,2048]{1,0:T(8,128)(2,1)S(1)} %constant_dynamic-update-slice_fusion, bf16[256,896]{1,0:T(8,128)(2,1)S(1)} %collective-permute-done.17, bf16[256,896]{1,0:T(8,128)(2,1)S(1)} %get-tuple-element.76), kind=kOutput, calls=%fused_computation.4 | convolution fusion | flops 1882718208 | bytes 6684672 | tf_op jit(solution)/shard_map/dot_general | solution.py:30
  341.7 45.5 %reduce-scatter.2.cloned.1.call-done = bf16[256,896]{1,0:T(8,128)(2,1)} async-done(((bf16[2048,896]{1,0:T(8,128)(2,1)}), bf16[256,896]{1,0:T(8,128)(2,1)}) %reduce-scatter.2.cloned.1.call-update) | async-done | bytes 458768 | tf_op jit(solution)/shard_map/reduce_scatter | solution.py:513
  390.6 3.0 collective-permute-done.19
  393.6 2.6 collective-permute-done.20
  (76 shorter events, 23.5 us)
Async XLA Ops:
  6.5 145.7 %all-gather.2.cloned.1.call-start = ((), (), s32[]{:S(2)}) async-start(), calls=%async_computation.1 | async-start | bytes 29818880 | tf_op jit(solution)/shard_map/all_gather | solution.py:474
  7.7 6.1 %collective-permute-start.2 = (bf16[64,1792]{1,0:T(8,128)(2,1)S(1)}, bf16[64,1792]{1,0:T(8,128)(2,1)S(1)}, u32[]{:S(2)}, u32[]{:S(2)}) collective-permute-start(bf16[64,1792]{1,0:T(8,128)(2,1)S(1)} %get-tuple-element.90), channel_id=1, source_target_pairs={{0,2},{2,0},{1,3},{3,1},{4,6},{6,4},{5,7},{7,5},{8,10},{10,8},{9,1... | collective-permute-start | bytes 688136 | tf_op jit(solution)/shard_map/ppermute | solution.py:434
  14.7 372.5 %reduce-scatter.2.cloned.1.call-start = ((), (), s32[]{:S(2)}) async-start(), calls=%async_computation.2 | async-start | bytes 4128768 | tf_op jit(solution)/shard_map/reduce_scatter | solution.py:513
  14.7 3.2 collective-permute-start.1
  17.0 3.9 collective-permute-start
  166.6 7.1 %collective-permute-start.3 = (bf16[64,2048]{1,0:T(8,128)(2,1)S(1)}, bf16[64,2048]{1,0:T(8,128)(2,1)S(1)}, u32[]{:S(2)}, u32[]{:S(2)}) collective-permute-start(bf16[64,2048]{1,0:T(8,128)(2,1)S(1)} %get-tuple-element.36), channel_id=1, source_target_pairs={{0,128},{1,129},{4,132},{5,133},{8,136},{9,137},{12,140},{13,141},... | collective-permute-start | bytes 786440 | tf_op jit(solution)/shard_map/ppermute | solution.py:488
  173.9 1.7 collective-permute-start.4
  175.5 4.4 %collective-permute-start.6 = (bf16[32,2048]{1,0:T(8,128)(2,1)S(1)}, bf16[32,2048]{1,0:T(8,128)(2,1)S(1)}, u32[]{:S(2)}, u32[]{:S(2)}) collective-permute-start(bf16[32,2048]{1,0:T(8,128)(2,1)S(1)} %bitcast.75), channel_id=1, source_target_pairs={{0,2},{2,0},{1,3},{3,1},{4,6},{6,4},{5,7},{7,5},{8,10},{10,8},{9,1... | collective-permute-start | bytes 393224 | tf_op jit(solution)/shard_map/ppermute | solution.py:434
  176.4 3.5 collective-permute-start.5
  180.0 14.0 %collective-permute-start.11 = (bf16[64,2048]{1,0:T(8,128)(2,1)S(1)}, bf16[64,2048]{1,0:T(8,128)(2,1)S(1)}, u32[]{:S(2)}, u32[]{:S(2)}) collective-permute-start(bf16[64,2048]{1,0:T(8,128)(2,1)S(1)} %get-tuple-element.54), channel_id=1, source_target_pairs={{130,2},{131,3},{134,6},{135,7},{138,10},{139,11},{142,14},{143,15... | collective-permute-start | bytes 786440 | tf_op jit(solution)/shard_map/ppermute | solution.py:500
  197.4 3.7 collective-permute-start.12
  198.3 7.9 %collective-permute-start.7 = (bf16[64,2048]{1,0:T(8,128)(2,1)S(1)}, bf16[64,2048]{1,0:T(8,128)(2,1)S(1)}, u32[]{:S(2)}, u32[]{:S(2)}) collective-permute-start(bf16[64,2048]{1,0:T(8,128)(2,1)S(1)} %get-tuple-element.75), channel_id=1, source_target_pairs={{0,32},{32,64},{64,96},{96,0},{1,33},{33,65},{65,97},{97,1},{2,34}... | collective-permute-start | bytes 786440 | tf_op jit(solution)/shard_map/ppermute | solution.py:458
  198.4 7.8 %collective-permute-start.8 = (bf16[64,2048]{1,0:T(8,128)(2,1)S(1)}, bf16[64,2048]{1,0:T(8,128)(2,1)S(1)}, u32[]{:S(2)}, u32[]{:S(2)}) collective-permute-start(bf16[64,2048]{1,0:T(8,128)(2,1)S(1)} %get-tuple-element.74), channel_id=1, source_target_pairs={{0,96},{32,0},{64,32},{96,64},{1,97},{33,1},{65,33},{97,65},{2,98}... | collective-permute-start | bytes 786440 | tf_op jit(solution)/shard_map/ppermute | solution.py:458
  201.1 9.9 %collective-permute-start.9 = (bf16[64,2048]{1,0:T(8,128)(2,1)S(1)}, bf16[64,2048]{1,0:T(8,128)(2,1)S(1)}, u32[]{:S(2)}, u32[]{:S(2)}) collective-permute-start(bf16[64,2048]{1,0:T(8,128)(2,1)S(1)} %get-tuple-element.73), channel_id=1, source_target_pairs={{0,64},{32,96},{64,0},{96,32},{1,65},{33,97},{65,1},{97,33},{2,66}... | collective-permute-start | bytes 786440 | tf_op jit(solution)/shard_map/ppermute | solution.py:458
  204.0 98.3 %collective-permute-start.13 = (bf16[64,2048]{1,0:T(8,128)(2,1)S(1)}, bf16[64,2048]{1,0:T(8,128)(2,1)S(1)}, u32[]{:S(2)}, u32[]{:S(2)}) collective-permute-start(bf16[64,2048]{1,0:T(8,128)(2,1)S(1)} %get-tuple-element.64), channel_id=1, source_target_pairs={{128,0},{129,1},{132,4},{133,5},{136,8},{137,9},{140,12},{141,13},... | collective-permute-start | bytes 786440 | tf_op jit(solution)/shard_map/ppermute | solution.py:500
  211.1 124.8 %collective-permute-start.10 = (bf16[256,2048]{1,0:T(8,128)(2,1)S(1)}, bf16[256,2048]{1,0:T(8,128)(2,1)S(1)}, u32[]{:S(2)}, u32[]{:S(2)}) collective-permute-start(bf16[256,2048]{1,0:T(8,128)(2,1)S(1)} %pad_maximum_fusion), channel_id=1, source_target_pairs={{0,1},{1,0},{2,3},{3,2},{4,5},{5,4},{6,7},{7,6},{8,9},{9,8},{10,11... | collective-permute-start | bytes 3145736 | tf_op jit(solution)/shard_map/ppermute | solution.py:505
  320.2 6.2 %collective-permute-start.14 = (bf16[64,1792]{1,0:T(8,128)(2,1)S(1)}, bf16[64,1792]{1,0:T(8,128)(2,1)S(1)}, u32[]{:S(2)}, u32[]{:S(2)}) collective-permute-start(bf16[64,1792]{1,0:T(8,128)(2,1)S(1)} %get-tuple-element.81), channel_id=1, source_target_pairs={{0,32},{32,64},{64,96},{96,0},{1,33},{33,65},{65,97},{97,1},{2,34}... | collective-permute-start | bytes 688136 | tf_op jit(solution)/shard_map/ppermute | solution.py:458
  320.2 8.1 %collective-permute-start.15 = (bf16[64,1792]{1,0:T(8,128)(2,1)S(1)}, bf16[64,1792]{1,0:T(8,128)(2,1)S(1)}, u32[]{:S(2)}, u32[]{:S(2)}) collective-permute-start(bf16[64,1792]{1,0:T(8,128)(2,1)S(1)} %get-tuple-element.80), channel_id=1, source_target_pairs={{0,96},{32,0},{64,32},{96,64},{1,97},{33,1},{65,33},{97,65},{2,98}... | collective-permute-start | bytes 688136 | tf_op jit(solution)/shard_map/ppermute | solution.py:458
  322.9 7.9 %collective-permute-start.16 = (bf16[64,1792]{1,0:T(8,128)(2,1)S(1)}, bf16[64,1792]{1,0:T(8,128)(2,1)S(1)}, u32[]{:S(2)}, u32[]{:S(2)}) collective-permute-start(bf16[64,1792]{1,0:T(8,128)(2,1)S(1)} %get-tuple-element.79), channel_id=1, source_target_pairs={{0,64},{32,96},{64,0},{96,32},{1,65},{33,97},{65,1},{97,33},{2,66}... | collective-permute-start | bytes 688136 | tf_op jit(solution)/shard_map/ppermute | solution.py:458
  331.0 6.4 %collective-permute-start.17 = (bf16[256,896]{1,0:T(8,128)(2,1)S(1)}, bf16[256,896]{1,0:T(8,128)(2,1)S(1)}, u32[]{:S(2)}, u32[]{:S(2)}) collective-permute-start(bf16[256,896]{1,0:T(8,128)(2,1)S(1)} %get-tuple-element.77), channel_id=1, source_target_pairs={{0,1},{1,0},{2,3},{3,2},{4,5},{5,4},{6,7},{7,6},{8,9},{9,8},{10,11... | collective-permute-start | bytes 1376264 | tf_op jit(solution)/shard_map/ppermute | solution.py:505
  341.6 56.6 %copy-start.1 = (bf16[8,16,2048]{2,1,0:T(8,128)(2,1)S(1)}, bf16[8,16,2048]{2,1,0:T(8,128)(2,1)}, u32[]{:S(2)}) copy-start(bf16[8,16,2048]{2,1,0:T(8,128)(2,1)} %param.4) | copy-start | bytes 1572868
  388.2 2.4 collective-permute-start.18
  388.9 4.7 %collective-permute-start.19 = (bf16[64,896]{1,0:T(8,128)(2,1)S(1)}, bf16[64,896]{1,0:T(8,128)(2,1)S(1)}, u32[]{:S(2)}, u32[]{:S(2)}) collective-permute-start(bf16[64,896]{1,0:T(8,128)(2,1)S(1)} %get-tuple-element.88), channel_id=1, source_target_pairs={{0,2},{1,3},{2,0},{3,1},{4,6},{5,7},{6,4},{7,5},{8,10},{9,11},{10,... | collective-permute-start | bytes 344072 | tf_op jit(solution)/shard_map/ppermute | solution.py:524
  390.1 6.1 %collective-permute-start.20 = (bf16[64,896]{1,0:T(8,128)(2,1)S(1)}, bf16[64,896]{1,0:T(8,128)(2,1)S(1)}, u32[]{:S(2)}, u32[]{:S(2)}) collective-permute-start(bf16[64,896]{1,0:T(8,128)(2,1)S(1)} %get-tuple-element.87), channel_id=1, source_target_pairs={{0,3},{1,2},{2,1},{3,0},{4,7},{5,6},{6,5},{7,4},{8,11},{9,10},{10,... | collective-permute-start | bytes 344072 | tf_op jit(solution)/shard_map/ppermute | solution.py:524
  (5 other events, 27.1 us)
Sparse Core Ops, SparseCore 0:
  14.8 137.3 all-gather.1
  341.7 45.3 reduce-scatter.1
